TPU v7x, 32 devices: a whole 2x2x4 slice. The times are simulated.
32 devices in a mesh: req: 4 (over x, core), mlp: 8 (over z, y).
Axes of the slice: x: 2, y: 2, z: 4, core: 2. Of those that a mesh axis runs over, the one named last changes fastest.
Arguments:
- queries: bfloat16 [1024, 4096], P(('req', 'mlp')), may hold values from -80 to 80
- keys: bfloat16 [1024, 4096], P(('req', 'mlp')), may hold values from -4 to 4
- values: bfloat16 [1024, 4096], P(('req', 'mlp')), may hold values from -6 to 6
- block_hidden_input: bfloat16 [1024, 5120], P(('req', 'mlp')), may hold values from -6 to 6
- attention_out_weight: bfloat16 [4096, 5120], P('mlp'), may hold values from -0.09375 to 0.09375
- feedfwd_in_weight: bfloat16 [5120, 13824], P(None, 'mlp'), may hold values from -0.078125 to 0.078125
- feedfwd_out_weight: bfloat16 [13824, 5120], P('mlp'), may hold values from -0.0546875 to 0.0546875
- norm_gain_vector: float32 [5120], replicated, may hold values from 0.5 to 1.5
- norm_bias_vector: float32 [5120], replicated, may hold values from -3 to 3
- adapter_down_factors: bfloat16 [64, 5120, 16], P('req', 'mlp'), may hold values from -0.078125 to 0.078125
- adapter_up_factors: bfloat16 [64, 16, 13824], P('req', None, 'mlp'), may hold values from -0.75 to 0.75
- paged_key_cache: bfloat16 [12, 128, 4096], P('req', None, 'mlp'), may hold values from -6 to 6
- paged_value_cache: bfloat16 [12, 128, 4096], P('req', None, 'mlp'), may hold values from -6 to 6
- request_prompt_length: int32 [4, 16], P('req'), may hold values from 1 to 128, 256 in all within a row
- group_page_lookup: int32 [4, 2], P('req'), may hold values from 0 to 2, as said below
- adapter_per_request: int32 [4, 16], P('req'), may hold values from 0 to 63
- adapter_bank_slot: int32 [64], replicated, may hold values from 0 to 63, each once
Outputs:
- block_out: bfloat16 [1024, 5120], P(('req', 'mlp'))
- key_pages_out: bfloat16 [12, 128, 4096], P('req', None, 'mlp')
- value_pages_out: bfloat16 [12, 128, 4096], P('req', None, 'mlp')
Inputs may be any that keep to these rules, and one draw needn't show every extreme that they name: `group_page_lookup`: the 2 entries of a row are different pages of the group's 3. `request_prompt_length`: each row sums to 256; its longest request holds exactly half of that.
All inputs are finite; a program needn't handle non-finite values.
Results may differ from a plain program's by a relative error of at most 0.014.
Values may be sent and summed in bfloat16 or wider, within the bound.
No kernel may reach another device: no remote copies, remote signals or barrier semaphores. Data moves between devices by JAX's collectives and lax.ppermute only.
A program may use at most 128 MiB of HBM per device.

v0:
```python
import jax
import jax.numpy as jnp
from jax import lax
from jax.sharding import PartitionSpec as P

HS = 128
ADAPTER_RANK = 16
REQS = 16
PAGE = 128


EPS = 1e-06


def modulate(residual, norm_gain_vector, norm_bias_vector):
    row_mean = jnp.mean(residual, axis=-1, keepdims=True)
    centered = residual - row_mean
    row_var = jnp.mean(centered * centered, axis=-1, keepdims=True)
    return (centered * lax.rsqrt(row_var + EPS) * norm_gain_vector + norm_bias_vector).astype(
        jnp.bfloat16
    )


def softmax_rows(scores, allowed):
    masked = jnp.where(allowed, scores, -1e30)
    row_peak = jnp.max(masked, axis=-1, keepdims=True)
    exponent = jnp.exp(masked - row_peak)
    return (exponent / jnp.sum(exponent, axis=-1, keepdims=True)).astype(jnp.bfloat16)


def shards(
    queries,
    keys,
    values,
    block_hidden_input,
    attention_out_weight,
    feedfwd_in_weight,
    feedfwd_out_weight,
    norm_gain_vector,
    norm_bias_vector,
    adapter_down_factors,
    adapter_up_factors,
    paged_key_cache,
    paged_value_cache,
    request_prompt_length,
    group_page_lookup,
    adapter_per_request,
    adapter_bank_slot,
):
    tok_rows = block_hidden_input.shape[0]
    groups = lax.axis_size("mlp")
    group_rows = tok_rows * groups
    head_cols = attention_out_weight.shape[0]
    local_heads = head_cols // HS
    column_index = lax.axis_index("mlp")
    query_all, key_all, value_all = (
        lax.all_to_all(queries, "mlp", split_axis=1, concat_axis=0, tiled=True),
        lax.all_to_all(keys, "mlp", split_axis=1, concat_axis=0, tiled=True),
        lax.all_to_all(values, "mlp", split_axis=1, concat_axis=0, tiled=True),
    )
    adapter_ids = adapter_per_request[0]
    matched = (
        adapter_ids[:, None] == jnp.arange(adapter_bank_slot.shape[0], dtype=jnp.int32)[None, :]
    )
    wanted = jnp.sum(jnp.where(matched, adapter_bank_slot[None, :], 0), axis=1)
    down_factor_piece = lax.all_gather(adapter_down_factors, "req", axis=0, tiled=True)
    up_factor_piece = lax.all_gather(adapter_up_factors, "req", axis=0, tiled=True)
    row_count = down_factor_piece.shape[0]
    onehot = (wanted[:, None] == jnp.arange(row_count, dtype=jnp.int32)[None, :]).astype(
        jnp.bfloat16
    )
    down_add = jnp.einsum(
        "rn,ndk->rdk", onehot, down_factor_piece, preferred_element_type=jnp.float32
    )
    up_add = jnp.einsum("rn,nkf->rkf", onehot, up_factor_piece, preferred_element_type=jnp.float32)
    down_factor_chosen = down_add
    up_factor_chosen = up_add
    down_factor_chosen = down_factor_chosen.astype(jnp.bfloat16)
    up_factor_chosen = up_factor_chosen.astype(jnp.bfloat16)
    request_ends = jnp.cumsum(request_prompt_length[0])
    positions = jnp.arange(group_rows, dtype=jnp.int32)
    segment = jnp.sum((positions[:, None] >= request_ends[None, :]).astype(jnp.int32), axis=1)
    chosen = segment[:, None] == jnp.arange(REQS, dtype=jnp.int32)[None, :]
    query_heads = query_all.reshape(group_rows, local_heads, HS)
    key_heads = key_all.reshape(group_rows, local_heads, HS)
    value_heads = value_all.reshape(group_rows, local_heads, HS)
    score_scale = HS ** (-0.5)
    block_rows = min(512, group_rows)
    scores = (
        jnp.einsum("qhd,khd->hqk", query_heads, key_heads, preferred_element_type=jnp.float32)
        * score_scale
    )
    allowed = (segment[:, None] == segment[None, :]) & (positions[None, :] <= positions[:, None])
    weights = softmax_rows(scores, allowed[None])
    mixed = jnp.einsum("hqk,khd->qhd", weights, value_heads, preferred_element_type=jnp.float32)
    pieces_out = mixed.astype(jnp.bfloat16).reshape(block_rows, head_cols)
    page_count = group_rows // PAGE
    key_pages_out = paged_key_cache.at[group_page_lookup[0]].set(
        key_all.reshape(page_count, PAGE, head_cols)
    )
    value_pages_out = paged_value_cache.at[group_page_lookup[0]].set(
        value_all.reshape(page_count, PAGE, head_cols)
    )
    row_block = pieces_out
    residual = block_hidden_input.astype(jnp.float32) + lax.psum_scatter(
        jnp.dot(row_block, attention_out_weight, preferred_element_type=jnp.float32).astype(
            jnp.bfloat16
        ),
        "mlp",
        scatter_dimension=0,
        tiled=True,
    ).astype(jnp.float32)
    normed_all = lax.all_gather(
        modulate(residual, norm_gain_vector, norm_bias_vector), "mlp", axis=0, tiled=True
    )
    width_dev = down_factor_chosen.shape[1]
    column_block = lax.dynamic_slice_in_dim(normed_all, column_index * width_dev, width_dev, 1)
    down_flat = jnp.transpose(down_factor_chosen, (1, 0, 2)).reshape(width_dev, REQS * ADAPTER_RANK)
    every_rank = jnp.dot(column_block, down_flat, preferred_element_type=jnp.float32).reshape(
        group_rows, REQS, ADAPTER_RANK
    )
    own_rank = jnp.sum(every_rank * chosen.astype(jnp.float32)[:, :, None], axis=1)
    lowrank = lax.psum(own_rank.astype(jnp.bfloat16), "mlp")
    spread = (chosen.astype(jnp.bfloat16)[:, :, None] * lowrank[:, None, :]).reshape(
        group_rows, REQS * ADAPTER_RANK
    )
    up_flat = up_factor_chosen.reshape(REQS * ADAPTER_RANK, up_factor_chosen.shape[2])
    preact = jnp.dot(normed_all, feedfwd_in_weight, preferred_element_type=jnp.float32) + jnp.dot(
        spread, up_flat, preferred_element_type=jnp.float32
    )
    activated = jax.nn.gelu(preact, approximate=True).astype(jnp.bfloat16)
    row_block = activated
    mlp_out = lax.psum_scatter(
        jnp.dot(row_block, feedfwd_out_weight, preferred_element_type=jnp.float32).astype(
            jnp.bfloat16
        ),
        "mlp",
        scatter_dimension=0,
        tiled=True,
    ).astype(jnp.float32)
    block_out = (residual + mlp_out).astype(jnp.bfloat16)
    return (block_out, key_pages_out, value_pages_out)


def solution(mesh):
    in_specs = (
        P(("req", "mlp"), None),
        P(("req", "mlp"), None),
        P(("req", "mlp"), None),
        P(("req", "mlp"), None),
        P("mlp", None),
        P(None, "mlp"),
        P("mlp", None),
        P(),
        P(),
        P("req", "mlp", None),
        P("req", None, "mlp"),
        P("req", None, "mlp"),
        P("req", None, "mlp"),
        P("req", None),
        P("req", None),
        P("req", None),
        P(),
    )
    out_specs = (P(("req", "mlp"), None), P("req", None, "mlp"), P("req", None, "mlp"))
    return jax.shard_map(shards, mesh=mesh, in_specs=in_specs, out_specs=out_specs, check_vma=False)
```

profile of v0, /device:TPU:0, one launch (start us, length us, event | category | flops | bytes accessed | tf_op | source)
XLA Modules:
  0.0 314.3 jit_solution(10489238109344441619)
XLA Ops:
  8.0 1.7 copy.93
  9.8 7.3 %all-to-all-start.1 = ((bf16[32,8,512]{2,0,1:T(8,128)(2,1)}), bf16[32,8,512]{2,0,1:T(8,128)(2,1)S(1)}, u32[]{:S(2)}, u32[]{:S(2)}) async-start(bf16[32,8,512]{2,0,1:T(8,128)(2,1)} %bitcast.59), calls=%async_computation.1 | async-start | bytes 524288 | tf_op jit(solution)/shard_map/all_to_all | solution.py:58
  17.1 0.7 copy.94
  17.8 8.2 %all-to-all-done.1 = bf16[32,8,512]{2,0,1:T(8,128)(2,1)S(1)} async-done(((bf16[32,8,512]{2,0,1:T(8,128)(2,1)}), bf16[32,8,512]{2,0,1:T(8,128)(2,1)S(1)}, u32[]{:S(2)}, u32[]{:S(2)}) %all-to-all-start.1) | async-done | bytes 262176 | tf_op jit(solution)/shard_map/all_to_all | solution.py:58
  26.0 3.6 %all-to-all-start = ((bf16[32,8,512]{2,0,1:T(8,128)(2,1)}), bf16[32,8,512]{2,0,1:T(8,128)(2,1)S(1)}, u32[]{:S(2)}, u32[]{:S(2)}) async-start(bf16[32,8,512]{2,0,1:T(8,128)(2,1)} %bitcast.60), calls=%async_computation | async-start | bytes 524288 | tf_op jit(solution)/shard_map/all_to_all | solution.py:57
  29.6 0.1 copy.50
  29.7 0.1 reduce
  29.8 0.7 copy.95
  30.5 0.1 convert_reduce_fusion
  30.6 7.5 %all-to-all-done = bf16[32,8,512]{2,0,1:T(8,128)(2,1)S(1)} async-done(((bf16[32,8,512]{2,0,1:T(8,128)(2,1)}), bf16[32,8,512]{2,0,1:T(8,128)(2,1)S(1)}, u32[]{:S(2)}, u32[]{:S(2)}) %all-to-all-start) | async-done | bytes 262176 | tf_op jit(solution)/shard_map/all_to_all | solution.py:57
  38.1 3.6 %all-to-all-start.2 = ((bf16[32,8,512]{2,0,1:T(8,128)(2,1)}), bf16[32,8,512]{2,0,1:T(8,128)(2,1)S(1)}, u32[]{:S(2)}, u32[]{:S(2)}) async-start(bf16[32,8,512]{2,0,1:T(8,128)(2,1)} %bitcast.61), calls=%async_computation.2 | async-start | bytes 524288 | tf_op jit(solution)/shard_map/all_to_all | solution.py:59
  41.7 0.0 reduce-scatter.3.cloned.1.call-start
  41.8 0.1 fusion.28
  41.9 0.1 reshape.198
  41.9 0.1 reshape.197
  42.0 0.5 fusion.48
  42.5 0.3 fusion.16
  42.8 7.4 %all-to-all-done.2 = bf16[32,8,512]{2,0,1:T(8,128)(2,1)S(1)} async-done(((bf16[32,8,512]{2,0,1:T(8,128)(2,1)}), bf16[32,8,512]{2,0,1:T(8,128)(2,1)S(1)}, u32[]{:S(2)}, u32[]{:S(2)}) %all-to-all-start.2) | async-done | bytes 262176 | tf_op jit(solution)/shard_map/all_to_all | solution.py:59
  50.2 0.1 reshape.199
  50.3 0.4 convolution_convert_fusion.3
  50.7 5.5 %convolution_convert_fusion.1 = bf16[256,5120]{1,0:T(8,128)(2,1)} fusion(bf16[256,512]{0,1:T(8,128)(2,1)S(1)} %bitcast.67, bf16[512,5120]{1,0:T(8,128)(2,1)} %param.21), kind=kOutput, calls=%fused_computation.4 | convolution fusion | flops 1343488000 | bytes 8126464 | tf_op jit(solution)/shard_map/dot_general | solution.py:106
  56.3 0.0 all-gather.6.cloned.1.call-start
  56.4 0.9 copy-done.6
  57.2 0.8 copy.58
  58.0 0.0 all-gather.8.cloned.1.call-start
  58.1 0.5 all-gather.8.cloned.1.call-update
  58.6 0.0 all-gather.4.cloned.1.call-start
  58.7 66.8 %reduce-scatter.3.cloned.1.call-done = bf16[32,5120]{1,0:T(8,128)(2,1)} async-done(((bf16[256,5120]{1,0:T(8,128)(2,1)}), bf16[32,5120]{1,0:T(8,128)(2,1)}) %reduce-scatter.3.cloned.1.call-update) | async-done | bytes 327696 | tf_op jit(solution)/shard_map/reduce_scatter | solution.py:105
  125.5 1.2 fusion.20
  126.6 1.2 multiply_reduce_fusion
  127.9 1.9 add_convert_fusion.1
  129.8 0.0 reduce-scatter.5.cloned.1.call-start
  129.9 0.2 select_reduce_fusion
  130.1 0.0 all-gather.6.cloned.1.call-done
  130.1 1.7 fusion.17
  131.8 0.0 all-gather.8.cloned.1.call-done
  131.8 4.1 %fusion.3 = bf16[16,16,1728]{2,0,1:T(8,128)(2,1)S(1)} fusion(bf16[64,16,1728]{2,1,0:T(8,128)(2,1)} %all-gather.8.cloned.1.call-done, s32[16]{0:T(128)S(1)} %select_reduce_fusion), kind=kOutput, calls=%fused_computation.10 | convolution fusion | flops 57066496 | bytes 4423744 | tf_op jit(solution)/shard_map/rn,nkf->rkf/dot_general | solution.py:75
  135.9 47.4 %all-gather.4.cloned.1.call-done = bf16[256,5120]{1,0:T(8,128)(2,1)} async-done(((bf16[32,5120]{1,0:T(8,128)(2,1)}), bf16[256,5120]{1,0:T(8,128)(2,1)}) %all-gather.4.cloned.1.call-update) | async-done | bytes 2621456 | tf_op jit(solution)/shard_map/all_gather | solution.py:113
  183.4 1.3 fusion.18
  184.6 19.5 %psum.7 = bf16[256,16]{0,1:T(8,128)(2,1)S(1)} all-reduce(bf16[256,16]{0,1:T(8,128)(2,1)S(1)} %fusion.18), channel_id=1, replica_groups=mesh['req'=4,'mlp'=8] {'mlp'}, use_global_device_ids=true, to_apply=%region_9.10 | all-reduce | flops 4096 | bytes 16384 | tf_op jit(solution)/shard_map/psum | solution.py:123
  204.1 0.5 convolution_bitcast_fusion
  204.6 32.4 %convolution_convert_fusion = bf16[256,5120]{1,0:T(8,128)(2,1)} fusion(bf16[1728,5120]{1,0:T(8,128)(2,1)} %param.23, f32[256,1728]{0,1:T(8,128)S(1)} %convolution_bitcast_fusion, bf16[256,5120]{1,0:T(8,128)(2,1)} %all-gather.4.cloned.1.call-done, bf16[5120,1728]{0,1:T(8,128)(2,1)} %param.22), kind=kOutput, calls=%fused_computation.3 | convolution fusion | flops 9065431040 | bytes 42401792 | tf_op jit(solution)/shard_map/dot_general | solution.py:134
  237.1 0.6 copy-done.14
  237.7 0.4 copy-done.5
  238.1 0.6 scatter_fusion
  238.7 0.6 scatter_fusion.1
  239.4 65.5 %reduce-scatter.5.cloned.1.call-done = bf16[32,5120]{1,0:T(8,128)(2,1)} async-done(((bf16[256,5120]{1,0:T(8,128)(2,1)}), bf16[32,5120]{1,0:T(8,128)(2,1)}) %reduce-scatter.5.cloned.1.call-update) | async-done | bytes 327696 | tf_op jit(solution)/shard_map/reduce_scatter | solution.py:133
  304.9 1.8 add_convert_fusion
  (36 shorter events, 0.2 us)
Async XLA Ops:
  8.0 9.0 %copy-start.7 = (bf16[32,4096]{1,0:T(8,128)(2,1)S(1)}, bf16[32,4096]{1,0:T(8,128)(2,1)}, u32[]{:S(2)}) copy-start(bf16[32,4096]{1,0:T(8,128)(2,1)} %param.17) | copy-start | bytes 786436
  8.0 21.8 %copy-start.8 = (bf16[32,4096]{1,0:T(8,128)(2,1)S(1)}, bf16[32,4096]{1,0:T(8,128)(2,1)}, u32[]{:S(2)}) copy-start(bf16[32,4096]{1,0:T(8,128)(2,1)} %param.19) | copy-start | bytes 786436
  8.0 21.5 %copy-start.11 = (s32[1,16]{1,0:T(1,128)S(1)}, s32[1,16]{1,0:T(1,128)}, u32[]{:S(2)}) copy-start(s32[1,16]{1,0:T(1,128)} %param.30) | copy-start | bytes 196
  9.8 16.2 %all-to-all-start.1 = ((bf16[32,8,512]{2,0,1:T(8,128)(2,1)}), bf16[32,8,512]{2,0,1:T(8,128)(2,1)S(1)}, u32[]{:S(2)}, u32[]{:S(2)}) async-start(bf16[32,8,512]{2,0,1:T(8,128)(2,1)} %bitcast.59), calls=%async_computation.1 | async-start | bytes 524288 | tf_op jit(solution)/shard_map/all_to_all | solution.py:58
  26.0 12.2 %all-to-all-start = ((bf16[32,8,512]{2,0,1:T(8,128)(2,1)}), bf16[32,8,512]{2,0,1:T(8,128)(2,1)S(1)}, u32[]{:S(2)}, u32[]{:S(2)}) async-start(bf16[32,8,512]{2,0,1:T(8,128)(2,1)} %bitcast.60), calls=%async_computation | async-start | bytes 524288 | tf_op jit(solution)/shard_map/all_to_all | solution.py:57
  38.1 12.1 %all-to-all-start.2 = ((bf16[32,8,512]{2,0,1:T(8,128)(2,1)}), bf16[32,8,512]{2,0,1:T(8,128)(2,1)S(1)}, u32[]{:S(2)}, u32[]{:S(2)}) async-start(bf16[32,8,512]{2,0,1:T(8,128)(2,1)} %bitcast.61), calls=%async_computation.2 | async-start | bytes 524288 | tf_op jit(solution)/shard_map/all_to_all | solution.py:59
  41.7 83.8 %reduce-scatter.3.cloned.1.call-start = ((), (), s32[]{:S(2)}) async-start(), calls=%async_computation.5 | async-start | bytes 2949120 | tf_op jit(solution)/shard_map/reduce_scatter | solution.py:105
  56.3 1.0 copy-start.6
  56.3 69.2 %copy-start = (bf16[32,5120]{1,0:T(8,128)(2,1)S(1)}, bf16[32,5120]{1,0:T(8,128)(2,1)}, u32[]{:S(2)}) copy-start(bf16[32,5120]{1,0:T(8,128)(2,1)} %param.20) | copy-start | bytes 983044
  56.3 71.6 %copy-start.9 = (f32[5120]{0:T(1024)S(1)}, f32[5120]{0:T(1024)}, u32[]{:S(2)}) copy-start(f32[5120]{0:T(1024)} %param.25) | copy-start | bytes 61444
  56.3 71.6 %copy-start.10 = (f32[5120]{0:T(1024)S(1)}, f32[5120]{0:T(1024)}, u32[]{:S(2)}) copy-start(f32[5120]{0:T(1024)} %param.24) | copy-start | bytes 61444
  56.3 73.6 %copy-start.12 = (s32[64]{0:T(128)S(1)}, s32[64]{0:T(128)}, u32[]{:S(2)}) copy-start(s32[64]{0:T(128)} %param.33) | copy-start | bytes 772
  56.3 73.6 %copy-start.13 = (s32[1,16]{1,0:T(1,128)S(1)}, s32[1,16]{1,0:T(1,128)}, u32[]{:S(2)}) copy-start(s32[1,16]{1,0:T(1,128)} %param.32) | copy-start | bytes 196
  56.3 73.8 %all-gather.6.cloned.1.call-start = ((), (), s32[]{:S(2)}) async-start(), calls=%async_computation.7 | async-start | bytes 1638400 | tf_op jit(solution)/shard_map/all_gather | solution.py:66
  58.0 73.8 %all-gather.8.cloned.1.call-start = ((), (), s32[]{:S(2)}) async-start(), calls=%async_computation.8 | async-start | bytes 4587520 | tf_op jit(solution)/shard_map/all_gather | solution.py:67
  58.6 124.7 %all-gather.4.cloned.1.call-start = ((), (), s32[]{:S(2)}) async-start(), calls=%async_computation.6 | async-start | bytes 2949120 | tf_op jit(solution)/shard_map/all_gather | solution.py:113
  129.8 175.0 %reduce-scatter.5.cloned.1.call-start = ((), (), s32[]{:S(2)}) async-start(), calls=%async_computation.9 | async-start | bytes 2949120 | tf_op jit(solution)/shard_map/reduce_scatter | solution.py:133
  237.1 0.7 copy-start.14
  237.1 1.0 copy-start.5
  237.1 1.7 copy-start.3
  237.1 67.8 %copy-start.1 = (bf16[32,5120]{1,0:T(8,128)(2,1)S(1)}, bf16[32,5120]{1,0:T(8,128)(2,1)}, u32[]{:S(2)}) copy-start(bf16[32,5120]{1,0:T(8,128)(2,1)} %reduce-scatter.3.cloned.1.call-done) | copy-start | bytes 983044
  238.7 68.0 %copy-start.4 = (bf16[3,128,512]{2,1,0:T(8,128)(2,1)}, bf16[3,128,512]{2,1,0:T(8,128)(2,1)S(1)}, u32[]{:S(2)}) copy-start(bf16[3,128,512]{2,1,0:T(8,128)(2,1)S(1)} %scatter_fusion) | copy-start | bytes 1179652
  239.4 67.3 %copy-start.2 = (bf16[3,128,512]{2,1,0:T(8,128)(2,1)}, bf16[3,128,512]{2,1,0:T(8,128)(2,1)S(1)}, u32[]{:S(2)}) copy-start(bf16[3,128,512]{2,1,0:T(8,128)(2,1)S(1)} %scatter_fusion.1) | copy-start | bytes 1179652
Sparse Core Ops, SparseCore 0:
  56.4 68.9 reduce-scatter.2
  237.2 67.5 reduce-scatter.4
Sparse Core Ops, SparseCore 1:
  58.9 16.9 all-gather.5
  77.4 31.4 all-gather.7
  129.9 53.4 all-gather.3
where the time goes:
time: 315 us; the launch traced here: 314 us
  waiting for transfers between devices  203 us (64%)
  matrix products  46.8 us (15%)
  blocking collectives  19.5 us (6%)
  between operations  15.9 us (5%)
  starting transfers between devices  14.7 us (5%)
  local copies, waits for them, and re-layouts  7.4 us (2%)
  other arithmetic  6.63 us (2%)
    reduce_scatter x1, waiting for transfers between devices, shards(): lax.psum_scatter(jnp.dot(row_block, attention_out_weight, preferred_eleme...  66.8 us
    reduce_scatter x1, waiting for transfers between devices, shards(): lax.psum_scatter(jnp.dot(row_block, feedfwd_out_weight, preferred_element...  65.5 us
    all_gather x1, waiting for transfers between devices, shards(): lax.all_gather(modulate(residual, norm_gain_vector, norm_bias_vector), 'm...  47.4 us
    dot_general x1, matrix products, shards(): jnp.dot(row_block, feedfwd_out_weight, preferred_element_type=jnp.float32)  32.4 us
    psum x1, blocking collectives, shards(): lowrank = lax.psum(own_rank.astype(jnp.bfloat16), 'mlp')  19.5 us
    all_to_all x1, waiting for transfers between devices, shards(): lax.all_to_all(keys, 'mlp', split_axis=1, concat_axis=0, tiled=True)  8.19 us
    all_to_all x1, waiting for transfers between devices, shards(): lax.all_to_all(queries, 'mlp', split_axis=1, concat_axis=0, tiled=True)  7.5 us
    all_to_all x1, waiting for transfers between devices, shards(): lax.all_to_all(values, 'mlp', split_axis=1, concat_axis=0, tiled=True)  7.41 us
  transfers between devices with their start and end apart: 8, of which 6 were waited for; matrix products, arithmetic and copies ran while one was open for 5% of the time, Pallas kernels for 0%

commit v1 on v0

v1 whole, which is shorter than its diff:
```python
import functools

import jax
import jax.numpy as jnp
from jax import lax
from jax.experimental import pallas as pl
from jax.experimental.pallas import tpu as pltpu
from jax.sharding import PartitionSpec as P

HS = 128
ADAPTER_RANK = 16
REQS = 16
PAGE = 128
EPS = 1e-06
MIB = 1024 * 1024
PREFERRED, CHUNK, SPAN, PARTNER_A, PARTNER_B, ORDERS = range(6)
BF16 = jnp.bfloat16
F32 = jnp.float32


def params(mib=48):
    return pltpu.CompilerParams(vmem_limit_bytes=mib * MIB)


SMALL = pl.CostEstimate(flops=0, bytes_accessed=1, transcendentals=0)
SIDE = pl.CostEstimate(flops=0, bytes_accessed=8 * MIB, transcendentals=0)


def exchange(x, axis, mask):
    size = lax.axis_size(axis)
    return lax.ppermute(x, axis, [(i, i ^ mask) for i in range(size)])


def block_offsets(masks):
    offsets = [0]
    for mask in reversed(masks):
        offsets = offsets + [o ^ mask for o in offsets]
    return offsets


def reduce_step(kept, sent, mask):
    rows, width = kept.shape
    half = rows // 2

    def kernel(kept_ref, got_ref, out_ref, next_ref):
        out_ref[...] = kept_ref[:half].astype(F32) + got_ref[:half].astype(F32)
        next_ref[...] = (kept_ref[half:].astype(F32) + got_ref[half:].astype(F32)).astype(BF16)

    return pl.pallas_call(
        kernel,
        out_shape=[jax.ShapeDtypeStruct((half, width), t) for t in (F32, BF16)],
        cost_estimate=SMALL,
        compiler_params=params(),
        name="reduce_step",
    )(kept, exchange(sent, "mlp", mask))


def reduce_rest(kept, sent, masks):
    for mask in masks[:-1]:
        kept, sent = reduce_step(kept, sent, mask)
    return kept, exchange(sent, "mlp", masks[-1])


def gather_most(rows, masks):
    for mask in masks[:0:-1]:
        rows = jnp.concatenate([rows, exchange(rows, "mlp", mask)], axis=0)
    return rows, exchange(rows, "mlp", masks[0])


def out_projection(control, blocks, order, weight, start, width, tile):
    count, rows, depth = blocks.shape
    total = count * rows
    first = start // tile

    def kernel(control_ref, x_ref, w_ref, kept_ref, sent_ref, x_scratch):
        @pl.when(pl.program_id(0) == 0)
        def _():
            for i in range(count):
                at = control_ref[order + i] if isinstance(order, int) else order[i]
                x_scratch[i * rows : (i + 1) * rows, :] = x_ref[at]

        y = jnp.dot(x_scratch[...], w_ref[...], preferred_element_type=F32).astype(BF16)
        kept_ref[...] = y[: total // 2]
        sent_ref[...] = y[total // 2 :]

    half = jax.ShapeDtypeStruct((total // 2, width), BF16)
    return pl.pallas_call(
        kernel,
        grid_spec=pltpu.PrefetchScalarGridSpec(
            num_scalar_prefetch=1,
            grid=(width // tile,),
            in_specs=[
                pl.BlockSpec((count, rows, depth), lambda j, c: (0, 0, 0)),
                pl.BlockSpec((depth, tile), lambda j, c: (0, first + j)),
            ],
            out_specs=[pl.BlockSpec((total // 2, tile), lambda j, c: (0, j))] * 2,
            scratch_shapes=[pltpu.VMEM((total, depth), BF16)],
        ),
        out_shape=[half, half],
        cost_estimate=SMALL,
        compiler_params=params(),
        name="out_projection",
    )(control, blocks, weight)


def norm(hidden, halves, gain, bias, outs_widths):
    rows, width = hidden.shape
    widths = [a.shape[1] for a, _ in halves]
    flat = [x for pair in halves for x in pair]

    def kernel(*refs):
        hidden_ref, gain_ref, bias_ref = refs[:3]
        parts = refs[3 : 3 + len(flat)]
        residual_ref = refs[3 + len(flat)]
        outs = refs[4 + len(flat) :]
        start = 0
        for i, chunk in enumerate(widths):
            cols = slice(start, start + chunk)
            residual_ref[:, cols] = hidden_ref[:, cols].astype(F32) + (
                parts[2 * i][...].astype(F32) + parts[2 * i + 1][...].astype(F32)
            )
            start += chunk
        residual = residual_ref[...]
        centered = residual - jnp.sum(residual, axis=1, keepdims=True) * (1.0 / width)
        var = jnp.sum(centered * centered, axis=1, keepdims=True) * (1.0 / width)
        normed = centered * lax.rsqrt(var + EPS) * gain_ref[...] + bias_ref[...]
        start = 0
        for out, chunk in zip(outs, outs_widths):
            out[...] = normed[:, start : start + chunk].astype(BF16)
            start += chunk

    return pl.pallas_call(
        kernel,
        out_shape=[jax.ShapeDtypeStruct((rows, width), F32)]
        + [jax.ShapeDtypeStruct((rows, chunk), BF16) for chunk in outs_widths],
        cost_estimate=SMALL,
        compiler_params=params(),
        name="norm",
    )(hidden, gain.reshape(1, width), bias.reshape(1, width), *flat)


def feedfwd_in(control, first, second, swap, late, weight, acc=None):
    half, piece = first[1].shape
    total, units = 2 * half, weight.shape[0]
    rows = total // len(swap)
    per = half // rows
    pieces = first[0].shape[1] // piece

    def times(x, w):
        return lax.dot_general(x, w, (((1,), (1,)), ((), ())), preferred_element_type=F32)

    def kernel(control_ref, a0, a1, b0, b1, w_ref, *refs):
        out_ref = refs[-1]

        @pl.when(pl.program_id(0) == 0)
        def _():
            y = times(jnp.concatenate([a0[...], a1[...]], axis=0), w_ref[...])
            out_ref[...] = y if acc is None else refs[0][...] + y

        @pl.when(pl.program_id(0) == 1)
        def _():
            x = [(b0 if i < per else b1)[(i % per) * rows : (i % per + 1) * rows, :] for i in swap]
            out_ref[...] += times(jnp.concatenate(x, axis=0), w_ref[...])

    which = (lambda c: 1 - c[PREFERRED]) if late else (lambda c: c[PREFERRED])
    own = pl.BlockSpec((half, piece), lambda k, c: (0, which(c)))
    got = pl.BlockSpec((half, piece), lambda k, c: (0, 0))
    full = pl.BlockSpec((total, units), lambda k, c: (0, 0))
    return pl.pallas_call(
        kernel,
        grid_spec=pltpu.PrefetchScalarGridSpec(
            num_scalar_prefetch=1,
            grid=(2,),
            in_specs=[own, got, own, got, pl.BlockSpec((units, piece), lambda k, c: (0, k * pieces + which(c)))]
            + ([] if acc is None else [full]),
            out_specs=full,
        ),
        out_shape=jax.ShapeDtypeStruct((total, units), F32),
        cost_estimate=pl.CostEstimate(
            flops=4 * total * piece * units, bytes_accessed=4 * piece * units, transcendentals=0
        ),
        compiler_params=params(),
        name="feedfwd_in",
    )(control, *first, *second, weight, *([] if acc is None else [acc]))


def down_products(control, first, second, groups, down_flat, segment):
    half, piece = first[1].shape
    total, count = 2 * half, groups
    rows = total // count
    per = half // rows
    width = down_flat.shape[1]
    reps = 1
    while (reps * width) % 128:
        reps *= 2
    span = reps * width
    if reps > 1:
        pos = lax.rem(lax.axis_index("mlp"), reps)
        down_flat = jnp.concatenate(
            [jnp.where(pos == i, down_flat, jnp.zeros_like(down_flat)) for i in range(reps)], axis=1
        )
    reqs = REQS
    rank = down_flat.shape[0] // reqs

    def kernel(control_ref, a0, a1, b0, b1, down_ref, segment_ref, out_ref, x_scratch):
        for chunk, order, lower, upper in ((0, ORDERS, a0, a1), (1, ORDERS + groups, b0, b1)):

            @pl.when(control_ref[CHUNK] == chunk)
            def _():
                for i in range(count):
                    start = pl.multiple_of(control_ref[order + i] * rows, rows)
                    x = (lower if i < per else upper)[(i % per) * rows : (i % per + 1) * rows, :]
                    x_scratch[pl.ds(start, rows), :] = x

        every_rank = lax.dot_general(
            down_ref[...], x_scratch[...], (((1,), (1,)), ((), ())), preferred_element_type=F32
        ).reshape(reqs, rank, total)
        chosen = lax.broadcasted_iota(jnp.int32, (reqs, total), 0) == segment_ref[...]
        out_ref[...] = jnp.sum(jnp.where(chosen[:, None, :], every_rank, 0.0), axis=0)

    own = pl.BlockSpec((half, span), lambda k, c: (0, c[PREFERRED] * (piece // span) + c[SPAN]))
    got = pl.BlockSpec((half, span), lambda k, c: (0, c[SPAN]))
    return pl.pallas_call(
        kernel,
        grid_spec=pltpu.PrefetchScalarGridSpec(
            num_scalar_prefetch=1,
            grid=(1,),
            in_specs=[own, got, own, got]
            + [pl.BlockSpec(x.shape, lambda k, c: (0, 0)) for x in (down_flat, segment)],
            out_specs=pl.BlockSpec((rank, total), lambda k, c: (0, 0)),
            scratch_shapes=[pltpu.VMEM((total, span), BF16)],
        ),
        out_shape=jax.ShapeDtypeStruct((rank, total), F32),
        cost_estimate=SMALL,
        compiler_params=params(),
        name="down_products",
    )(control, *first, *second, down_flat, segment)


def preferred(me, groups):
    return lax.rem(me // (groups // 4), 2)


def stack(control, rows, got, key):
    count, width = rows.shape
    piece = width // 2

    def kernel(control_ref, rows_ref, got_ref, out_ref, first_ref, second_ref):
        out_ref[:count, :] = rows_ref[...]
        out_ref[count:, :] = got_ref[...]
        for which in range(2):

            @pl.when(control_ref[key] == which)
            def _():
                for ref, at in ((first_ref, which), (second_ref, 1 - which)):
                    ref[:count, :] = rows_ref[:, at * piece : (at + 1) * piece]
                    ref[count:, :] = got_ref[:, at * piece : (at + 1) * piece]

    def whole(*shape):
        return pl.BlockSpec(shape, lambda j, c: (0, 0))

    return pl.pallas_call(
        kernel,
        grid_spec=pltpu.PrefetchScalarGridSpec(
            num_scalar_prefetch=1,
            grid=(1,),
            in_specs=[whole(count, width)] * 2,
            out_specs=[whole(2 * count, width)] + [whole(2 * count, piece)] * 2,
        ),
        out_shape=[jax.ShapeDtypeStruct((2 * count, w), BF16) for w in (width, piece, piece)],
        cost_estimate=SMALL,
        compiler_params=params(),
        name="stack",
    )(control, rows, got)


def feedfwd_out_first(control, acc, lowrank, segment, up_flat, weight, width, tile, groups):
    total, units = acc.shape
    reqs, rank = REQS, lowrank.shape[0]
    rows = total // groups

    def kernel(control_ref, acc_ref, low_ref, segment_ref, up_ref, w_ref, act_ref, kept_ref, sent_ref, up_scratch):
        @pl.when(pl.program_id(0) == 0)
        def _():
            low = low_ref[...].astype(BF16).astype(F32)
            chosen = lax.broadcasted_iota(jnp.int32, (reqs, total), 0) == segment_ref[...]
            spread = jnp.where(chosen[:, None, :], low[None, :, :], 0.0).reshape(reqs * rank, total)
            up_scratch[...] = lax.dot_general(
                spread.astype(BF16),
                up_ref[...],
                (((0,), (0,)), ((), ())),
                preferred_element_type=F32,
            )
            for i in range(groups):
                here = slice(i * rows, (i + 1) * rows)
                start = pl.multiple_of(control_ref[ORDERS + i] * rows, rows)
                preact = acc_ref[here, :] + up_scratch[pl.ds(start, rows), :]
                act_ref[here, :] = jax.nn.gelu(preact, approximate=True).astype(BF16)

        y = jnp.dot(act_ref[...], w_ref[...], preferred_element_type=F32).astype(BF16)
        kept_ref[...] = y[: total // 2]
        sent_ref[...] = y[total // 2 :]

    half = jax.ShapeDtypeStruct((total // 2, width), BF16)

    def whole(*shape):
        return pl.BlockSpec(shape, lambda j, c: (0,) * len(shape))

    return pl.pallas_call(
        kernel,
        grid_spec=pltpu.PrefetchScalarGridSpec(
            num_scalar_prefetch=1,
            grid=(width // tile,),
            in_specs=[
                whole(total, units),
                whole(rank, total),
                whole(1, total),
                whole(reqs * rank, units),
                pl.BlockSpec((units, tile), lambda j, c: (0, j)),
            ],
            out_specs=[whole(total, units)]
            + [pl.BlockSpec((total // 2, tile), lambda j, c: (0, j))] * 2,
            scratch_shapes=[pltpu.VMEM((total, units), F32)],
        ),
        out_shape=[jax.ShapeDtypeStruct((total, units), BF16), half, half],
        cost_estimate=SMALL,
        compiler_params=params(),
        name="feedfwd_out_first",
    )(control, acc, lowrank, segment, up_flat, weight)


def gather_req(x, masks):
    parts = [x]
    for mask in masks:
        parts = parts + [exchange(part, "req", mask) for part in parts]
    return parts


def pick(held_at, *banks):
    reqs = held_at.shape[0]
    slots, rank = banks[0][0].shape[:2]
    count = len(banks[0])

    def kernel(at_ref, *refs):
        parts = [refs[i * count : (i + 1) * count] for i in range(len(banks))]
        outs = refs[len(banks) * count : -1]
        sems = refs[-1]

        def fetch(i, part, r):
            to = outs[i].at[r * rank : (r + 1) * rank, :]
            return pltpu.make_async_copy(part.at[lax.rem(at_ref[r], slots)], to, sems.at[i, r])

        for r in range(reqs):
            for p in range(count):

                @pl.when(at_ref[r] // slots == p)
                def _():
                    for i in range(len(banks)):
                        fetch(i, parts[i][p], r).start()

        for r in range(reqs):
            for i in range(len(banks)):
                fetch(i, parts[i][0], r).wait()

    return pl.pallas_call(
        kernel,
        grid_spec=pltpu.PrefetchScalarGridSpec(
            num_scalar_prefetch=1,
            grid=(1,),
            in_specs=[pl.BlockSpec(memory_space=pl.ANY)] * (len(banks) * count),
            out_specs=[pl.BlockSpec(memory_space=pl.ANY)] * len(banks),
            scratch_shapes=[pltpu.SemaphoreType.DMA((len(banks), reqs))],
        ),
        out_shape=[jax.ShapeDtypeStruct((reqs * rank, b[0].shape[2]), BF16) for b in banks],
        cost_estimate=SIDE,
        compiler_params=params(),
        name="pick",
    )(held_at, *(part for bank in banks for part in bank))


def join(arrays, groups):
    rows, width = arrays[0].shape
    depth = width // groups

    per = 2
    steps = groups // per

    def kernel(*refs):
        out_ref = refs[-1]
        for i, ref in enumerate(refs[:-1]):
            for g in range(per):
                out_ref[g, :, i * depth : (i + 1) * depth] = ref[:, g * depth : (g + 1) * depth]

    return pl.pallas_call(
        kernel,
        grid=(steps,),
        in_specs=[pl.BlockSpec((rows, per * depth), lambda g: (0, g))] * len(arrays),
        out_specs=pl.BlockSpec((per, rows, len(arrays) * depth), lambda g: (g, 0, 0)),
        out_shape=jax.ShapeDtypeStruct((groups, rows, len(arrays) * depth), BF16),
        cost_estimate=SMALL,
        compiler_params=params(60),
        name="join",
    )(*arrays)


def attend(control, joined, segment, count, weight, width, tile):
    total = joined.shape[0]
    depth = joined.shape[1] // 3
    rows = total // count

    def kernel(control_ref, joined_ref, col_ref, row_ref, w_ref, att_ref, kept_ref, sent_ref, x_scratch):
        @pl.when(pl.program_id(0) == 0)
        def _():
            across = lax.broadcasted_iota(jnp.int32, (total, total), 1)
            down = lax.broadcasted_iota(jnp.int32, (total, total), 0)
            allowed = (col_ref[...] == row_ref[...]) & (across <= down)
            for head in range(depth // HS):
                q, k, v = (
                    joined_ref[:, i * depth + head * HS : i * depth + (head + 1) * HS] for i in range(3)
                )
                scores = lax.dot_general(
                    q, k, (((1,), (1,)), ((), ())), preferred_element_type=F32
                ) * (HS ** (-0.5))
                masked = jnp.where(allowed, scores, -1e30)
                exponent = jnp.exp(masked - jnp.max(masked, axis=1, keepdims=True))
                weights = (exponent / jnp.sum(exponent, axis=1, keepdims=True)).astype(BF16)
                mixed = jnp.dot(weights, v, preferred_element_type=F32).astype(BF16)
                att_ref[:, :, head * HS : (head + 1) * HS] = mixed.reshape(count, rows, HS)
            for i in range(count):
                x_scratch[i * rows : (i + 1) * rows, :] = att_ref[control_ref[ORDERS + i]]

        y = jnp.dot(x_scratch[...], w_ref[...], preferred_element_type=F32).astype(BF16)
        kept_ref[...] = y[: total // 2]
        sent_ref[...] = y[total // 2 :]

    half = jax.ShapeDtypeStruct((total // 2, width), BF16)
    return pl.pallas_call(
        kernel,
        grid_spec=pltpu.PrefetchScalarGridSpec(
            num_scalar_prefetch=1,
            grid=(width // tile,),
            in_specs=[
                pl.BlockSpec((total, 3 * depth), lambda j, o: (0, 0)),
                pl.BlockSpec((total, 1), lambda j, o: (0, 0)),
                pl.BlockSpec((1, total), lambda j, o: (0, 0)),
                pl.BlockSpec((depth, tile), lambda j, o: (0, j)),
            ],
            out_specs=[pl.BlockSpec((count, rows, depth), lambda j, o: (0, 0, 0))]
            + [pl.BlockSpec((total // 2, tile), lambda j, o: (0, j))] * 2,
            scratch_shapes=[pltpu.VMEM((total, depth), BF16)],
        ),
        out_shape=[jax.ShapeDtypeStruct((count, rows, depth), BF16), half, half],
        cost_estimate=SMALL,
        compiler_params=params(),
        name="attend",
    )(control, joined, segment.reshape(total, 1), segment.reshape(1, total), weight)


def write_pages(joined, lookup, key_cache, value_cache):
    pages, page, depth = key_cache.shape
    blocks = lookup.shape[0]
    hits = lookup[None, :] == jnp.arange(pages, dtype=jnp.int32)[:, None]
    source = jnp.sum(jnp.where(hits, jnp.arange(1, blocks + 1, dtype=jnp.int32)[None, :], 0), axis=1) - 1

    def kernel(source_ref, k_ref, v_ref, key_cache_ref, value_cache_ref, key_ref, value_ref):
        fresh = source_ref[pl.program_id(0)] >= 0

        @pl.when(fresh)
        def _():
            key_ref[0] = k_ref[...]
            value_ref[0] = v_ref[...]

        @pl.when(jnp.logical_not(fresh))
        def _():
            key_ref[...] = key_cache_ref[...]
            value_ref[...] = value_cache_ref[...]

    def block(part):
        return pl.BlockSpec((page, depth), lambda p, source: (jnp.maximum(source[p], 0), part))

    paged = pl.BlockSpec((1, page, depth), lambda p, source: (p, 0, 0))
    return pl.pallas_call(
        kernel,
        grid_spec=pltpu.PrefetchScalarGridSpec(
            num_scalar_prefetch=1,
            grid=(pages,),
            in_specs=[block(1), block(2), paged, paged],
            out_specs=[paged, paged],
        ),
        out_shape=[jax.ShapeDtypeStruct(key_cache.shape, BF16)] * 2,
        cost_estimate=SIDE,
        compiler_params=params(),
        name="write_pages",
    )(source, joined, joined, key_cache, value_cache)


def shards(
    queries,
    keys,
    values,
    block_hidden_input,
    attention_out_weight,
    feedfwd_in_weight,
    feedfwd_out_weight,
    norm_gain_vector,
    norm_bias_vector,
    adapter_down_factors,
    adapter_up_factors,
    paged_key_cache,
    paged_value_cache,
    request_prompt_length,
    group_page_lookup,
    adapter_per_request,
    adapter_bank_slot,
):
    tok_rows, width = block_hidden_input.shape
    groups = lax.axis_size("mlp")
    group_rows = tok_rows * groups
    head_cols = attention_out_weight.shape[0]
    me = lax.axis_index("mlp")
    chunk = width // 2
    bits = [1 << i for i in range(groups.bit_length() - 1)]
    minor = len(bits) - 2
    masks_a = bits
    masks_b = bits[minor : minor + 1] + bits[:minor] + bits[minor + 1 :]
    offsets_a, offsets_b = block_offsets(masks_a), block_offsets(masks_b)
    width_dev = width // groups
    control = jnp.concatenate(
        [
            jnp.stack(
                [
                    preferred(me, groups),
                    me // (groups // 2),
                    lax.rem(me, groups // 4) * width_dev // (-(-width_dev // 128) * 128),
                    preferred(me ^ masks_a[0], groups),
                    preferred(me ^ masks_b[0], groups),
                ]
            ),
            jnp.asarray(offsets_a + offsets_b, jnp.int32) ^ me,
        ]
    ).astype(jnp.int32)
    b_of_a = [offsets_b.index(o) for o in offsets_a]
    a_of_b = [offsets_a.index(o) for o in offsets_b]

    req_masks = [1 << i for i in range(lax.axis_size("req").bit_length() - 1)]
    down_bank = gather_req(jnp.swapaxes(adapter_down_factors, 1, 2), req_masks[::-1])
    up_bank = gather_req(adapter_up_factors, req_masks[::-1])
    slots = adapter_down_factors.shape[0]
    adapter_ids = adapter_per_request[0]
    matched = (
        adapter_ids[:, None] == jnp.arange(adapter_bank_slot.shape[0], dtype=jnp.int32)[None, :]
    )
    wanted = jnp.sum(jnp.where(matched, adapter_bank_slot[None, :], 0), axis=1)
    part_owner = jnp.asarray(block_offsets(req_masks), jnp.int32) ^ lax.axis_index("req")
    held_slot = (
        part_owner[:, None] * slots + jnp.arange(slots, dtype=jnp.int32)[None, :]
    ).reshape(-1)
    hit = wanted[:, None] == held_slot[None, :]
    held_at = jnp.sum(jnp.where(hit, jnp.arange(hit.shape[1], dtype=jnp.int32)[None, :], 0), axis=1)

    joined = lax.all_to_all(
        join((queries, keys, values), groups), "mlp", split_axis=0, concat_axis=0, tiled=True
    ).reshape(group_rows, 3 * head_cols)

    wide = width * 3 // 5
    tile = wide // 3
    request_ends = jnp.cumsum(request_prompt_length[0])
    positions = jnp.arange(group_rows, dtype=jnp.int32)
    segment = jnp.sum((positions[:, None] >= request_ends[None, :]).astype(jnp.int32), axis=1)
    joined, segment, control, held_at = lax.optimization_barrier((joined, segment, control, held_at))
    attended, *part_a = attend(control, joined, segment, groups, attention_out_weight, wide, tile)
    part_b = out_projection(
        control, attended, ORDERS + groups, attention_out_weight, wide, width - wide, tile
    )
    kept_b, sent_b = reduce_step(*part_b, masks_b[0])
    kept_a, sent_a = reduce_step(*part_a, masks_a[0])

    sent_a, joined = lax.optimization_barrier((sent_a, joined))
    key_pages_out, value_pages_out = write_pages(
        joined, group_page_lookup[0], paged_key_cache, paged_value_cache
    )
    down_flat, up_flat = pick(held_at, down_bank, up_bank)

    sum_a = reduce_rest(kept_a, sent_a, masks_a[1:])
    sum_b = reduce_rest(kept_b, sent_b, masks_b[1:])
    residual, normed_a, normed_b = norm(
        block_hidden_input, (sum_a, sum_b), norm_gain_vector, norm_bias_vector, (chunk, chunk)
    )
    most_a, most_b = gather_most(normed_a, masks_a[1:]), gather_most(normed_b, masks_b[1:])
    most_a, most_b, down_flat, up_flat, key_pages_out, value_pages_out = lax.optimization_barrier(
        (most_a, most_b, down_flat, up_flat, key_pages_out, value_pages_out)
    )
    half_a, *pieces_a = stack(control, *most_a, PARTNER_A)
    half_b, *pieces_b = stack(control, *most_b, PARTNER_B)
    early_a, early_b = exchange(pieces_a[0], "mlp", masks_a[0]), exchange(pieces_b[0], "mlp", masks_b[0])
    late_a, late_b = exchange(pieces_a[1], "mlp", masks_a[0]), exchange(pieces_b[1], "mlp", masks_b[0])

    early = ((half_a, early_a), (half_b, early_b))
    late = ((half_a, late_a), (half_b, late_b))
    segment = segment.reshape(1, group_rows)
    lowrank = down_products(control, *early, groups, down_flat, segment)
    acc = feedfwd_in(control, *early, b_of_a, False, feedfwd_in_weight.T)
    for mask in bits[:minor]:
        lowrank = lowrank + exchange(lowrank, "mlp", mask)
    lowrank, acc = lax.optimization_barrier((lowrank, acc))
    lowrank = lowrank + sum(exchange(lowrank, "mlp", k << minor) for k in range(1, groups >> minor))
    acc = feedfwd_in(control, *late, b_of_a, True, feedfwd_in_weight.T, acc)

    activated, *part_a = feedfwd_out_first(
        control, acc, lowrank, segment, up_flat, feedfwd_out_weight, wide, tile, groups
    )
    part_b = out_projection(
        control,
        activated.reshape(groups, tok_rows, -1),
        a_of_b,
        feedfwd_out_weight,
        wide,
        width - wide,
        tile,
    )
    sums = (reduce_rest(*part_a, masks_a), reduce_rest(*part_b, masks_b))
    block_out = (
        residual
        + jnp.concatenate([a.astype(F32) + b.astype(F32) for a, b in sums], axis=1)
    ).astype(BF16)
    return (block_out, key_pages_out, value_pages_out)


def solution(mesh):
    in_specs = (
        P(("req", "mlp"), None),
        P(("req", "mlp"), None),
        P(("req", "mlp"), None),
        P(("req", "mlp"), None),
        P("mlp", None),
        P(None, "mlp"),
        P("mlp", None),
        P(),
        P(),
        P("req", "mlp", None),
        P("req", None, "mlp"),
        P("req", None, "mlp"),
        P("req", None, "mlp"),
        P("req", None),
        P("req", None),
        P("req", None),
        P(),
    )
    out_specs = (P(("req", "mlp"), None), P("req", None, "mlp"), P("req", None, "mlp"))
    return jax.shard_map(shards, mesh=mesh, in_specs=in_specs, out_specs=out_specs, check_vma=False)
```

time: 315 us -> 190 us (0.60)
  waiting for transfers between devices: 203 us -> 102 us
  matrix products: 46.8 us -> 0 us
  Pallas kernels: 0 us -> 45 us
  starting transfers between devices: 14.7 us -> 35.8 us
  blocking collectives: 19.5 us -> 0 us
  between operations: 15.9 us -> 1.07 us
  local copies, waits for them, and re-layouts: 7.4 us -> 2.06 us
    reduce_scatter x2 -> x0, waiting for transfers between devices: 132 us -> none  [the longest x1 66.8 us: shards(): lax.psum_scatter(jnp.dot(row_block, attention_out_weight, preferred_eleme...]
    ppermute x0 -> x30, waiting for transfers between devices: none -> 85.3 us  [exchange(): return lax.ppermute(x, axis, [(i, i ^ mask) for i in range(size)])]
    all_gather x3 -> x0, waiting for transfers between devices: 47.5 us -> none  [the longest x1 47.4 us: shards(): lax.all_gather(modulate(residual, norm_gain_vector, norm_bias_vector), 'm...]
    dot_general x8 -> x0, matrix products: 46.3 us -> none  [the longest x1 32.4 us: shards(): jnp.dot(row_block, feedfwd_out_weight, preferred_element_type=jnp.float32)]
    pallas_call x0 -> x21, Pallas kernels: none -> 45 us  [the longest x2 11.4 us: feedfwd_in(): pl.pallas_call(kernel, grid_spec=pltpu.PrefetchScalarGridSpec(num_scalar_...]
    ppermute x0 -> x30, starting transfers between devices: none -> 28.5 us  [exchange(): return lax.ppermute(x, axis, [(i, i ^ mask) for i in range(size)])]
    psum x1 -> x0, blocking collectives: 19.5 us -> none  [shards(): lowrank = lax.psum(own_rank.astype(jnp.bfloat16), 'mlp')]
    all_to_all x3 -> x1, starting transfers between devices: 14.5 us -> 7.28 us  [shards(): lax.all_to_all(join((queries, keys, values), groups), 'mlp', split_axis=0...]
  transfers between devices with their start and end apart: 8 -> 31, of which waited for: 6 -> 16; matrix products, arithmetic and copies ran while one was open for 5% -> 2% of each run, Pallas kernels for 0% -> 15%
where the time goes in v1:
time: 190 us
  waiting for transfers between devices  102 us (54%)
  Pallas kernels  45 us (24%)
  starting transfers between devices  35.8 us (19%)
  other arithmetic  3.63 us (2%)
  local copies, waits for them, and re-layouts  2.06 us (1%)
    ppermute x30, waiting for transfers between devices, exchange(): return lax.ppermute(x, axis, [(i, i ^ mask) for i in range(size)])  85.3 us
    ppermute x30, starting transfers between devices, exchange(): return lax.ppermute(x, axis, [(i, i ^ mask) for i in range(size)])  28.5 us
    all_to_all x1, waiting for transfers between devices, shards(): lax.all_to_all(join((queries, keys, values), groups), 'mlp', split_axis=0...  16.6 us
    pallas_call x2, Pallas kernels, feedfwd_in(): pl.pallas_call(kernel, grid_spec=pltpu.PrefetchScalarGridSpec(num_scalar_...  11.4 us
    pallas_call x1, Pallas kernels, feedfwd_out_first(): pl.pallas_call(kernel, grid_spec=pltpu.PrefetchScalarGridSpec(num_scalar_...  8.16 us
    pallas_call x2, Pallas kernels, out_projection(): pl.pallas_call(kernel, grid_spec=pltpu.PrefetchScalarGridSpec(num_scalar_...  7.68 us
    all_to_all x1, starting transfers between devices, shards(): lax.all_to_all(join((queries, keys, values), groups), 'mlp', split_axis=0...  7.28 us
    pallas_call x1, Pallas kernels, attend(): pl.pallas_call(kernel, grid_spec=pltpu.PrefetchScalarGridSpec(num_scalar_...  5.11 us
  transfers between devices with their start and end apart: 31, of which 16 were waited for; matrix products, arithmetic and copies ran while one was open for 2% of the time, Pallas kernels for 15%

profile of v1, /device:TPU:0, one launch (start us, length us, event | category | flops | bytes accessed | tf_op | source)
XLA Modules:
  0.0 189.5 jit_solution(12623237497824517239)
XLA Ops:
  0.6 3.2 %join.1 = bf16[8,32,1536]{2,1,0:T(8,128)(2,1)} custom-call(bf16[32,4096]{1,0:T(8,128)(2,1)} %refs_0_.2, bf16[32,4096]{1,0:T(8,128)(2,1)} %refs_1_.1, bf16[32,4096]{1,0:T(8,128)(2,1)} %refs_2_.1), custom_call_target="tpu_custom_call" | custom-call | bytes 1 | tf_op jit(solution)/shard_map/join/pallas_call | solution.py:394
  3.9 7.3 %all-to-all-start = ((bf16[8,32,1536]{2,1,0:T(8,128)(2,1)}), bf16[8,32,1536]{2,1,0:T(8,128)(2,1)S(1)}, u32[]{:S(2)}, u32[]{:S(2)}) async-start(bf16[8,32,1536]{2,1,0:T(8,128)(2,1)} %join.1), calls=%async_computation | async-start | bytes 1572864 | tf_op jit(solution)/shard_map/all_to_all | solution.py:561
  11.1 0.7 xor_multiply_fusion
  12.0 0.7 copy.25
  12.9 0.7 broadcast_xor_fusion
  13.7 0.9 select_reduce_fusion.1
  14.7 16.6 %all-to-all-done = bf16[8,32,1536]{2,1,0:T(8,128)(2,1)S(1)} async-done(((bf16[8,32,1536]{2,1,0:T(8,128)(2,1)}), bf16[8,32,1536]{2,1,0:T(8,128)(2,1)S(1)}, u32[]{:S(2)}, u32[]{:S(2)}) %all-to-all-start) | async-done | bytes 786464 | tf_op jit(solution)/shard_map/all_to_all | solution.py:561
  31.5 5.1 %attend.1 = (bf16[8,32,512]{2,1,0:T(8,128)(2,1)S(1)}, bf16[128,3072]{1,0:T(8,128)(2,1)S(1)}, bf16[128,3072]{1,0:T(8,128)(2,1)S(1)}) custom-call(s32[21]{0:T(128)S(1)} %concatenate.12.control_ref, bf16[256,1536]{1,0:T(8,128)(2,1)S(1)} %bitcast.16, s32[256,1]{1,0:T(8,128)S(1)} %copy.26.col_ref, s32[1,256]{1,0:T(1,128)S(1)} %bitcast.26, bf16[512,5120]{1,0:T(8,128)(2,1)} %w_ref.5), custom_call_target="tpu_custom_call" | custom-call | bytes 1 | tf_op jit(solution)/shard_map/attend/pallas_call | solution.py:437
  36.6 1.5 collective-permute-start
  38.1 2.8 %out_projection.2 = (bf16[128,2048]{1,0:T(8,128)(2,1)S(1)}, bf16[128,2048]{1,0:T(8,128)(2,1)S(1)}) custom-call(s32[21]{0:T(128)S(1)} %concatenate.12.control_ref, bf16[8,32,512]{2,1,0:T(8,128)(2,1)S(1)} %get-tuple-element.68.x_ref, bf16[512,5120]{1,0:T(8,128)(2,1)} %w_ref.5), custom_call_target="tpu_custom_call" | custom-call | bytes 1 | tf_op jit(solution)/shard_map/out_projection/pallas_call | solution.py:87
  41.0 1.6 collective-permute-start.13
  42.5 12.3 %collective-permute-done.got_ref = bf16[128,3072]{1,0:T(8,128)(2,1)S(1)} collective-permute-done((bf16[128,3072]{1,0:T(8,128)(2,1)S(1)}, bf16[128,3072]{1,0:T(8,128)(2,1)S(1)}, u32[]{:S(2)}, u32[]{:S(2)}) %collective-permute-start) | collective-permute-done | bytes 786464 | tf_op jit(solution)/shard_map/ppermute | solution.py:31
  55.3 1.8 collective-permute-start.4
  57.1 1.5 collective-permute-start.10
  58.6 5.3 %collective-permute-done.1.got_ref = bf16[64,3072]{1,0:T(8,128)(2,1)S(1)} collective-permute-done((bf16[64,3072]{1,0:T(8,128)(2,1)S(1)}, bf16[64,3072]{1,0:T(8,128)(2,1)S(1)}, u32[]{:S(2)}, u32[]{:S(2)}) %collective-permute-start.1) | collective-permute-done | bytes 393248 | tf_op jit(solution)/shard_map/ppermute | solution.py:31
  64.0 2.7 %collective-permute-start.2 = (bf16[32,3072]{1,0:T(8,128)(2,1)S(1)}, bf16[32,3072]{1,0:T(8,128)(2,1)S(1)}, u32[]{:S(2)}, u32[]{:S(2)}) collective-permute-start(bf16[32,3072]{1,0:T(8,128)(2,1)S(1)} %get-tuple-element.67), channel_id=1, source_target_pairs={{0,4},{1,5},{2,6},{3,7},{4,0},{5,1},{6,2},{7,3},{8,12},{9,13},{10,... | collective-permute-start | bytes 589832 | tf_op jit(solution)/shard_map/ppermute | solution.py:31
  67.1 2.0 %collective-permute-done.10.refs_1_ = bf16[16,16,640]{2,1,0:T(8,128)(2,1)S(1)} collective-permute-done((bf16[16,16,640]{2,1,0:T(8,128)(2,1)S(1)}, bf16[16,16,640]{2,1,0:T(8,128)(2,1)S(1)}, u32[]{:S(2)}, u32[]{:S(2)}) %collective-permute-start.10) | collective-permute-done | bytes 327712 | tf_op jit(solution)/shard_map/ppermute | solution.py:31
  69.6 10.5 %collective-permute-done.5.refs_6_ = bf16[32,2048]{1,0:T(8,128)(2,1)S(1)} collective-permute-done((bf16[32,2048]{1,0:T(8,128)(2,1)S(1)}, bf16[32,2048]{1,0:T(8,128)(2,1)S(1)}, u32[]{:S(2)}, u32[]{:S(2)}) %collective-permute-start.5) | collective-permute-done | bytes 131104 | tf_op jit(solution)/shard_map/ppermute | solution.py:31
  80.7 11.0 %collective-permute-done.8 = bf16[32,2560]{1,0:T(8,128)(2,1)S(1)} collective-permute-done((bf16[32,2560]{1,0:T(8,128)(2,1)S(1)}, bf16[32,2560]{1,0:T(8,128)(2,1)S(1)}, u32[]{:S(2)}, u32[]{:S(2)}) %collective-permute-start.8) | collective-permute-done | bytes 163872 | tf_op jit(solution)/shard_map/ppermute | solution.py:31
  91.7 9.1 %collective-permute-done.6 = bf16[32,2560]{1,0:T(8,128)(2,1)S(1)} collective-permute-done((bf16[32,2560]{1,0:T(8,128)(2,1)S(1)}, bf16[32,2560]{1,0:T(8,128)(2,1)S(1)}, u32[]{:S(2)}, u32[]{:S(2)}) %collective-permute-start.6) | collective-permute-done | bytes 163872 | tf_op jit(solution)/shard_map/ppermute | solution.py:31
  100.8 1.7 collective-permute-start.9
  102.8 0.9 copy-done.7
  103.7 3.7 %pick.1 = (bf16[256,640]{1,0:T(8,128)(2,1)S(1)}, bf16[256,1728]{1,0:T(8,128)(2,1)S(1)}) custom-call(s32[16]{0:T(128)S(1)} %select_reduce_fusion.at_ref, bf16[16,16,640]{2,1,0:T(8,128)(2,1)S(1)} %bitcast.22, bf16[16,16,640]{2,1,0:T(8,128)(2,1)S(1)} %collective-permute-done.10.refs_1_, bf16[16,16,640]{2,1,0:T(8,128)(2,1)S(1)} %collective-permute-done.11.refs_2_, ...), custom_call_target="tpu_custom_call" | custom-call | bytes 8388608 | tf_op jit(solution)/shard_map/pick/pallas_call | solution.py:365
  107.5 2.1 %write_pages.1 = (bf16[3,128,512]{2,1,0:T(8,128)(2,1)}, bf16[3,128,512]{2,1,0:T(8,128)(2,1)}) custom-call(s32[3]{0:T(128)S(1)} %broadcast_add_fusion.source_ref, bf16[256,1536]{1,0:T(8,128)(2,1)S(1)} %bitcast.17, bf16[256,1536]{1,0:T(8,128)(2,1)S(1)} %bitcast.18, bf16[3,128,512]{2,1,0:T(8,128)(2,1)S(1)} %copy-done.1, bf16[3,128,512]{2,1,0:T(8,128)(2,1)S(1)} %copy-done.2), custom_call_target="tpu_custom_call" | custom-call | bytes 8388608 | tf_op jit(solution)/shard_map/write_pages/pallas_call | solution.py:482
  109.6 0.9 collective-permute-done.9.got_ref
  110.5 1.5 collective-permute-done.7.got_ref
  112.0 0.6 stack.22
  113.0 0.6 stack.23
  114.0 1.7 collective-permute-start.16
  115.7 1.7 collective-permute-start.17
  117.5 5.9 %collective-permute-done.18.a1 = bf16[128,1280]{1,0:T(8,128)(2,1)S(1)} collective-permute-done((bf16[128,1280]{1,0:T(8,128)(2,1)S(1)}, bf16[128,1280]{1,0:T(8,128)(2,1)S(1)}, u32[]{:S(2)}, u32[]{:S(2)}) %collective-permute-start.18) | collective-permute-done | bytes 327712 | tf_op jit(solution)/shard_map/ppermute | solution.py:31
  123.3 1.0 collective-permute-done.19.b1
  124.3 1.1 down_products.1
  125.5 1.8 collective-permute-start.20
  127.3 5.7 %feedfwd_in.2.refs_0_ = f32[256,1728]{1,0:T(8,128)S(1)} custom-call(s32[21]{0:T(128)S(1)} %concatenate.12.control_ref, bf16[128,2560]{1,0:T(8,128)(2,1)S(1)} %get-tuple-element.86.a0, bf16[128,1280]{1,0:T(8,128)(2,1)S(1)} %collective-permute-done.18.a1, bf16[128,2560]{1,0:T(8,128)(2,1)S(1)} %get-tuple-element.90.b0, ...), custom_call_target="tpu_custom_call" | custom-call | flops 2264924160 | bytes 8847360 | tf_op jit(solution)/shard_map/feedfwd_in/pallas_call | solution.py:169
  133.0 2.3 %collective-permute-start.23 = (f32[16,256]{1,0:T(8,128)S(1)}, f32[16,256]{1,0:T(8,128)S(1)}, u32[]{:S(2)}, u32[]{:S(2)}) collective-permute-start(f32[16,256]{1,0:T(8,128)S(1)} %add.59), channel_id=1, source_target_pairs={{0,6},{1,7},{2,4},{3,5},{4,2},{5,3},{6,0},{7,1},{8,14},{9,15},{10,... | collective-permute-start | bytes 49160 | tf_op jit(solution)/shard_map/ppermute | solution.py:31
  135.3 2.1 %collective-permute-start.21 = (f32[16,256]{1,0:T(8,128)S(1)}, f32[16,256]{1,0:T(8,128)S(1)}, u32[]{:S(2)}, u32[]{:S(2)}) collective-permute-start(f32[16,256]{1,0:T(8,128)S(1)} %add.59), channel_id=1, source_target_pairs={{0,2},{1,3},{2,0},{3,1},{4,6},{5,7},{6,4},{7,5},{8,10},{9,11},{10,... | collective-permute-start | bytes 49160 | tf_op jit(solution)/shard_map/ppermute | solution.py:31
  137.5 5.7 %feedfwd_in.3.acc_ref = f32[256,1728]{1,0:T(8,128)S(1)} custom-call(s32[21]{0:T(128)S(1)} %concatenate.12.control_ref, bf16[128,2560]{1,0:T(8,128)(2,1)S(1)} %get-tuple-element.86.a0, bf16[128,1280]{1,0:T(8,128)(2,1)S(1)} %collective-permute-done.16.a1, bf16[128,2560]{1,0:T(8,128)(2,1)S(1)} %get-tuple-element.90.b0, ...), custom_call_target="tpu_custom_call" | custom-call | flops 2264924160 | bytes 8847360 | tf_op jit(solution)/shard_map/feedfwd_in/pallas_call | solution.py:169
  143.2 8.2 %feedfwd_out_first.1 = (bf16[256,1728]{1,0:T(8,128)(2,1)S(1)}, bf16[128,3072]{1,0:T(8,128)(2,1)S(1)}, bf16[128,3072]{1,0:T(8,128)(2,1)S(1)}) custom-call(s32[21]{0:T(128)S(1)} %concatenate.12.control_ref, f32[256,1728]{1,0:T(8,128)S(1)} %feedfwd_in.3.acc_ref, f32[16,256]{1,0:T(8,128)S(1)} %add_add_fusion.low_ref, s32[1,256]{1,0:T(1,128)S(1)} %bitcast.28, ...), custom_call_target="tpu_custom_call" | custom-call | bytes 1 | tf_op jit(solution)/shard_map/feedfwd_out_first/pallas_call | solution.py:309
  151.7 4.9 %out_projection.3 = (bf16[128,2048]{1,0:T(8,128)(2,1)S(1)}, bf16[128,2048]{1,0:T(8,128)(2,1)S(1)}) custom-call(s32[21]{0:T(128)S(1)} %concatenate.12.control_ref, bf16[8,32,1728]{2,1,0:T(8,128)(2,1)S(1)} %bitcast.19, bf16[1728,5120]{1,0:T(8,128)(2,1)} %w_ref.7), custom_call_target="tpu_custom_call" | custom-call | bytes 1 | tf_op jit(solution)/shard_map/out_projection/pallas_call | solution.py:87
  156.8 12.7 %collective-permute-done.27.got_ref = bf16[128,2048]{1,0:T(8,128)(2,1)S(1)} collective-permute-done((bf16[128,2048]{1,0:T(8,128)(2,1)S(1)}, bf16[128,2048]{1,0:T(8,128)(2,1)S(1)}, u32[]{:S(2)}, u32[]{:S(2)}) %collective-permute-start.27) | collective-permute-done | bytes 524320 | tf_op jit(solution)/shard_map/ppermute | solution.py:31
  169.9 2.2 %collective-permute-start.28 = (bf16[64,2048]{1,0:T(8,128)(2,1)S(1)}, bf16[64,2048]{1,0:T(8,128)(2,1)S(1)}, u32[]{:S(2)}, u32[]{:S(2)}) collective-permute-start(bf16[64,2048]{1,0:T(8,128)(2,1)S(1)} %get-tuple-element.108), channel_id=1, source_target_pairs={{0,1},{1,0},{2,3},{3,2},{4,5},{5,4},{6,7},{7,6},{8,9},{9,8},{10,11... | collective-permute-start | bytes 786440 | tf_op jit(solution)/shard_map/ppermute | solution.py:31
  172.1 4.4 %collective-permute-done.28.got_ref = bf16[64,2048]{1,0:T(8,128)(2,1)S(1)} collective-permute-done((bf16[64,2048]{1,0:T(8,128)(2,1)S(1)}, bf16[64,2048]{1,0:T(8,128)(2,1)S(1)}, u32[]{:S(2)}, u32[]{:S(2)}) %collective-permute-start.28) | collective-permute-done | bytes 262176 | tf_op jit(solution)/shard_map/ppermute | solution.py:31
  176.5 2.8 %collective-permute-start.29 = (bf16[32,2048]{1,0:T(8,128)(2,1)S(1)}, bf16[32,2048]{1,0:T(8,128)(2,1)S(1)}, u32[]{:S(2)}, u32[]{:S(2)}) collective-permute-start(bf16[32,2048]{1,0:T(8,128)(2,1)S(1)} %get-tuple-element.110), channel_id=1, source_target_pairs={{0,4},{1,5},{2,6},{3,7},{4,0},{5,1},{6,2},{7,3},{8,12},{9,13},{10,... | collective-permute-start | bytes 393224 | tf_op jit(solution)/shard_map/ppermute | solution.py:31
  179.4 1.0 collective-permute-done.25.got_ref
  181.0 1.4 collective-permute-done.29
  182.5 6.2 %collective-permute-done.26 = bf16[32,3072]{1,0:T(8,128)(2,1)S(1)} collective-permute-done((bf16[32,3072]{1,0:T(8,128)(2,1)S(1)}, bf16[32,3072]{1,0:T(8,128)(2,1)S(1)}, u32[]{:S(2)}, u32[]{:S(2)}) %collective-permute-start.26) | collective-permute-done | bytes 196640 | tf_op jit(solution)/shard_map/ppermute | solution.py:31
  188.7 0.8 fusion
  (77 shorter events, 5.4 us)
Async XLA Ops:
  3.9 27.5 %all-to-all-start = ((bf16[8,32,1536]{2,1,0:T(8,128)(2,1)}), bf16[8,32,1536]{2,1,0:T(8,128)(2,1)S(1)}, u32[]{:S(2)}, u32[]{:S(2)}) async-start(bf16[8,32,1536]{2,1,0:T(8,128)(2,1)} %join.1), calls=%async_computation | async-start | bytes 1572864 | tf_op jit(solution)/shard_map/all_to_all | solution.py:561
  31.5 9.5 %copy-start = (bf16[16,16,1728]{2,1,0:T(8,128)(2,1)S(1)}, bf16[16,16,1728]{2,1,0:T(8,128)(2,1)}, u32[]{:S(2)}) copy-start(bf16[16,16,1728]{2,1,0:T(8,128)(2,1)} %refs_4_.1) | copy-start | bytes 2654212
  36.6 20.5 %copy-start.3 = (bf16[16,640,16]{1,2,0:T(8,128)(2,1)S(1)}, bf16[16,640,16]{1,2,0:T(8,128)(2,1)}, u32[]{:S(2)}) copy-start(bf16[16,640,16]{1,2,0:T(8,128)(2,1)} %param.28) | copy-start | bytes 983044
  36.6 43.5 %copy-start.4 = (bf16[32,5120]{1,0:T(8,128)(2,1)S(1)}, bf16[32,5120]{1,0:T(8,128)(2,1)}, u32[]{:S(2)}) copy-start(bf16[32,5120]{1,0:T(8,128)(2,1)} %refs_0_.3) | copy-start | bytes 983044
  36.6 43.5 %copy-start.5 = (f32[5120]{0:T(1024)S(1)}, f32[5120]{0:T(1024)}, u32[]{:S(2)}) copy-start(f32[5120]{0:T(1024)} %param.26) | copy-start | bytes 61444
  36.6 43.5 %copy-start.6 = (f32[5120]{0:T(1024)S(1)}, f32[5120]{0:T(1024)}, u32[]{:S(2)}) copy-start(f32[5120]{0:T(1024)} %param.27) | copy-start | bytes 61444
  36.6 18.2 %collective-permute-start = (bf16[128,3072]{1,0:T(8,128)(2,1)S(1)}, bf16[128,3072]{1,0:T(8,128)(2,1)S(1)}, u32[]{:S(2)}, u32[]{:S(2)}) collective-permute-start(bf16[128,3072]{1,0:T(8,128)(2,1)S(1)} %get-tuple-element.62), channel_id=1, source_target_pairs={{0,1},{1,0},{2,3},{3,2},{4,5},{5,4},{6,7},{7,6},{8,9},{9,8},{10,11... | collective-permute-start | bytes 2359304 | tf_op jit(solution)/shard_map/ppermute | solution.py:31
  38.1 64.6 %copy-start.8 = (s32[1,2]{1,0:T(1,128)S(1)}, s32[1,2]{1,0:T(1,128)}, u32[]{:S(2)}) copy-start(s32[1,2]{1,0:T(1,128)} %param.33) | copy-start | bytes 28
  40.9 14.2 %collective-permute-start.3 = (bf16[128,2048]{1,0:T(8,128)(2,1)S(1)}, bf16[128,2048]{1,0:T(8,128)(2,1)S(1)}, u32[]{:S(2)}, u32[]{:S(2)}) collective-permute-start(bf16[128,2048]{1,0:T(8,128)(2,1)S(1)} %get-tuple-element.70), channel_id=1, source_target_pairs={{0,2},{1,3},{2,0},{3,1},{4,6},{5,7},{6,4},{7,5},{8,10},{9,11},{10,... | collective-permute-start | bytes 1572872 | tf_op jit(solution)/shard_map/ppermute | solution.py:31
  41.0 28.1 %collective-permute-start.13 = (bf16[16,16,1728]{2,1,0:T(8,128)(2,1)S(1)}, bf16[16,16,1728]{2,1,0:T(8,128)(2,1)S(1)}, u32[]{:S(2)}, u32[]{:S(2)}) collective-permute-start(bf16[16,16,1728]{2,1,0:T(8,128)(2,1)S(1)} %copy-done), channel_id=1, source_target_pairs={{0,16},{8,24},{16,0},{24,8},{1,17},{9,25},{17,1},{25,9},{2,18},{10... | collective-permute-start | bytes 2654216 | tf_op jit(solution)/shard_map/ppermute | solution.py:31
  55.0 8.9 %collective-permute-start.1 = (bf16[64,3072]{1,0:T(8,128)(2,1)S(1)}, bf16[64,3072]{1,0:T(8,128)(2,1)S(1)}, u32[]{:S(2)}, u32[]{:S(2)}) collective-permute-start(bf16[64,3072]{1,0:T(8,128)(2,1)S(1)} %get-tuple-element.65), channel_id=1, source_target_pairs={{0,2},{1,3},{2,0},{3,1},{4,6},{5,7},{6,4},{7,5},{8,10},{9,11},{10,... | collective-permute-start | bytes 1179656 | tf_op jit(solution)/shard_map/ppermute | solution.py:31
  55.1 52.3 %copy-start.1 = (bf16[3,128,512]{2,1,0:T(8,128)(2,1)S(1)}, bf16[3,128,512]{2,1,0:T(8,128)(2,1)}, u32[]{:S(2)}) copy-start(bf16[3,128,512]{2,1,0:T(8,128)(2,1)} %key_cache_ref.1) | copy-start | bytes 1179652
  55.1 52.3 %copy-start.2 = (bf16[3,128,512]{2,1,0:T(8,128)(2,1)S(1)}, bf16[3,128,512]{2,1,0:T(8,128)(2,1)}, u32[]{:S(2)}) copy-start(bf16[3,128,512]{2,1,0:T(8,128)(2,1)} %value_cache_ref.1) | copy-start | bytes 1179652
  55.3 11.4 %collective-permute-start.4 = (bf16[64,2048]{1,0:T(8,128)(2,1)S(1)}, bf16[64,2048]{1,0:T(8,128)(2,1)S(1)}, u32[]{:S(2)}, u32[]{:S(2)}) collective-permute-start(bf16[64,2048]{1,0:T(8,128)(2,1)S(1)} %get-tuple-element.72), channel_id=1, source_target_pairs={{0,1},{1,0},{2,3},{3,2},{4,5},{5,4},{6,7},{7,6},{8,9},{9,8},{10,11... | collective-permute-start | bytes 786440 | tf_op jit(solution)/shard_map/ppermute | solution.py:31
  57.1 12.0 %collective-permute-start.10 = (bf16[16,16,640]{2,1,0:T(8,128)(2,1)S(1)}, bf16[16,16,640]{2,1,0:T(8,128)(2,1)S(1)}, u32[]{:S(2)}, u32[]{:S(2)}) collective-permute-start(bf16[16,16,640]{2,1,0:T(8,128)(2,1)S(1)} %bitcast.20), channel_id=1, source_target_pairs={{0,16},{8,24},{16,0},{24,8},{1,17},{9,25},{17,1},{25,9},{2,18},{10... | collective-permute-start | bytes 983048 | tf_op jit(solution)/shard_map/ppermute | solution.py:31
  64.0 16.1 %collective-permute-start.2 = (bf16[32,3072]{1,0:T(8,128)(2,1)S(1)}, bf16[32,3072]{1,0:T(8,128)(2,1)S(1)}, u32[]{:S(2)}, u32[]{:S(2)}) collective-permute-start(bf16[32,3072]{1,0:T(8,128)(2,1)S(1)} %get-tuple-element.67), channel_id=1, source_target_pairs={{0,4},{1,5},{2,6},{3,7},{4,0},{5,1},{6,2},{7,3},{8,12},{9,13},{10,... | collective-permute-start | bytes 589832 | tf_op jit(solution)/shard_map/ppermute | solution.py:31
  66.7 13.4 %collective-permute-start.5 = (bf16[32,2048]{1,0:T(8,128)(2,1)S(1)}, bf16[32,2048]{1,0:T(8,128)(2,1)S(1)}, u32[]{:S(2)}, u32[]{:S(2)}) collective-permute-start(bf16[32,2048]{1,0:T(8,128)(2,1)S(1)} %get-tuple-element.74), channel_id=1, source_target_pairs={{0,4},{1,5},{2,6},{3,7},{4,0},{5,1},{6,2},{7,3},{8,12},{9,13},{10,... | collective-permute-start | bytes 393224 | tf_op jit(solution)/shard_map/ppermute | solution.py:31
  67.1 35.5 %collective-permute-start.11 = (bf16[16,16,640]{2,1,0:T(8,128)(2,1)S(1)}, bf16[16,16,640]{2,1,0:T(8,128)(2,1)S(1)}, u32[]{:S(2)}, u32[]{:S(2)}) collective-permute-start(bf16[16,16,640]{2,1,0:T(8,128)(2,1)S(1)} %bitcast.21), channel_id=1, source_target_pairs={{0,8},{8,0},{16,24},{24,16},{1,9},{9,1},{17,25},{25,17},{2,10},{10... | collective-permute-start | bytes 983048 | tf_op jit(solution)/shard_map/ppermute | solution.py:31
  69.1 33.7 %collective-permute-start.14 = (bf16[16,16,1728]{2,1,0:T(8,128)(2,1)S(1)}, bf16[16,16,1728]{2,1,0:T(8,128)(2,1)S(1)}, u32[]{:S(2)}, u32[]{:S(2)}) collective-permute-start(bf16[16,16,1728]{2,1,0:T(8,128)(2,1)S(1)} %copy-done), channel_id=1, source_target_pairs={{0,8},{8,0},{16,24},{24,16},{1,9},{9,1},{17,25},{25,17},{2,10},{10... | collective-permute-start | bytes 2654216 | tf_op jit(solution)/shard_map/ppermute | solution.py:31
  69.1 33.7 %collective-permute-start.12 = (bf16[16,16,640]{2,1,0:T(8,128)(2,1)S(1)}, bf16[16,16,640]{2,1,0:T(8,128)(2,1)S(1)}, u32[]{:S(2)}, u32[]{:S(2)}) collective-permute-start(bf16[16,16,640]{2,1,0:T(8,128)(2,1)S(1)} %collective-permute-done.10.refs_1_), channel_id=1, source_target_pairs={{0,8},{8,0},{16,24},{24,16},{1,9},{9,1},{17,25},{25,17},{2,10},{10... | collective-permute-start | bytes 983048 | tf_op jit(solution)/shard_map/ppermute | solution.py:31
  80.1 22.7 %collective-permute-start.15 = (bf16[16,16,1728]{2,1,0:T(8,128)(2,1)S(1)}, bf16[16,16,1728]{2,1,0:T(8,128)(2,1)S(1)}, u32[]{:S(2)}, u32[]{:S(2)}) collective-permute-start(bf16[16,16,1728]{2,1,0:T(8,128)(2,1)S(1)} %collective-permute-done.13.refs_5_), channel_id=1, source_target_pairs={{0,8},{8,0},{16,24},{24,16},{1,9},{9,1},{17,25},{25,17},{2,10},{10... | collective-permute-start | bytes 2654216 | tf_op jit(solution)/shard_map/ppermute | solution.py:31
  80.6 11.1 %collective-permute-start.8 = (bf16[32,2560]{1,0:T(8,128)(2,1)S(1)}, bf16[32,2560]{1,0:T(8,128)(2,1)S(1)}, u32[]{:S(2)}, u32[]{:S(2)}) collective-permute-start(bf16[32,2560]{1,0:T(8,128)(2,1)S(1)} %get-tuple-element.77), channel_id=1, source_target_pairs={{0,4},{1,5},{2,6},{3,7},{4,0},{5,1},{6,2},{7,3},{8,12},{9,13},{10,... | collective-permute-start | bytes 491528 | tf_op jit(solution)/shard_map/ppermute | solution.py:31
  91.7 9.1 %collective-permute-start.6 = (bf16[32,2560]{1,0:T(8,128)(2,1)S(1)}, bf16[32,2560]{1,0:T(8,128)(2,1)S(1)}, u32[]{:S(2)}, u32[]{:S(2)}) collective-permute-start(bf16[32,2560]{1,0:T(8,128)(2,1)S(1)} %get-tuple-element.76), channel_id=1, source_target_pairs={{0,4},{1,5},{2,6},{3,7},{4,0},{5,1},{6,2},{7,3},{8,12},{9,13},{10,... | collective-permute-start | bytes 491528 | tf_op jit(solution)/shard_map/ppermute | solution.py:31
  100.8 9.6 %collective-permute-start.9 = (bf16[64,2560]{1,0:T(8,128)(2,1)S(1)}, bf16[64,2560]{1,0:T(8,128)(2,1)S(1)}, u32[]{:S(2)}, u32[]{:S(2)}) collective-permute-start(bf16[64,2560]{1,0:T(8,128)(2,1)S(1)} %constant_dynamic-update-slice_fusion.2.rows_ref), channel_id=1, source_target_pairs={{0,1},{1,0},{2,3},{3,2},{4,5},{5,4},{6,7},{7,6},{8,9},{9,8},{10,11... | collective-permute-start | bytes 983048 | tf_op jit(solution)/shard_map/ppermute | solution.py:31
  102.6 9.4 %collective-permute-start.7 = (bf16[64,2560]{1,0:T(8,128)(2,1)S(1)}, bf16[64,2560]{1,0:T(8,128)(2,1)S(1)}, u32[]{:S(2)}, u32[]{:S(2)}) collective-permute-start(bf16[64,2560]{1,0:T(8,128)(2,1)S(1)} %constant_dynamic-update-slice_fusion.rows_ref), channel_id=1, source_target_pairs={{0,2},{1,3},{2,0},{3,1},{4,6},{5,7},{6,4},{7,5},{8,10},{9,11},{10,... | collective-permute-start | bytes 983048 | tf_op jit(solution)/shard_map/ppermute | solution.py:31
  102.8 0.9 copy-start.7
  112.6 10.7 %collective-permute-start.18 = (bf16[128,1280]{1,0:T(8,128)(2,1)S(1)}, bf16[128,1280]{1,0:T(8,128)(2,1)S(1)}, u32[]{:S(2)}, u32[]{:S(2)}) collective-permute-start(bf16[128,1280]{1,0:T(8,128)(2,1)S(1)} %get-tuple-element.92), channel_id=1, source_target_pairs={{0,1},{1,0},{2,3},{3,2},{4,5},{5,4},{6,7},{7,6},{8,9},{9,8},{10,11... | collective-permute-start | bytes 983048 | tf_op jit(solution)/shard_map/ppermute | solution.py:31
  113.6 10.7 %collective-permute-start.19 = (bf16[128,1280]{1,0:T(8,128)(2,1)S(1)}, bf16[128,1280]{1,0:T(8,128)(2,1)S(1)}, u32[]{:S(2)}, u32[]{:S(2)}) collective-permute-start(bf16[128,1280]{1,0:T(8,128)(2,1)S(1)} %get-tuple-element.93), channel_id=1, source_target_pairs={{0,2},{1,3},{2,0},{3,1},{4,6},{5,7},{6,4},{7,5},{8,10},{9,11},{10,... | collective-permute-start | bytes 983048 | tf_op jit(solution)/shard_map/ppermute | solution.py:31
  114.0 23.5 %collective-permute-start.16 = (bf16[128,1280]{1,0:T(8,128)(2,1)S(1)}, bf16[128,1280]{1,0:T(8,128)(2,1)S(1)}, u32[]{:S(2)}, u32[]{:S(2)}) collective-permute-start(bf16[128,1280]{1,0:T(8,128)(2,1)S(1)} %get-tuple-element.87), channel_id=1, source_target_pairs={{0,1},{1,0},{2,3},{3,2},{4,5},{5,4},{6,7},{7,6},{8,9},{9,8},{10,11... | collective-permute-start | bytes 983048 | tf_op jit(solution)/shard_map/ppermute | solution.py:31
  115.7 21.8 %collective-permute-start.17 = (bf16[128,1280]{1,0:T(8,128)(2,1)S(1)}, bf16[128,1280]{1,0:T(8,128)(2,1)S(1)}, u32[]{:S(2)}, u32[]{:S(2)}) collective-permute-start(bf16[128,1280]{1,0:T(8,128)(2,1)S(1)} %get-tuple-element.91), channel_id=1, source_target_pairs={{0,2},{1,3},{2,0},{3,1},{4,6},{5,7},{6,4},{7,5},{8,10},{9,11},{10,... | collective-permute-start | bytes 983048 | tf_op jit(solution)/shard_map/ppermute | solution.py:31
  125.5 7.5 %collective-permute-start.20 = (f32[16,256]{1,0:T(8,128)S(1)}, f32[16,256]{1,0:T(8,128)S(1)}, u32[]{:S(2)}, u32[]{:S(2)}) collective-permute-start(f32[16,256]{1,0:T(8,128)S(1)} %down_products.1), channel_id=1, source_target_pairs={{0,1},{1,0},{2,3},{3,2},{4,5},{5,4},{6,7},{7,6},{8,9},{9,8},{10,11... | collective-permute-start | bytes 49160 | tf_op jit(solution)/shard_map/ppermute | solution.py:31
  133.0 10.1 %collective-permute-start.23 = (f32[16,256]{1,0:T(8,128)S(1)}, f32[16,256]{1,0:T(8,128)S(1)}, u32[]{:S(2)}, u32[]{:S(2)}) collective-permute-start(f32[16,256]{1,0:T(8,128)S(1)} %add.59), channel_id=1, source_target_pairs={{0,6},{1,7},{2,4},{3,5},{4,2},{5,3},{6,0},{7,1},{8,14},{9,15},{10,... | collective-permute-start | bytes 49160 | tf_op jit(solution)/shard_map/ppermute | solution.py:31
  135.3 7.8 %collective-permute-start.22 = (f32[16,256]{1,0:T(8,128)S(1)}, f32[16,256]{1,0:T(8,128)S(1)}, u32[]{:S(2)}, u32[]{:S(2)}) collective-permute-start(f32[16,256]{1,0:T(8,128)S(1)} %add.59), channel_id=1, source_target_pairs={{0,4},{1,5},{2,6},{3,7},{4,0},{5,1},{6,2},{7,3},{8,12},{9,13},{10,... | collective-permute-start | bytes 49160 | tf_op jit(solution)/shard_map/ppermute | solution.py:31
  135.3 7.8 %collective-permute-start.21 = (f32[16,256]{1,0:T(8,128)S(1)}, f32[16,256]{1,0:T(8,128)S(1)}, u32[]{:S(2)}, u32[]{:S(2)}) collective-permute-start(f32[16,256]{1,0:T(8,128)S(1)} %add.59), channel_id=1, source_target_pairs={{0,2},{1,3},{2,0},{3,1},{4,6},{5,7},{6,4},{7,5},{8,10},{9,11},{10,... | collective-permute-start | bytes 49160 | tf_op jit(solution)/shard_map/ppermute | solution.py:31
  151.4 18.3 %collective-permute-start.24 = (bf16[128,3072]{1,0:T(8,128)(2,1)S(1)}, bf16[128,3072]{1,0:T(8,128)(2,1)S(1)}, u32[]{:S(2)}, u32[]{:S(2)}) collective-permute-start(bf16[128,3072]{1,0:T(8,128)(2,1)S(1)} %get-tuple-element.99), channel_id=1, source_target_pairs={{0,1},{1,0},{2,3},{3,2},{4,5},{5,4},{6,7},{7,6},{8,9},{9,8},{10,11... | collective-permute-start | bytes 2359304 | tf_op jit(solution)/shard_map/ppermute | solution.py:31
  156.7 12.8 %collective-permute-start.27 = (bf16[128,2048]{1,0:T(8,128)(2,1)S(1)}, bf16[128,2048]{1,0:T(8,128)(2,1)S(1)}, u32[]{:S(2)}, u32[]{:S(2)}) collective-permute-start(bf16[128,2048]{1,0:T(8,128)(2,1)S(1)} %get-tuple-element.106), channel_id=1, source_target_pairs={{0,2},{1,3},{2,0},{3,1},{4,6},{5,7},{6,4},{7,5},{8,10},{9,11},{10,... | collective-permute-start | bytes 1572872 | tf_op jit(solution)/shard_map/ppermute | solution.py:31
  169.8 10.6 %collective-permute-start.25 = (bf16[64,3072]{1,0:T(8,128)(2,1)S(1)}, bf16[64,3072]{1,0:T(8,128)(2,1)S(1)}, u32[]{:S(2)}, u32[]{:S(2)}) collective-permute-start(bf16[64,3072]{1,0:T(8,128)(2,1)S(1)} %get-tuple-element.101), channel_id=1, source_target_pairs={{0,2},{1,3},{2,0},{3,1},{4,6},{5,7},{6,4},{7,5},{8,10},{9,11},{10,... | collective-permute-start | bytes 1179656 | tf_op jit(solution)/shard_map/ppermute | solution.py:31
  169.9 6.6 %collective-permute-start.28 = (bf16[64,2048]{1,0:T(8,128)(2,1)S(1)}, bf16[64,2048]{1,0:T(8,128)(2,1)S(1)}, u32[]{:S(2)}, u32[]{:S(2)}) collective-permute-start(bf16[64,2048]{1,0:T(8,128)(2,1)S(1)} %get-tuple-element.108), channel_id=1, source_target_pairs={{0,1},{1,0},{2,3},{3,2},{4,5},{5,4},{6,7},{7,6},{8,9},{9,8},{10,11... | collective-permute-start | bytes 786440 | tf_op jit(solution)/shard_map/ppermute | solution.py:31
  176.5 5.9 %collective-permute-start.29 = (bf16[32,2048]{1,0:T(8,128)(2,1)S(1)}, bf16[32,2048]{1,0:T(8,128)(2,1)S(1)}, u32[]{:S(2)}, u32[]{:S(2)}) collective-permute-start(bf16[32,2048]{1,0:T(8,128)(2,1)S(1)} %get-tuple-element.110), channel_id=1, source_target_pairs={{0,4},{1,5},{2,6},{3,7},{4,0},{5,1},{6,2},{7,3},{8,12},{9,13},{10,... | collective-permute-start | bytes 393224 | tf_op jit(solution)/shard_map/ppermute | solution.py:31
  180.5 8.2 %collective-permute-start.26 = (bf16[32,3072]{1,0:T(8,128)(2,1)S(1)}, bf16[32,3072]{1,0:T(8,128)(2,1)S(1)}, u32[]{:S(2)}, u32[]{:S(2)}) collective-permute-start(bf16[32,3072]{1,0:T(8,128)(2,1)S(1)} %get-tuple-element.103), channel_id=1, source_target_pairs={{0,4},{1,5},{2,6},{3,7},{4,0},{5,1},{6,2},{7,3},{8,12},{9,13},{10,... | collective-permute-start | bytes 589832 | tf_op jit(solution)/shard_map/ppermute | solution.py:31

commit v2 on v1

v2 whole, which is shorter than its diff:
```python
import functools

import jax
import jax.numpy as jnp
from jax import lax
from jax.experimental import pallas as pl
from jax.experimental.pallas import tpu as pltpu
from jax.sharding import PartitionSpec as P

HS = 128
ADAPTER_RANK = 16
REQS = 16
PAGE = 128
EPS = 1e-06
MIB = 1024 * 1024
SPAN, ORDER = range(2)
BF16 = jnp.bfloat16
F32 = jnp.float32


def params(mib=22):
    return pltpu.CompilerParams(vmem_limit_bytes=mib * MIB)


SMALL = pl.CostEstimate(flops=0, bytes_accessed=1, transcendentals=0)
SIDE = pl.CostEstimate(flops=0, bytes_accessed=8 * MIB, transcendentals=0)


def exchange(x, axis, mask):
    size = lax.axis_size(axis)
    return lax.ppermute(x, axis, [(i, i ^ mask) for i in range(size)])


def swap(x, masks):
    reqs, size = lax.axis_size("req"), lax.axis_size("mlp")
    pairs = [
        (r * size + i, r * size + (i ^ masks[r % 2])) for r in range(reqs) for i in range(size)
    ]
    return lax.ppermute(x, ("req", "mlp"), pairs)


def block_offsets(masks):
    offsets = [0]
    for mask in reversed(masks):
        offsets = offsets + [o ^ mask for o in offsets]
    return offsets


def reduce_step(kept, sent, masks):
    rows, width = kept.shape
    half = rows // 2

    def kernel(kept_ref, got_ref, out_ref, next_ref):
        out_ref[...] = kept_ref[:half].astype(F32) + got_ref[:half].astype(F32)
        next_ref[...] = (kept_ref[half:].astype(F32) + got_ref[half:].astype(F32)).astype(BF16)

    return pl.pallas_call(
        kernel,
        out_shape=[jax.ShapeDtypeStruct((half, width), t) for t in (F32, BF16)],
        cost_estimate=SMALL,
        compiler_params=params(16),
        name="reduce_step",
    )(kept, swap(sent, masks))


def reduce_rows(kept, sent, steps):
    for masks in steps[:-1]:
        kept, sent = reduce_step(kept, sent, masks)
    return kept, swap(sent, steps[-1])


def grow(rows, masks, *first):
    return jnp.concatenate([rows, after(swap(rows, masks), *first)], axis=0)


def tied(*values):
    return lax.optimization_barrier(values)


def after(value, *first):
    return tied(value, *first)[0]


def out_projection(control, blocks, part, weight):
    count, rows, depth = blocks.shape
    rows = rows // 2
    total = count * rows
    width = weight.shape[1]
    tile = width // 4

    def kernel(control_ref, x_ref, w_ref, kept_ref, sent_ref, x_scratch):
        @pl.when(pl.program_id(0) == 0)
        def _():
            for i in range(count):
                x = x_ref[control_ref[ORDER + i], part * rows : (part + 1) * rows, :]
                x_scratch[i * rows : (i + 1) * rows, :] = x

        y = jnp.dot(x_scratch[...], w_ref[...], preferred_element_type=F32).astype(BF16)
        kept_ref[...] = y[: total // 2]
        sent_ref[...] = y[total // 2 :]

    half = jax.ShapeDtypeStruct((total // 2, width), BF16)
    return pl.pallas_call(
        kernel,
        grid_spec=pltpu.PrefetchScalarGridSpec(
            num_scalar_prefetch=1,
            grid=(width // tile,),
            in_specs=[
                pl.BlockSpec(blocks.shape, lambda j, c: (0, 0, 0)),
                pl.BlockSpec((depth, tile), lambda j, c: (0, j)),
            ],
            out_specs=[pl.BlockSpec((total // 2, tile), lambda j, c: (0, j))] * 2,
            scratch_shapes=[pltpu.VMEM((total, depth), BF16)],
        ),
        out_shape=[half, half],
        cost_estimate=SMALL,
        compiler_params=params(48),
        name="out_projection",
    )(control, blocks, weight)


def feedfwd_out(activated, weight, start, width, tile):
    total, depth = activated.shape
    first = start // tile

    def kernel(x_ref, w_ref, kept_ref, sent_ref):
        y = jnp.dot(x_ref[...], w_ref[...], preferred_element_type=F32).astype(BF16)
        kept_ref[...] = y[: total // 2]
        sent_ref[...] = y[total // 2 :]

    half = jax.ShapeDtypeStruct((total // 2, width), BF16)
    return pl.pallas_call(
        kernel,
        grid=(width // tile,),
        in_specs=[
            pl.BlockSpec((total, depth), lambda j: (0, 0)),
            pl.BlockSpec((depth, tile), lambda j: (0, first + j)),
        ],
        out_specs=[pl.BlockSpec((total // 2, tile), lambda j: (0, j))] * 2,
        out_shape=[half, half],
        cost_estimate=SMALL,
        compiler_params=params(),
        name="feedfwd_out",
    )(activated, weight)


def norm(hidden, part, sums, gain, bias):
    width = hidden.shape[1]
    rows = hidden.shape[0] // 2

    def kernel(hidden_ref, a_ref, b_ref, gain_ref, bias_ref, residual_ref, out_ref):
        residual = hidden_ref[part * rows : (part + 1) * rows, :].astype(F32) + (
            a_ref[...].astype(F32) + b_ref[...].astype(F32)
        )
        residual_ref[...] = residual
        centered = residual - jnp.sum(residual, axis=1, keepdims=True) * (1.0 / width)
        var = jnp.sum(centered * centered, axis=1, keepdims=True) * (1.0 / width)
        out_ref[...] = (centered * lax.rsqrt(var + EPS) * gain_ref[...] + bias_ref[...]).astype(BF16)

    return pl.pallas_call(
        kernel,
        out_shape=[jax.ShapeDtypeStruct((rows, width), t) for t in (F32, BF16)],
        cost_estimate=SMALL,
        compiler_params=params(16),
        name="norm",
    )(hidden, *sums, gain.reshape(1, width), bias.reshape(1, width))


def streamed(weight):
    return pltpu.with_memory_space_constraint(weight, pltpu.HBM)


def feedfwd_in(parts, weight, which, accs=()):
    half, width = parts[0][0].shape
    units = weight.shape[0]
    count = len(parts)
    steps = 2
    piece = width // (2 * steps)

    def kernel(*refs):
        rows, w_ref = refs[: 2 * count], refs[2 * count]
        acc_refs, outs = refs[2 * count + 1 : -count], refs[-count:]
        x = jnp.concatenate([ref[...] for ref in rows], axis=0)
        y = lax.dot_general(x, w_ref[...], (((1,), (1,)), ((), ())), preferred_element_type=F32)

        @pl.when(pl.program_id(0) == 0)
        def _():
            for i, out_ref in enumerate(outs):
                here = y[2 * half * i : 2 * half * (i + 1)]
                out_ref[...] = acc_refs[i][...] + here if acc_refs else here

        @pl.when(pl.program_id(0) > 0)
        def _():
            for i, out_ref in enumerate(outs):
                out_ref[...] += y[2 * half * i : 2 * half * (i + 1)]

    rows = pl.BlockSpec((half, piece), lambda k: (0, which * steps + k))
    full = pl.BlockSpec((2 * half, units), lambda k: (0, 0))
    return pl.pallas_call(
        kernel,
        grid=(steps,),
        in_specs=[rows] * (2 * count)
        + [pl.BlockSpec((units, piece), lambda k: (0, which * steps + k))]
        + [full] * len(accs),
        out_specs=[full] * count,
        out_shape=[jax.ShapeDtypeStruct((2 * half, units), F32)] * count,
        cost_estimate=pl.CostEstimate(
            flops=4 * count * steps * half * piece * units,
            bytes_accessed=2 * steps * piece * units,
            transcendentals=0,
        ),
        compiler_params=params(24),
        name="feedfwd_in",
    )(*(x for part in parts for x in part), streamed(weight), *accs)


def down_products(control, upper, lower, groups, down_flat, segment):
    half = upper.shape[0]
    total = 2 * half
    rows = total // groups
    per = groups // 2
    width = down_flat.shape[1]
    reps = 1
    while (reps * width) % 128:
        reps *= 2
    span = reps * width
    if reps > 1:
        pos = lax.rem(lax.axis_index("mlp"), reps)
        down_flat = jnp.concatenate(
            [jnp.where(pos == i, down_flat, jnp.zeros_like(down_flat)) for i in range(reps)], axis=1
        )
    reqs = REQS
    rank = down_flat.shape[0] // reqs

    def kernel(control_ref, a_ref, b_ref, down_ref, segment_ref, out_ref, x_scratch):
        for i in range(groups):
            start = pl.multiple_of(control_ref[ORDER + i] * rows, rows)
            x = (a_ref if i < per else b_ref)[(i % per) * rows : (i % per + 1) * rows, :]
            x_scratch[pl.ds(start, rows), :] = x

        every_rank = lax.dot_general(
            down_ref[...], x_scratch[...], (((1,), (1,)), ((), ())), preferred_element_type=F32
        ).reshape(reqs, rank, total)
        chosen = lax.broadcasted_iota(jnp.int32, (reqs, total), 0) == segment_ref[...]
        out_ref[...] = jnp.sum(jnp.where(chosen[:, None, :], every_rank, 0.0), axis=0)

    own = pl.BlockSpec((half, span), lambda k, c: (0, c[SPAN]))
    return pl.pallas_call(
        kernel,
        grid_spec=pltpu.PrefetchScalarGridSpec(
            num_scalar_prefetch=1,
            grid=(1,),
            in_specs=[own, own]
            + [pl.BlockSpec(x.shape, lambda k, c: (0, 0)) for x in (down_flat, segment)],
            out_specs=pl.BlockSpec((rank, total), lambda k, c: (0, 0)),
            scratch_shapes=[pltpu.VMEM((total, span), BF16)],
        ),
        out_shape=jax.ShapeDtypeStruct((rank, total), F32),
        cost_estimate=SMALL,
        compiler_params=params(16),
        name="down_products",
    )(control, upper, lower, down_flat, segment)


def feedfwd_out_first(control, accs, lowrank, segments, up_flat, weight, width, tile, groups):
    count, units = accs[0].shape
    parts = len(accs)
    total = parts * count
    reqs, rank = REQS, lowrank.shape[0]
    rows = count // groups

    def kernel(control_ref, *refs):
        acc_refs, segment_refs = (refs[i * parts : (i + 1) * parts] for i in range(2))
        low_ref, up_ref, w_ref, act_ref, kept_ref, sent_ref, up_scratch = refs[2 * parts :]

        @pl.when(pl.program_id(0) == 0)
        def _():
            spreads = []
            for part, segment_ref in enumerate(segment_refs):
                low = low_ref[:, part * count : (part + 1) * count].astype(BF16).astype(F32)
                chosen = lax.broadcasted_iota(jnp.int32, (reqs, count), 0) == segment_ref[...]
                spread = jnp.where(chosen[:, None, :], low[None, :, :], 0.0)
                spreads.append(spread.reshape(reqs * rank, count).astype(BF16))
            up_scratch[...] = lax.dot_general(
                jnp.concatenate(spreads, axis=1),
                up_ref[...],
                (((0,), (0,)), ((), ())),
                preferred_element_type=F32,
            )
            for i in range(groups):
                for part, acc_ref in enumerate(acc_refs):
                    start = pl.multiple_of(part * count + control_ref[ORDER + i] * rows, rows)
                    preact = acc_ref[i * rows : (i + 1) * rows, :] + up_scratch[pl.ds(start, rows), :]
                    here = (i * parts + part) * rows
                    act_ref[here : here + rows, :] = jax.nn.gelu(preact, approximate=True).astype(BF16)

        y = jnp.dot(act_ref[...], w_ref[...], preferred_element_type=F32).astype(BF16)
        kept_ref[...] = y[: total // 2]
        sent_ref[...] = y[total // 2 :]

    half = jax.ShapeDtypeStruct((total // 2, width), BF16)

    def whole(*shape):
        return pl.BlockSpec(shape, lambda j, c: (0,) * len(shape))

    return pl.pallas_call(
        kernel,
        grid_spec=pltpu.PrefetchScalarGridSpec(
            num_scalar_prefetch=1,
            grid=(width // tile,),
            in_specs=[whole(count, units)] * parts
            + [whole(1, count)] * parts
            + [whole(rank, total), whole(reqs * rank, units), pl.BlockSpec((units, tile), lambda j, c: (0, j))],
            out_specs=[whole(total, units)]
            + [pl.BlockSpec((total // 2, tile), lambda j, c: (0, j))] * 2,
            scratch_shapes=[pltpu.VMEM((total, units), F32)],
        ),
        out_shape=[jax.ShapeDtypeStruct((total, units), BF16), half, half],
        cost_estimate=SMALL,
        compiler_params=params(),
        name="feedfwd_out_first",
    )(control, *accs, *segments, lowrank, up_flat, weight)


def pick(held_at, *banks):
    reqs = held_at.shape[0]
    slots, rank = banks[0][0].shape[:2]
    count = len(banks[0])

    def kernel(at_ref, *refs):
        parts = [refs[i * count : (i + 1) * count] for i in range(len(banks))]
        outs = refs[len(banks) * count : -1]
        sems = refs[-1]

        def fetch(i, part, r):
            to = outs[i].at[r * rank : (r + 1) * rank, :]
            return pltpu.make_async_copy(part.at[lax.rem(at_ref[r], slots)], to, sems.at[i, r])

        for r in range(reqs):
            for p in range(count):

                @pl.when(at_ref[r] // slots == p)
                def _():
                    for i in range(len(banks)):
                        fetch(i, parts[i][p], r).start()

        for r in range(reqs):
            for i in range(len(banks)):
                fetch(i, parts[i][0], r).wait()

    return pl.pallas_call(
        kernel,
        grid_spec=pltpu.PrefetchScalarGridSpec(
            num_scalar_prefetch=1,
            grid=(1,),
            in_specs=[pl.BlockSpec(memory_space=pl.ANY)] * (len(banks) * count),
            out_specs=[pl.BlockSpec(memory_space=pl.ANY)] * len(banks),
            scratch_shapes=[pltpu.SemaphoreType.DMA((len(banks), reqs))],
        ),
        out_shape=[jax.ShapeDtypeStruct((reqs * rank, b[0].shape[2]), BF16) for b in banks],
        cost_estimate=SIDE,
        compiler_params=params(16),
        name="pick",
    )(held_at, *(part for bank in banks for part in bank))


def join(arrays, groups):
    rows, width = arrays[0].shape
    depth = width // groups

    per = 2
    steps = groups // per

    def kernel(*refs):
        out_ref = refs[-1]
        for i, ref in enumerate(refs[:-1]):
            for g in range(per):
                out_ref[g, :, i * depth : (i + 1) * depth] = ref[:, g * depth : (g + 1) * depth]

    return pl.pallas_call(
        kernel,
        grid=(steps,),
        in_specs=[pl.BlockSpec((rows, per * depth), lambda g: (0, g))] * len(arrays),
        out_specs=pl.BlockSpec((per, rows, len(arrays) * depth), lambda g: (g, 0, 0)),
        out_shape=jax.ShapeDtypeStruct((groups, rows, len(arrays) * depth), BF16),
        cost_estimate=SMALL,
        compiler_params=params(60),
        name="join",
    )(*arrays)


def attend(control, joined, segment, count, weight):
    total = joined.shape[0]
    depth = joined.shape[1] // 3
    rows = total // count
    first = rows // 2
    width = weight.shape[1]
    tile = width // 4

    def kernel(control_ref, joined_ref, col_ref, row_ref, w_ref, att_ref, kept_ref, sent_ref, x_scratch):
        @pl.when(pl.program_id(0) == 0)
        def _():
            across = lax.broadcasted_iota(jnp.int32, (total, total), 1)
            down = lax.broadcasted_iota(jnp.int32, (total, total), 0)
            allowed = (col_ref[...] == row_ref[...]) & (across <= down)
            for head in range(depth // HS):
                q, k, v = (
                    joined_ref[:, i * depth + head * HS : i * depth + (head + 1) * HS] for i in range(3)
                )
                scores = lax.dot_general(
                    q, k, (((1,), (1,)), ((), ())), preferred_element_type=F32
                ) * (HS ** (-0.5))
                masked = jnp.where(allowed, scores, -1e30)
                exponent = jnp.exp(masked - jnp.max(masked, axis=1, keepdims=True))
                weights = (exponent / jnp.sum(exponent, axis=1, keepdims=True)).astype(BF16)
                mixed = jnp.dot(weights, v, preferred_element_type=F32).astype(BF16)
                att_ref[:, :, head * HS : (head + 1) * HS] = mixed.reshape(count, rows, HS)
            for i in range(count):
                x_scratch[i * first : (i + 1) * first, :] = att_ref[control_ref[ORDER + i], :first, :]

        y = jnp.dot(x_scratch[...], w_ref[...], preferred_element_type=F32).astype(BF16)
        kept_ref[...] = y[: total // 4]
        sent_ref[...] = y[total // 4 :]

    half = jax.ShapeDtypeStruct((total // 4, width), BF16)
    return pl.pallas_call(
        kernel,
        grid_spec=pltpu.PrefetchScalarGridSpec(
            num_scalar_prefetch=1,
            grid=(width // tile,),
            in_specs=[
                pl.BlockSpec((total, 3 * depth), lambda j, o: (0, 0)),
                pl.BlockSpec((total, 1), lambda j, o: (0, 0)),
                pl.BlockSpec((1, total), lambda j, o: (0, 0)),
                pl.BlockSpec((depth, tile), lambda j, o: (0, j)),
            ],
            out_specs=[pl.BlockSpec((count, rows, depth), lambda j, o: (0, 0, 0))]
            + [pl.BlockSpec((total // 4, tile), lambda j, o: (0, j))] * 2,
            scratch_shapes=[pltpu.VMEM((total // 2, depth), BF16)],
        ),
        out_shape=[jax.ShapeDtypeStruct((count, rows, depth), BF16), half, half],
        cost_estimate=SMALL,
        compiler_params=params(48),
        name="attend",
    )(control, joined, segment.reshape(total, 1), segment.reshape(1, total), weight)


def write_pages(joined, lookup, key_cache, value_cache):
    pages, page, depth = key_cache.shape
    blocks = lookup.shape[0]
    hits = lookup[None, :] == jnp.arange(pages, dtype=jnp.int32)[:, None]
    source = jnp.sum(jnp.where(hits, jnp.arange(1, blocks + 1, dtype=jnp.int32)[None, :], 0), axis=1) - 1

    def kernel(source_ref, k_ref, v_ref, key_cache_ref, value_cache_ref, key_ref, value_ref):
        fresh = source_ref[pl.program_id(0)] >= 0

        @pl.when(fresh)
        def _():
            key_ref[0] = k_ref[...]
            value_ref[0] = v_ref[...]

        @pl.when(jnp.logical_not(fresh))
        def _():
            key_ref[...] = key_cache_ref[...]
            value_ref[...] = value_cache_ref[...]

    def block(part):
        return pl.BlockSpec((page, depth), lambda p, source: (jnp.maximum(source[p], 0), part))

    paged = pl.BlockSpec((1, page, depth), lambda p, source: (p, 0, 0))
    return pl.pallas_call(
        kernel,
        grid_spec=pltpu.PrefetchScalarGridSpec(
            num_scalar_prefetch=1,
            grid=(pages,),
            in_specs=[block(1), block(2), paged, paged],
            out_specs=[paged, paged],
        ),
        out_shape=[jax.ShapeDtypeStruct(key_cache.shape, BF16)] * 2,
        cost_estimate=SIDE,
        compiler_params=params(16),
        name="write_pages",
    )(source, joined, joined, key_cache, value_cache)


def shards(
    queries,
    keys,
    values,
    block_hidden_input,
    attention_out_weight,
    feedfwd_in_weight,
    feedfwd_out_weight,
    norm_gain_vector,
    norm_bias_vector,
    adapter_down_factors,
    adapter_up_factors,
    paged_key_cache,
    paged_value_cache,
    request_prompt_length,
    group_page_lookup,
    adapter_per_request,
    adapter_bank_slot,
):
    tok_rows, width = block_hidden_input.shape
    groups = lax.axis_size("mlp")
    group_rows = tok_rows * groups
    head_cols = attention_out_weight.shape[0]
    me = lax.axis_index("mlp")
    bits = [1 << i for i in range(groups.bit_length() - 1)]
    minor = len(bits) - 2
    orders = bits, bits[minor : minor + 1] + bits[:minor] + bits[minor + 1 :]
    steps = list(zip(*orders))
    width_dev = width // groups
    span = width_dev
    while span % 128:
        span *= 2
    first_core = lax.rem(lax.axis_index("req"), 2) == 0
    offsets = [jnp.asarray(block_offsets(masks), jnp.int32) for masks in orders]
    control = jnp.concatenate(
        [jnp.reshape(me * width_dev // span, (1,)), jnp.where(first_core, *offsets) ^ me]
    ).astype(jnp.int32)

    req_masks = [1 << i for i in range(lax.axis_size("req").bit_length() - 1)]
    banks = jnp.swapaxes(adapter_down_factors, 1, 2), adapter_up_factors
    banks = [[x, exchange(x, "req", req_masks[-1])] for x in banks]
    slots = adapter_down_factors.shape[0]
    adapter_ids = adapter_per_request[0]
    matched = (
        adapter_ids[:, None] == jnp.arange(adapter_bank_slot.shape[0], dtype=jnp.int32)[None, :]
    )
    wanted = jnp.sum(jnp.where(matched, adapter_bank_slot[None, :], 0), axis=1)
    part_owner = jnp.asarray(block_offsets(req_masks), jnp.int32) ^ lax.axis_index("req")
    held_slot = (
        part_owner[:, None] * slots + jnp.arange(slots, dtype=jnp.int32)[None, :]
    ).reshape(-1)
    hit = wanted[:, None] == held_slot[None, :]
    held_at = jnp.sum(jnp.where(hit, jnp.arange(hit.shape[1], dtype=jnp.int32)[None, :], 0), axis=1)

    joined = lax.all_to_all(
        join((queries, keys, values), groups), "mlp", split_axis=0, concat_axis=0, tiled=True
    ).reshape(group_rows, 3 * head_cols)

    request_ends = jnp.cumsum(request_prompt_length[0])
    positions = jnp.arange(group_rows, dtype=jnp.int32)
    segment = jnp.sum((positions[:, None] >= request_ends[None, :]).astype(jnp.int32), axis=1)
    joined, segment, control, held_at = tied(joined, segment, control, held_at)
    attended, *partial_a = attend(control, joined, segment, groups, attention_out_weight)
    partial_b = out_projection(control, attended, 1, attention_out_weight)
    kept_a, sent_a = reduce_step(*partial_a, steps[0])

    sent_a, joined, banks = tied(sent_a, joined, banks)
    for mask in req_masks[-2::-1]:
        banks = [parts + [exchange(part, "req", mask) for part in parts] for parts in banks]
    pages_out = write_pages(joined, group_page_lookup[0], paged_key_cache, paged_value_cache)
    factors = pick(held_at, *banks)

    vectors = norm_gain_vector, norm_bias_vector
    residual_a, rows_a = norm(
        block_hidden_input, 0, reduce_rows(kept_a, sent_a, steps[1:]), *vectors
    )
    rows_a = grow(rows_a, steps[-1])
    sum_b, (key_pages_out, value_pages_out), (down_flat, up_flat), _ = tied(
        reduce_rows(*partial_b, steps), pages_out, factors, rows_a
    )
    residual_b, rows_b = norm(block_hidden_input, 1, sum_b, *vectors)
    ahead = steps[-2::-1]
    for masks, masks_ahead in zip(steps[:0:-1], ahead):
        if masks_ahead is steps[0]:
            rows_a = rows_a, swap(rows_a, masks_ahead)
            rows_b = grow(rows_b, masks, rows_a[1])
        else:
            rows_a = grow(rows_a, masks_ahead)
            rows_b = grow(rows_b, masks, rows_a)
    rows_b = rows_b, swap(rows_b, steps[0])

    part_rows = tok_rows // 2
    segments = [
        segment.reshape(groups, 2, part_rows)[:, part].reshape(1, groups * part_rows)
        for part in range(2)
    ]
    win = feedfwd_in_weight.T
    low_a = down_products(control, *rows_a, groups, down_flat, segments[0])
    acc_a = feedfwd_in([rows_a], win, 0)
    rows_b, low_a, acc_a = tied(rows_b, low_a, acc_a)
    low_b = down_products(control, *rows_b, groups, down_flat, segments[1])
    lowrank = jnp.concatenate([low_a, low_b], axis=1)
    acc_b = feedfwd_in([rows_b], win, 0)
    for mask in bits[:minor]:
        lowrank = lowrank + exchange(lowrank, "mlp", mask)
    lowrank, acc_b = tied(lowrank, acc_b)
    lowrank = lowrank + sum(
        exchange(lowrank, "mlp", k << minor) for k in range(1, groups >> minor)
    )
    acc = feedfwd_in([rows_a, rows_b], win, 1, acc_a + acc_b)

    wide = width * 3 // 5
    tile = wide // 3
    activated, *partial_a = feedfwd_out_first(
        control, acc, lowrank, segments, up_flat, feedfwd_out_weight, wide, tile, groups
    )
    partial_b = feedfwd_out(activated, feedfwd_out_weight, wide, width - wide, tile)
    partial_a = reduce_step(*partial_a, steps[0])
    partial_a, partial_b = tied(partial_a, partial_b)
    partial_b = reduce_step(*partial_b, steps[0])
    for masks in steps[1:-1]:
        partial_a = reduce_step(*partial_a, masks)
        partial_a, partial_b = tied(partial_a, partial_b)
        partial_b = reduce_step(*partial_b, masks)
    sums = (
        (partial_a[0], swap(partial_a[1], steps[-1])),
        (partial_b[0], swap(partial_b[1], steps[-1])),
    )
    block_out = (
        jnp.concatenate([residual_a, residual_b], axis=0)
        + jnp.concatenate([a.astype(F32) + b.astype(F32) for a, b in sums], axis=1)
    ).astype(BF16)
    return (block_out, key_pages_out, value_pages_out)


def solution(mesh):
    in_specs = (
        P(("req", "mlp"), None),
        P(("req", "mlp"), None),
        P(("req", "mlp"), None),
        P(("req", "mlp"), None),
        P("mlp", None),
        P(None, "mlp"),
        P("mlp", None),
        P(),
        P(),
        P("req", "mlp", None),
        P("req", None, "mlp"),
        P("req", None, "mlp"),
        P("req", None, "mlp"),
        P("req", None),
        P("req", None),
        P("req", None),
        P(),
    )
    out_specs = (P(("req", "mlp"), None), P("req", None, "mlp"), P("req", None, "mlp"))
    return jax.shard_map(shards, mesh=mesh, in_specs=in_specs, out_specs=out_specs, check_vma=False)
```

time: 190 us -> 181 us (0.953)
  starting transfers between devices: 35.8 us -> 30.5 us
  waiting for transfers between devices: 102 us -> 99 us
  Pallas kernels: 45 us -> 47.5 us
    ppermute x30 -> x10, waiting for transfers between devices: 85.3 us -> 0.03 us  [exchange(): return lax.ppermute(x, axis, [(i, i ^ mask) for i in range(size)])]
    ppermute x0 -> x18, waiting for transfers between devices: none -> 81.3 us  [swap(): return lax.ppermute(x, ('req', 'mlp'), pairs)]
    ppermute x30 -> x10, starting transfers between devices: 28.5 us -> 9.89 us  [exchange(): return lax.ppermute(x, axis, [(i, i ^ mask) for i in range(size)])]
    ppermute x0 -> x18, starting transfers between devices: none -> 13.3 us  [swap(): return lax.ppermute(x, ('req', 'mlp'), pairs)]
    pallas_call x5 -> x6, Pallas kernels: 13.1 us -> 20 us  [the longest x3 16.6 us: feedfwd_in(): pl.pallas_call(kernel, grid=(steps,), in_specs=[rows] * (2 * count) + [pl...]
    pallas_call x2 -> x1, Pallas kernels: 7.68 us -> 4.42 us  [out_projection(): pl.pallas_call(kernel, grid_spec=pltpu.PrefetchScalarGridSpec(num_scalar_...]
    pallas_call x1, Pallas kernels: 8.16 us -> 5.81 us  [feedfwd_out_first(): pl.pallas_call(kernel, grid_spec=pltpu.PrefetchScalarGridSpec(num_scalar_...]
  transfers between devices with their start and end apart: 31 -> 29, of which waited for: 16 -> 18; matrix products, arithmetic and copies ran while one was open for 2% -> 1% of each run, Pallas kernels for 15% -> 21%
where the time goes in v2:
time: 181 us
  waiting for transfers between devices  99 us (55%)
  Pallas kernels  47.5 us (26%)
  starting transfers between devices  30.5 us (17%)
  other arithmetic  1.84 us (1%)
    ppermute x18, waiting for transfers between devices, swap(): return lax.ppermute(x, ('req', 'mlp'), pairs)  81.3 us
    all_to_all x1, waiting for transfers between devices, shards(): lax.all_to_all(join((queries, keys, values), groups), 'mlp', split_axis=0...  17.6 us
    pallas_call x3, Pallas kernels, feedfwd_in(): pl.pallas_call(kernel, grid=(steps,), in_specs=[rows] * (2 * count) + [pl...  16.6 us
    ppermute x18, starting transfers between devices, swap(): return lax.ppermute(x, ('req', 'mlp'), pairs)  13.3 us
    ppermute x10, starting transfers between devices, exchange(): return lax.ppermute(x, axis, [(i, i ^ mask) for i in range(size)])  9.89 us
    all_to_all x1, starting transfers between devices, shards(): lax.all_to_all(join((queries, keys, values), groups), 'mlp', split_axis=0...  7.28 us
    pallas_call x1, Pallas kernels, feedfwd_out_first(): pl.pallas_call(kernel, grid_spec=pltpu.PrefetchScalarGridSpec(num_scalar_...  5.81 us
    pallas_call x1, Pallas kernels, attend(): pl.pallas_call(kernel, grid_spec=pltpu.PrefetchScalarGridSpec(num_scalar_...  5.58 us
  transfers between devices with their start and end apart: 29, of which 18 were waited for; matrix products, arithmetic and copies ran while one was open for 1% of the time, Pallas kernels for 21%

profile of v2, /device:TPU:0, one launch (start us, length us, event | category | flops | bytes accessed | tf_op | source)
XLA Modules:
  0.0 180.8 jit_solution(5253239749983206010)
XLA Ops:
  0.7 3.3 %join.1 = bf16[8,32,1536]{2,1,0:T(8,128)(2,1)} custom-call(bf16[32,4096]{1,0:T(8,128)(2,1)} %refs_0_.1, bf16[32,4096]{1,0:T(8,128)(2,1)} %refs_1_.1, bf16[32,4096]{1,0:T(8,128)(2,1)} %refs_2_.1), custom_call_target="tpu_custom_call" | custom-call | bytes 1 | tf_op jit(solution)/shard_map/join/pallas_call | solution.py:380
  4.0 7.3 %all-to-all-start = ((bf16[8,32,1536]{2,1,0:T(8,128)(2,1)}), bf16[8,32,1536]{2,1,0:T(8,128)(2,1)S(1)}, u32[]{:S(2)}, u32[]{:S(2)}) async-start(bf16[8,32,1536]{2,1,0:T(8,128)(2,1)} %join.1), calls=%async_computation | async-start | bytes 1572864 | tf_op jit(solution)/shard_map/all_to_all | solution.py:540
  11.3 1.6 collective-permute-start.2
  13.9 17.6 %all-to-all-done = bf16[8,32,1536]{2,1,0:T(8,128)(2,1)S(1)} async-done(((bf16[8,32,1536]{2,1,0:T(8,128)(2,1)}), bf16[8,32,1536]{2,1,0:T(8,128)(2,1)S(1)}, u32[]{:S(2)}, u32[]{:S(2)}) %all-to-all-start) | async-done | bytes 786464 | tf_op jit(solution)/shard_map/all_to_all | solution.py:540
  31.6 5.6 %attend.1 = (bf16[8,32,512]{2,1,0:T(8,128)(2,1)S(1)}, bf16[64,5120]{1,0:T(8,128)(2,1)S(1)}, bf16[64,5120]{1,0:T(8,128)(2,1)S(1)}) custom-call(s32[9]{0:T(128)S(1)} %pad_add_fusion.control_ref, bf16[256,1536]{1,0:T(8,128)(2,1)S(1)} %bitcast.13, s32[256,1]{1,0:T(8,128)S(1)} %copy.27.col_ref, s32[1,256]{1,0:T(1,128)S(1)} %bitcast.24, bf16[512,5120]{1,0:T(8,128)(2,1)} %w_ref.4), custom_call_target="tpu_custom_call" | custom-call | bytes 1 | tf_op jit(solution)/shard_map/attend/pallas_call | solution.py:426
  37.2 1.5 collective-permute-start
  38.7 1.5 collective-permute-start.1
  40.2 4.4 %out_projection.1 = (bf16[64,5120]{1,0:T(8,128)(2,1)S(1)}, bf16[64,5120]{1,0:T(8,128)(2,1)S(1)}) custom-call(s32[9]{0:T(128)S(1)} %pad_add_fusion.control_ref, bf16[8,32,512]{2,1,0:T(8,128)(2,1)S(1)} %get-tuple-element.82.x_ref, bf16[512,5120]{1,0:T(8,128)(2,1)} %w_ref.4), custom_call_target="tpu_custom_call" | custom-call | bytes 1 | tf_op jit(solution)/shard_map/out_projection/pallas_call | solution.py:103
  44.6 0.7 collective-permute-start.5
  45.3 2.6 %collective-permute-done.got_ref = bf16[64,5120]{1,0:T(8,128)(2,1)S(1)} collective-permute-done((bf16[64,5120]{1,0:T(8,128)(2,1)S(1)}, bf16[64,5120]{1,0:T(8,128)(2,1)S(1)}, u32[]{:S(2)}, u32[]{:S(2)}) %collective-permute-start) | collective-permute-done | bytes 655392 | tf_op jit(solution)/shard_map/ppermute | solution.py:39
  48.1 0.4 collective-permute-start.3
  48.5 7.4 %collective-permute-done.3.got_ref = bf16[32,5120]{1,0:T(8,128)(2,1)S(1)} collective-permute-done((bf16[32,5120]{1,0:T(8,128)(2,1)S(1)}, bf16[32,5120]{1,0:T(8,128)(2,1)S(1)}, u32[]{:S(2)}, u32[]{:S(2)}) %collective-permute-start.3) | collective-permute-done | bytes 327712 | tf_op jit(solution)/shard_map/ppermute | solution.py:39
  55.9 1.4 collective-permute-start.4
  57.4 1.4 collective-permute-done.5.got_ref
  59.3 0.4 collective-permute-start.11
  59.8 6.6 %collective-permute-done.4.b_ref = bf16[16,5120]{1,0:T(8,128)(2,1)S(1)} collective-permute-done((bf16[16,5120]{1,0:T(8,128)(2,1)S(1)}, bf16[16,5120]{1,0:T(8,128)(2,1)S(1)}, u32[]{:S(2)}, u32[]{:S(2)}) %collective-permute-start.4) | collective-permute-done | bytes 163872 | tf_op jit(solution)/shard_map/ppermute | solution.py:39
  66.3 0.3 norm.2
  66.9 2.1 %write_pages.1 = (bf16[3,128,512]{2,1,0:T(8,128)(2,1)}, bf16[3,128,512]{2,1,0:T(8,128)(2,1)}) custom-call(s32[3]{0:T(128)S(1)} %broadcast_add_fusion.source_ref, bf16[256,1536]{1,0:T(8,128)(2,1)S(1)} %bitcast.14, bf16[256,1536]{1,0:T(8,128)(2,1)S(1)} %bitcast.15, bf16[3,128,512]{2,1,0:T(8,128)(2,1)S(1)} %copy-done.4, bf16[3,128,512]{2,1,0:T(8,128)(2,1)S(1)} %copy-done.5), custom_call_target="tpu_custom_call" | custom-call | bytes 8388608 | tf_op jit(solution)/shard_map/write_pages/pallas_call | solution.py:471
  68.9 0.5 collective-permute-done.6.got_ref
  69.5 7.2 %collective-permute-done.12 = bf16[16,5120]{1,0:T(8,128)(2,1)S(1)} collective-permute-done((bf16[16,5120]{1,0:T(8,128)(2,1)S(1)}, bf16[16,5120]{1,0:T(8,128)(2,1)S(1)}, u32[]{:S(2)}, u32[]{:S(2)}) %collective-permute-start.12) | collective-permute-done | bytes 163872 | tf_op jit(solution)/shard_map/ppermute | solution.py:39
  76.8 2.2 %collective-permute-start.13 = (bf16[32,5120]{1,0:T(8,128)(2,1)S(1)}, bf16[32,5120]{1,0:T(8,128)(2,1)S(1)}, u32[]{:S(2)}, u32[]{:S(2)}) collective-permute-start(bf16[32,5120]{1,0:T(8,128)(2,1)S(1)} %pad_maximum_fusion.1), channel_id=1, source_target_pairs={{0,2},{1,3},{2,0},{3,1},{4,6},{5,7},{6,4},{7,5},{8,9},{9,8},{10,11... | collective-permute-start | bytes 983048 | tf_op jit(solution)/shard_map/ppermute | solution.py:39
  79.1 3.7 %pick.1 = (bf16[256,640]{1,0:T(8,128)(2,1)S(1)}, bf16[256,1728]{1,0:T(8,128)(2,1)S(1)}) custom-call(s32[16]{0:T(128)S(1)} %select_reduce_fusion.at_ref, bf16[16,16,640]{2,1,0:T(8,128)(2,1)S(1)} %bitcast.18, bf16[16,16,640]{2,1,0:T(8,128)(2,1)S(1)} %collective-permute-done.1.refs_1_, bf16[16,16,640]{2,1,0:T(8,128)(2,1)S(1)} %collective-permute-done.8.refs_2_, ...), custom_call_target="tpu_custom_call" | custom-call | bytes 8388608 | tf_op jit(solution)/shard_map/pick/pallas_call | solution.py:351
  82.8 3.6 %collective-permute-done.7.b_ref = bf16[16,5120]{1,0:T(8,128)(2,1)S(1)} collective-permute-done((bf16[16,5120]{1,0:T(8,128)(2,1)S(1)}, bf16[16,5120]{1,0:T(8,128)(2,1)S(1)}, u32[]{:S(2)}, u32[]{:S(2)}) %collective-permute-start.7) | collective-permute-done | bytes 163872 | tf_op jit(solution)/shard_map/ppermute | solution.py:39
  86.8 0.8 collective-permute-done.13
  87.6 1.8 %collective-permute-start.14 = (bf16[64,5120]{1,0:T(8,128)(2,1)S(1)}, bf16[64,5120]{1,0:T(8,128)(2,1)S(1)}, u32[]{:S(2)}, u32[]{:S(2)}) collective-permute-start(bf16[64,5120]{1,0:T(8,128)(2,1)S(1)} %pad_maximum_fusion.a_ref.refs_0_), channel_id=1, source_target_pairs={{0,1},{1,0},{2,3},{3,2},{4,5},{5,4},{6,7},{7,6},{8,10},{9,11},{10,... | collective-permute-start | bytes 1966088 | tf_op jit(solution)/shard_map/ppermute | solution.py:39
  89.5 7.5 %collective-permute-done.15 = bf16[16,5120]{1,0:T(8,128)(2,1)S(1)} collective-permute-done((bf16[16,5120]{1,0:T(8,128)(2,1)S(1)}, bf16[16,5120]{1,0:T(8,128)(2,1)S(1)}, u32[]{:S(2)}, u32[]{:S(2)}) %collective-permute-start.15) | collective-permute-done | bytes 163872 | tf_op jit(solution)/shard_map/ppermute | solution.py:39
  97.1 7.2 %collective-permute-done.16 = bf16[32,5120]{1,0:T(8,128)(2,1)S(1)} collective-permute-done((bf16[32,5120]{1,0:T(8,128)(2,1)S(1)}, bf16[32,5120]{1,0:T(8,128)(2,1)S(1)}, u32[]{:S(2)}, u32[]{:S(2)}) %collective-permute-start.16) | collective-permute-done | bytes 327712 | tf_op jit(solution)/shard_map/ppermute | solution.py:39
  104.3 1.8 collective-permute-start.17
  106.4 0.8 down_products.2
  107.2 5.5 %feedfwd_in.3.refs_5_ = f32[128,1728]{1,0:T(8,128)S(1)} custom-call(bf16[64,5120]{1,0:T(8,128)(2,1)S(1)} %pad_maximum_fusion.a_ref.refs_0_, bf16[64,5120]{1,0:T(8,128)(2,1)S(1)} %collective-permute-done.14.b_ref.refs_1_, bf16[1728,5120]{1,0:T(8,128)(2,1)} %bitcast.25), custom_call_target="tpu_custom_call" | custom-call | flops 1132462080 | bytes 8847360 | tf_op jit(solution)/shard_map/feedfwd_in/pallas_call | solution.py:199
  112.8 2.2 %collective-permute-done.17.b_ref.refs_1_.refs_3_ = bf16[64,5120]{1,0:T(8,128)(2,1)S(1)} collective-permute-done((bf16[64,5120]{1,0:T(8,128)(2,1)S(1)}, bf16[64,5120]{1,0:T(8,128)(2,1)S(1)}, u32[]{:S(2)}, u32[]{:S(2)}) %collective-permute-start.17) | collective-permute-done | bytes 655392 | tf_op jit(solution)/shard_map/ppermute | solution.py:39
  115.0 0.8 down_products.3
  115.8 1.8 collective-permute-start.18
  117.6 5.6 %feedfwd_in.4.refs_6_ = f32[128,1728]{1,0:T(8,128)S(1)} custom-call(bf16[64,5120]{1,0:T(8,128)(2,1)S(1)} %constant_dynamic-update-slice_fusion.a_ref.refs_0_.refs_2_, bf16[64,5120]{1,0:T(8,128)(2,1)S(1)} %collective-permute-done.17.b_ref.refs_1_.refs_3_, bf16[1728,5120]{1,0:T(8,128)(2,1)} %bitcast.26), custom_call_target="tpu_custom_call" | custom-call | flops 1132462080 | bytes 8847360 | tf_op jit(solution)/shard_map/feedfwd_in/pallas_call | solution.py:199
  123.3 1.7 collective-permute-start.21
  125.0 2.7 %collective-permute-start.20 = (f32[16,256]{1,0:T(8,128)S(1)}, f32[16,256]{1,0:T(8,128)S(1)}, u32[]{:S(2)}, u32[]{:S(2)}) collective-permute-start(f32[16,256]{1,0:T(8,128)S(1)} %fusion.3), channel_id=1, source_target_pairs={{0,4},{1,5},{2,6},{3,7},{4,0},{5,1},{6,2},{7,3},{8,12},{9,13},{10,... | collective-permute-start | bytes 49160 | tf_op jit(solution)/shard_map/ppermute | solution.py:31
  127.7 5.5 %feedfwd_in.5 = (f32[128,1728]{1,0:T(8,128)S(1)}, f32[128,1728]{1,0:T(8,128)S(1)}) custom-call(bf16[64,5120]{1,0:T(8,128)(2,1)S(1)} %pad_maximum_fusion.a_ref.refs_0_, bf16[64,5120]{1,0:T(8,128)(2,1)S(1)} %collective-permute-done.14.b_ref.refs_1_, bf16[64,5120]{1,0:T(8,128)(2,1)S(1)} %constant_dynamic-update-slice_fusion.a_ref.refs_0_.refs_2_, ...), custom_call_target="tpu_custom_call" | custom-call | flops 2264924160 | bytes 8847360 | tf_op jit(solution)/shard_map/feedfwd_in/pallas_call | solution.py:199
  133.3 5.8 %feedfwd_out_first.1 = (bf16[256,1728]{1,0:T(8,128)(2,1)S(1)}, bf16[128,3072]{1,0:T(8,128)(2,1)S(1)}, bf16[128,3072]{1,0:T(8,128)(2,1)S(1)}) custom-call(s32[9]{0:T(128)S(1)} %pad_add_fusion.control_ref, f32[128,1728]{1,0:T(8,128)S(1)} %get-tuple-element.112.refs_0_, f32[128,1728]{1,0:T(8,128)S(1)} %get-tuple-element.113.refs_1_, ...), custom_call_target="tpu_custom_call" | custom-call | bytes 1 | tf_op jit(solution)/shard_map/feedfwd_out_first/pallas_call | solution.py:306
  139.1 0.4 collective-permute-start.22
  139.5 2.8 %feedfwd_out.1 = (bf16[128,2048]{1,0:T(8,128)(2,1)S(1)}, bf16[128,2048]{1,0:T(8,128)(2,1)S(1)}) custom-call(bf16[256,1728]{1,0:T(8,128)(2,1)S(1)} %get-tuple-element.120.x_ref, bf16[1728,5120]{1,0:T(8,128)(2,1)S(1)} %bitcast.12), custom_call_target="tpu_custom_call" | custom-call | bytes 1 | tf_op jit(solution)/shard_map/feedfwd_out/pallas_call | solution.py:132
  142.3 9.8 %collective-permute-done.22.got_ref = bf16[128,3072]{1,0:T(8,128)(2,1)S(1)} collective-permute-done((bf16[128,3072]{1,0:T(8,128)(2,1)S(1)}, bf16[128,3072]{1,0:T(8,128)(2,1)S(1)}, u32[]{:S(2)}, u32[]{:S(2)}) %collective-permute-start.22) | collective-permute-done | bytes 786464 | tf_op jit(solution)/shard_map/ppermute | solution.py:39
  152.6 9.0 %collective-permute-done.23.got_ref = bf16[64,3072]{1,0:T(8,128)(2,1)S(1)} collective-permute-done((bf16[64,3072]{1,0:T(8,128)(2,1)S(1)}, bf16[64,3072]{1,0:T(8,128)(2,1)S(1)}, u32[]{:S(2)}, u32[]{:S(2)}) %collective-permute-start.23) | collective-permute-done | bytes 393248 | tf_op jit(solution)/shard_map/ppermute | solution.py:39
  161.7 2.6 %collective-permute-done.24.got_ref = bf16[128,2048]{1,0:T(8,128)(2,1)S(1)} collective-permute-done((bf16[128,2048]{1,0:T(8,128)(2,1)S(1)}, bf16[128,2048]{1,0:T(8,128)(2,1)S(1)}, u32[]{:S(2)}, u32[]{:S(2)}) %collective-permute-start.24) | collective-permute-done | bytes 524320 | tf_op jit(solution)/shard_map/ppermute | solution.py:39
  164.6 2.2 %collective-permute-start.25 = (bf16[32,3072]{1,0:T(8,128)(2,1)S(1)}, bf16[32,3072]{1,0:T(8,128)(2,1)S(1)}, u32[]{:S(2)}, u32[]{:S(2)}) collective-permute-start(bf16[32,3072]{1,0:T(8,128)(2,1)S(1)} %get-tuple-element.132), channel_id=1, source_target_pairs={{0,4},{1,5},{2,6},{3,7},{4,0},{5,1},{6,2},{7,3},{8,12},{9,13},{10,... | collective-permute-start | bytes 589832 | tf_op jit(solution)/shard_map/ppermute | solution.py:39
  166.7 6.8 %collective-permute-done.26.got_ref = bf16[64,2048]{1,0:T(8,128)(2,1)S(1)} collective-permute-done((bf16[64,2048]{1,0:T(8,128)(2,1)S(1)}, bf16[64,2048]{1,0:T(8,128)(2,1)S(1)}, u32[]{:S(2)}, u32[]{:S(2)}) %collective-permute-start.26) | collective-permute-done | bytes 262176 | tf_op jit(solution)/shard_map/ppermute | solution.py:39
  173.7 0.8 collective-permute-done.25
  174.6 5.4 %collective-permute-done.27 = bf16[32,2048]{1,0:T(8,128)(2,1)S(1)} collective-permute-done((bf16[32,2048]{1,0:T(8,128)(2,1)S(1)}, bf16[32,2048]{1,0:T(8,128)(2,1)S(1)}, u32[]{:S(2)}, u32[]{:S(2)}) %collective-permute-start.27) | collective-permute-done | bytes 131104 | tf_op jit(solution)/shard_map/ppermute | solution.py:39
  180.0 0.8 fusion
  (110 shorter events, 4.1 us)
Async XLA Ops:
  0.6 12.6 %copy-start.17 = (s32[4]{0:T(128)S(1)}, s32[4]{0:T(128)}, u32[]{:S(2)}) copy-start(s32[4]{0:T(128)} %constant.39.clone) | copy-start | bytes 52
  0.6 12.6 %copy-start.12 = (s32[8]{0:T(128)S(1)}, s32[8]{0:T(128)}, u32[]{:S(2)}) copy-start(s32[8]{0:T(128)} %constant.37.clone) | copy-start | bytes 100
  0.7 12.6 %copy-start.13 = (s32[8]{0:T(128)S(1)}, s32[8]{0:T(128)}, u32[]{:S(2)}) copy-start(s32[8]{0:T(128)} %constant.38.clone) | copy-start | bytes 100
  0.7 10.6 %copy-start.1 = (bf16[16,16,1728]{2,1,0:T(8,128)(2,1)S(1)}, bf16[16,16,1728]{2,1,0:T(8,128)(2,1)}, u32[]{:S(2)}) copy-start(bf16[16,16,1728]{2,1,0:T(8,128)(2,1)} %refs_4_) | copy-start | bytes 2654212
  0.7 12.2 %copy-start.11 = (s32[1,16]{1,0:T(1,128)S(1)}, s32[1,16]{1,0:T(1,128)}, u32[]{:S(2)}) copy-start(s32[1,16]{1,0:T(1,128)} %param.33) | copy-start | bytes 196
  0.7 12.8 %copy-start.14 = (s32[64]{0:T(128)S(1)}, s32[64]{0:T(128)}, u32[]{:S(2)}) copy-start(s32[64]{0:T(128)} %param.36) | copy-start | bytes 772
  0.7 12.8 %copy-start.15 = (s32[1,16]{1,0:T(1,128)S(1)}, s32[1,16]{1,0:T(1,128)}, u32[]{:S(2)}) copy-start(s32[1,16]{1,0:T(1,128)} %param.35) | copy-start | bytes 196
  4.0 27.5 %all-to-all-start = ((bf16[8,32,1536]{2,1,0:T(8,128)(2,1)}), bf16[8,32,1536]{2,1,0:T(8,128)(2,1)S(1)}, u32[]{:S(2)}, u32[]{:S(2)}) async-start(bf16[8,32,1536]{2,1,0:T(8,128)(2,1)} %join.1), calls=%async_computation | async-start | bytes 1572864 | tf_op jit(solution)/shard_map/all_to_all | solution.py:540
  11.3 36.8 %collective-permute-start.2 = (bf16[16,16,1728]{2,1,0:T(8,128)(2,1)S(1)}, bf16[16,16,1728]{2,1,0:T(8,128)(2,1)S(1)}, u32[]{:S(2)}, u32[]{:S(2)}) collective-permute-start(bf16[16,16,1728]{2,1,0:T(8,128)(2,1)S(1)} %copy-done.1), channel_id=1, source_target_pairs={{0,16},{8,24},{16,0},{24,8},{1,17},{9,25},{17,1},{25,9},{2,18},{10... | collective-permute-start | bytes 2654216 | tf_op jit(solution)/shard_map/ppermute | solution.py:31
  37.2 10.7 %collective-permute-start = (bf16[64,5120]{1,0:T(8,128)(2,1)S(1)}, bf16[64,5120]{1,0:T(8,128)(2,1)S(1)}, u32[]{:S(2)}, u32[]{:S(2)}) collective-permute-start(bf16[64,5120]{1,0:T(8,128)(2,1)S(1)} %get-tuple-element.75), channel_id=1, source_target_pairs={{0,1},{1,0},{2,3},{3,2},{4,5},{5,4},{6,7},{7,6},{8,10},{9,11},{10,... | collective-permute-start | bytes 1966088 | tf_op jit(solution)/shard_map/ppermute | solution.py:39
  38.7 9.4 %collective-permute-start.1 = (bf16[16,16,640]{2,1,0:T(8,128)(2,1)S(1)}, bf16[16,16,640]{2,1,0:T(8,128)(2,1)S(1)}, u32[]{:S(2)}, u32[]{:S(2)}) collective-permute-start(bf16[16,16,640]{2,1,0:T(8,128)(2,1)S(1)} %bitcast.16), channel_id=1, source_target_pairs={{0,16},{8,24},{16,0},{24,8},{1,17},{9,25},{17,1},{25,9},{2,18},{10... | collective-permute-start | bytes 983048 | tf_op jit(solution)/shard_map/ppermute | solution.py:31
  44.6 14.2 %collective-permute-start.5 = (bf16[64,5120]{1,0:T(8,128)(2,1)S(1)}, bf16[64,5120]{1,0:T(8,128)(2,1)S(1)}, u32[]{:S(2)}, u32[]{:S(2)}) collective-permute-start(bf16[64,5120]{1,0:T(8,128)(2,1)S(1)} %get-tuple-element.84), channel_id=1, source_target_pairs={{0,1},{1,0},{2,3},{3,2},{4,5},{5,4},{6,7},{7,6},{8,10},{9,11},{10,... | collective-permute-start | bytes 1966088 | tf_op jit(solution)/shard_map/ppermute | solution.py:39
  48.0 11.7 %copy-start.16 = (s32[1,2]{1,0:T(1,128)S(1)}, s32[1,2]{1,0:T(1,128)}, u32[]{:S(2)}) copy-start(s32[1,2]{1,0:T(1,128)} %param.34) | copy-start | bytes 28
  48.0 18.3 %copy-start = (bf16[32,5120]{1,0:T(8,128)(2,1)S(1)}, bf16[32,5120]{1,0:T(8,128)(2,1)}, u32[]{:S(2)}) copy-start(bf16[32,5120]{1,0:T(8,128)(2,1)} %hidden_ref.3) | copy-start | bytes 983044
  48.0 18.3 %copy-start.9 = (f32[5120]{0:T(1024)S(1)}, f32[5120]{0:T(1024)}, u32[]{:S(2)}) copy-start(f32[5120]{0:T(1024)} %param.27) | copy-start | bytes 61444
  48.0 18.3 %copy-start.10 = (f32[5120]{0:T(1024)S(1)}, f32[5120]{0:T(1024)}, u32[]{:S(2)}) copy-start(f32[5120]{0:T(1024)} %param.28) | copy-start | bytes 61444
  48.1 7.8 %collective-permute-start.3 = (bf16[32,5120]{1,0:T(8,128)(2,1)S(1)}, bf16[32,5120]{1,0:T(8,128)(2,1)S(1)}, u32[]{:S(2)}, u32[]{:S(2)}) collective-permute-start(bf16[32,5120]{1,0:T(8,128)(2,1)S(1)} %get-tuple-element.78), channel_id=1, source_target_pairs={{0,2},{1,3},{2,0},{3,1},{4,6},{5,7},{6,4},{7,5},{8,9},{9,8},{10,11... | collective-permute-start | bytes 983048 | tf_op jit(solution)/shard_map/ppermute | solution.py:39
  55.9 10.9 %copy-start.4 = (bf16[3,128,512]{2,1,0:T(8,128)(2,1)S(1)}, bf16[3,128,512]{2,1,0:T(8,128)(2,1)}, u32[]{:S(2)}) copy-start(bf16[3,128,512]{2,1,0:T(8,128)(2,1)} %key_cache_ref.1) | copy-start | bytes 1179652
  55.9 10.9 %copy-start.5 = (bf16[3,128,512]{2,1,0:T(8,128)(2,1)S(1)}, bf16[3,128,512]{2,1,0:T(8,128)(2,1)}, u32[]{:S(2)}) copy-start(bf16[3,128,512]{2,1,0:T(8,128)(2,1)} %value_cache_ref.1) | copy-start | bytes 1179652
  55.9 10.4 %collective-permute-start.4 = (bf16[16,5120]{1,0:T(8,128)(2,1)S(1)}, bf16[16,5120]{1,0:T(8,128)(2,1)S(1)}, u32[]{:S(2)}, u32[]{:S(2)}) collective-permute-start(bf16[16,5120]{1,0:T(8,128)(2,1)S(1)} %get-tuple-element.80), channel_id=1, source_target_pairs={{0,4},{1,5},{2,6},{3,7},{4,0},{5,1},{6,2},{7,3},{8,12},{9,13},{10,... | collective-permute-start | bytes 491528 | tf_op jit(solution)/shard_map/ppermute | solution.py:39
  58.9 10.6 %collective-permute-start.6 = (bf16[32,5120]{1,0:T(8,128)(2,1)S(1)}, bf16[32,5120]{1,0:T(8,128)(2,1)S(1)}, u32[]{:S(2)}, u32[]{:S(2)}) collective-permute-start(bf16[32,5120]{1,0:T(8,128)(2,1)S(1)} %get-tuple-element.86), channel_id=1, source_target_pairs={{0,2},{1,3},{2,0},{3,1},{4,6},{5,7},{6,4},{7,5},{8,9},{9,8},{10,11... | collective-permute-start | bytes 983048 | tf_op jit(solution)/shard_map/ppermute | solution.py:39
  59.2 19.9 %collective-permute-start.10 = (bf16[16,16,1728]{2,1,0:T(8,128)(2,1)S(1)}, bf16[16,16,1728]{2,1,0:T(8,128)(2,1)S(1)}, u32[]{:S(2)}, u32[]{:S(2)}) collective-permute-start(bf16[16,16,1728]{2,1,0:T(8,128)(2,1)S(1)} %copy-done.1), channel_id=1, source_target_pairs={{0,8},{8,0},{16,24},{24,16},{1,9},{9,1},{17,25},{25,17},{2,10},{10... | collective-permute-start | bytes 2654216 | tf_op jit(solution)/shard_map/ppermute | solution.py:31
  59.3 19.8 %collective-permute-start.11 = (bf16[16,16,1728]{2,1,0:T(8,128)(2,1)S(1)}, bf16[16,16,1728]{2,1,0:T(8,128)(2,1)S(1)}, u32[]{:S(2)}, u32[]{:S(2)}) collective-permute-start(bf16[16,16,1728]{2,1,0:T(8,128)(2,1)S(1)} %collective-permute-done.2.refs_5_), channel_id=1, source_target_pairs={{0,8},{8,0},{16,24},{24,16},{1,9},{9,1},{17,25},{25,17},{2,10},{10... | collective-permute-start | bytes 2654216 | tf_op jit(solution)/shard_map/ppermute | solution.py:31
  66.7 10.1 %collective-permute-start.12 = (bf16[16,5120]{1,0:T(8,128)(2,1)S(1)}, bf16[16,5120]{1,0:T(8,128)(2,1)S(1)}, u32[]{:S(2)}, u32[]{:S(2)}) collective-permute-start(bf16[16,5120]{1,0:T(8,128)(2,1)S(1)} %get-tuple-element.99), channel_id=1, source_target_pairs={{0,4},{1,5},{2,6},{3,7},{4,0},{5,1},{6,2},{7,3},{8,12},{9,13},{10,... | collective-permute-start | bytes 491528 | tf_op jit(solution)/shard_map/ppermute | solution.py:39
  66.8 10.0 %collective-permute-start.8 = (bf16[16,16,640]{2,1,0:T(8,128)(2,1)S(1)}, bf16[16,16,640]{2,1,0:T(8,128)(2,1)S(1)}, u32[]{:S(2)}, u32[]{:S(2)}) collective-permute-start(bf16[16,16,640]{2,1,0:T(8,128)(2,1)S(1)} %bitcast.17), channel_id=1, source_target_pairs={{0,8},{8,0},{16,24},{24,16},{1,9},{9,1},{17,25},{25,17},{2,10},{10... | collective-permute-start | bytes 983048 | tf_op jit(solution)/shard_map/ppermute | solution.py:31
  69.4 9.6 %collective-permute-start.9 = (bf16[16,16,640]{2,1,0:T(8,128)(2,1)S(1)}, bf16[16,16,640]{2,1,0:T(8,128)(2,1)S(1)}, u32[]{:S(2)}, u32[]{:S(2)}) collective-permute-start(bf16[16,16,640]{2,1,0:T(8,128)(2,1)S(1)} %collective-permute-done.1.refs_1_), channel_id=1, source_target_pairs={{0,8},{8,0},{16,24},{24,16},{1,9},{9,1},{17,25},{25,17},{2,10},{10... | collective-permute-start | bytes 983048 | tf_op jit(solution)/shard_map/ppermute | solution.py:31
  76.8 9.6 %collective-permute-start.7 = (bf16[16,5120]{1,0:T(8,128)(2,1)S(1)}, bf16[16,5120]{1,0:T(8,128)(2,1)S(1)}, u32[]{:S(2)}, u32[]{:S(2)}) collective-permute-start(bf16[16,5120]{1,0:T(8,128)(2,1)S(1)} %get-tuple-element.88), channel_id=1, source_target_pairs={{0,4},{1,5},{2,6},{3,7},{4,0},{5,1},{6,2},{7,3},{8,12},{9,13},{10,... | collective-permute-start | bytes 491528 | tf_op jit(solution)/shard_map/ppermute | solution.py:39
  76.8 10.8 %collective-permute-start.13 = (bf16[32,5120]{1,0:T(8,128)(2,1)S(1)}, bf16[32,5120]{1,0:T(8,128)(2,1)S(1)}, u32[]{:S(2)}, u32[]{:S(2)}) collective-permute-start(bf16[32,5120]{1,0:T(8,128)(2,1)S(1)} %pad_maximum_fusion.1), channel_id=1, source_target_pairs={{0,2},{1,3},{2,0},{3,1},{4,6},{5,7},{6,4},{7,5},{8,9},{9,8},{10,11... | collective-permute-start | bytes 983048 | tf_op jit(solution)/shard_map/ppermute | solution.py:39
  82.8 14.2 %copy-start.2 = (bf16[256,1728]{1,0:T(8,128)(2,1)}, bf16[256,1728]{1,0:T(8,128)(2,1)S(1)}, u32[]{:S(2)}) copy-start(bf16[256,1728]{1,0:T(8,128)(2,1)S(1)} %get-tuple-element.115.refs_5_) | copy-start | bytes 2654212
  86.7 10.4 %copy-start.7 = (f32[16,5120]{1,0:T(8,128)}, f32[16,5120]{1,0:T(8,128)S(1)}, u32[]{:S(2)}) copy-start(f32[16,5120]{1,0:T(8,128)S(1)} %get-tuple-element.102) | copy-start | bytes 983044
  86.7 10.2 %collective-permute-start.15 = (bf16[16,5120]{1,0:T(8,128)(2,1)S(1)}, bf16[16,5120]{1,0:T(8,128)(2,1)S(1)}, u32[]{:S(2)}, u32[]{:S(2)}) collective-permute-start(bf16[16,5120]{1,0:T(8,128)(2,1)S(1)} %get-tuple-element.103), channel_id=1, source_target_pairs={{0,4},{1,5},{2,6},{3,7},{4,0},{5,1},{6,2},{7,3},{8,12},{9,13},{10,... | collective-permute-start | bytes 491528 | tf_op jit(solution)/shard_map/ppermute | solution.py:39
  87.6 16.6 %collective-permute-start.14 = (bf16[64,5120]{1,0:T(8,128)(2,1)S(1)}, bf16[64,5120]{1,0:T(8,128)(2,1)S(1)}, u32[]{:S(2)}, u32[]{:S(2)}) collective-permute-start(bf16[64,5120]{1,0:T(8,128)(2,1)S(1)} %pad_maximum_fusion.a_ref.refs_0_), channel_id=1, source_target_pairs={{0,1},{1,0},{2,3},{3,2},{4,5},{5,4},{6,7},{7,6},{8,10},{9,11},{10,... | collective-permute-start | bytes 1966088 | tf_op jit(solution)/shard_map/ppermute | solution.py:39
  97.0 7.3 %collective-permute-start.16 = (bf16[32,5120]{1,0:T(8,128)(2,1)S(1)}, bf16[32,5120]{1,0:T(8,128)(2,1)S(1)}, u32[]{:S(2)}, u32[]{:S(2)}) collective-permute-start(bf16[32,5120]{1,0:T(8,128)(2,1)S(1)} %pad_maximum_fusion.2), channel_id=1, source_target_pairs={{0,2},{1,3},{2,0},{3,1},{4,6},{5,7},{6,4},{7,5},{8,9},{9,8},{10,11... | collective-permute-start | bytes 983048 | tf_op jit(solution)/shard_map/ppermute | solution.py:39
  104.3 10.7 %collective-permute-start.17 = (bf16[64,5120]{1,0:T(8,128)(2,1)S(1)}, bf16[64,5120]{1,0:T(8,128)(2,1)S(1)}, u32[]{:S(2)}, u32[]{:S(2)}) collective-permute-start(bf16[64,5120]{1,0:T(8,128)(2,1)S(1)} %constant_dynamic-update-slice_fusion.a_ref.refs_0_.refs_2_), channel_id=1, source_target_pairs={{0,1},{1,0},{2,3},{3,2},{4,5},{5,4},{6,7},{7,6},{8,10},{9,11},{10,... | collective-permute-start | bytes 1966088 | tf_op jit(solution)/shard_map/ppermute | solution.py:39
  115.8 7.4 %collective-permute-start.18 = (f32[16,256]{1,0:T(8,128)S(1)}, f32[16,256]{1,0:T(8,128)S(1)}, u32[]{:S(2)}, u32[]{:S(2)}) collective-permute-start(f32[16,256]{1,0:T(8,128)S(1)} %pad_maximum_fusion.3), channel_id=1, source_target_pairs={{0,1},{1,0},{2,3},{3,2},{4,5},{5,4},{6,7},{7,6},{8,9},{9,8},{10,11... | collective-permute-start | bytes 49160 | tf_op jit(solution)/shard_map/ppermute | solution.py:31
  117.6 15.6 %slice-start = ((s8[17694720]{0:T(1024)(128)(4,1)}), s8[4194304]{0:T(1024)(128)(4,1)S(1)}, s32[]{:S(2)}) async-start(s8[17694720]{0:T(1024)(128)(4,1)} %bitcast.11), calls=%async_computation.1 | async-start | bytes 8388608
  117.6 15.7 %slice-start.1 = ((s8[17694720]{0:T(1024)(128)(4,1)}), s8[4194304]{0:T(1024)(128)(4,1)S(1)}, s32[]{:S(2)}) async-start(s8[17694720]{0:T(1024)(128)(4,1)} %bitcast.11), calls=%async_computation.2 | async-start | bytes 8388608
  117.6 15.7 %slice-start.2 = ((s8[17694720]{0:T(1024)(128)(4,1)}), s8[4194304]{0:T(1024)(128)(4,1)S(1)}, s32[]{:S(2)}) async-start(s8[17694720]{0:T(1024)(128)(4,1)} %bitcast.11), calls=%async_computation.3 | async-start | bytes 8388608
  123.3 9.9 %collective-permute-start.21 = (f32[16,256]{1,0:T(8,128)S(1)}, f32[16,256]{1,0:T(8,128)S(1)}, u32[]{:S(2)}, u32[]{:S(2)}) collective-permute-start(f32[16,256]{1,0:T(8,128)S(1)} %fusion.3), channel_id=1, source_target_pairs={{0,6},{1,7},{2,4},{3,5},{4,2},{5,3},{6,0},{7,1},{8,14},{9,15},{10,... | collective-permute-start | bytes 49160 | tf_op jit(solution)/shard_map/ppermute | solution.py:31
  125.0 8.2 %collective-permute-start.19 = (f32[16,256]{1,0:T(8,128)S(1)}, f32[16,256]{1,0:T(8,128)S(1)}, u32[]{:S(2)}, u32[]{:S(2)}) collective-permute-start(f32[16,256]{1,0:T(8,128)S(1)} %fusion.3), channel_id=1, source_target_pairs={{0,2},{1,3},{2,0},{3,1},{4,6},{5,7},{6,4},{7,5},{8,10},{9,11},{10,... | collective-permute-start | bytes 49160 | tf_op jit(solution)/shard_map/ppermute | solution.py:31
  125.0 8.2 %collective-permute-start.20 = (f32[16,256]{1,0:T(8,128)S(1)}, f32[16,256]{1,0:T(8,128)S(1)}, u32[]{:S(2)}, u32[]{:S(2)}) collective-permute-start(f32[16,256]{1,0:T(8,128)S(1)} %fusion.3), channel_id=1, source_target_pairs={{0,4},{1,5},{2,6},{3,7},{4,0},{5,1},{6,2},{7,3},{8,12},{9,13},{10,... | collective-permute-start | bytes 49160 | tf_op jit(solution)/shard_map/ppermute | solution.py:31
  139.1 12.9 %collective-permute-start.22 = (bf16[128,3072]{1,0:T(8,128)(2,1)S(1)}, bf16[128,3072]{1,0:T(8,128)(2,1)S(1)}, u32[]{:S(2)}, u32[]{:S(2)}) collective-permute-start(bf16[128,3072]{1,0:T(8,128)(2,1)S(1)} %get-tuple-element.117), channel_id=1, source_target_pairs={{0,1},{1,0},{2,3},{3,2},{4,5},{5,4},{6,7},{7,6},{8,10},{9,11},{10,... | collective-permute-start | bytes 2359304 | tf_op jit(solution)/shard_map/ppermute | solution.py:39
  152.3 12.1 %collective-permute-start.24 = (bf16[128,2048]{1,0:T(8,128)(2,1)S(1)}, bf16[128,2048]{1,0:T(8,128)(2,1)S(1)}, u32[]{:S(2)}, u32[]{:S(2)}) collective-permute-start(bf16[128,2048]{1,0:T(8,128)(2,1)S(1)} %get-tuple-element.128), channel_id=1, source_target_pairs={{0,1},{1,0},{2,3},{3,2},{4,5},{5,4},{6,7},{7,6},{8,10},{9,11},{10,... | collective-permute-start | bytes 1572872 | tf_op jit(solution)/shard_map/ppermute | solution.py:39
  152.6 9.0 %collective-permute-start.23 = (bf16[64,3072]{1,0:T(8,128)(2,1)S(1)}, bf16[64,3072]{1,0:T(8,128)(2,1)S(1)}, u32[]{:S(2)}, u32[]{:S(2)}) collective-permute-start(bf16[64,3072]{1,0:T(8,128)(2,1)S(1)} %get-tuple-element.124), channel_id=1, source_target_pairs={{0,2},{1,3},{2,0},{3,1},{4,6},{5,7},{6,4},{7,5},{8,9},{9,8},{10,11... | collective-permute-start | bytes 1179656 | tf_op jit(solution)/shard_map/ppermute | solution.py:39
  164.5 15.5 %copy-start.8 = (f32[16,5120]{1,0:T(8,128)S(1)}, f32[16,5120]{1,0:T(8,128)}, u32[]{:S(2)}) copy-start(f32[16,5120]{1,0:T(8,128)} %copy-done.7) | copy-start | bytes 983044
  164.5 9.1 %collective-permute-start.26 = (bf16[64,2048]{1,0:T(8,128)(2,1)S(1)}, bf16[64,2048]{1,0:T(8,128)(2,1)S(1)}, u32[]{:S(2)}, u32[]{:S(2)}) collective-permute-start(bf16[64,2048]{1,0:T(8,128)(2,1)S(1)} %get-tuple-element.134), channel_id=1, source_target_pairs={{0,2},{1,3},{2,0},{3,1},{4,6},{5,7},{6,4},{7,5},{8,9},{9,8},{10,11... | collective-permute-start | bytes 786440 | tf_op jit(solution)/shard_map/ppermute | solution.py:39
  164.6 10.0 %collective-permute-start.25 = (bf16[32,3072]{1,0:T(8,128)(2,1)S(1)}, bf16[32,3072]{1,0:T(8,128)(2,1)S(1)}, u32[]{:S(2)}, u32[]{:S(2)}) collective-permute-start(bf16[32,3072]{1,0:T(8,128)(2,1)S(1)} %get-tuple-element.132), channel_id=1, source_target_pairs={{0,4},{1,5},{2,6},{3,7},{4,0},{5,1},{6,2},{7,3},{8,12},{9,13},{10,... | collective-permute-start | bytes 589832 | tf_op jit(solution)/shard_map/ppermute | solution.py:39
  173.6 6.3 %collective-permute-start.27 = (bf16[32,2048]{1,0:T(8,128)(2,1)S(1)}, bf16[32,2048]{1,0:T(8,128)(2,1)S(1)}, u32[]{:S(2)}, u32[]{:S(2)}) collective-permute-start(bf16[32,2048]{1,0:T(8,128)(2,1)S(1)} %get-tuple-element.136), channel_id=1, source_target_pairs={{0,4},{1,5},{2,6},{3,7},{4,0},{5,1},{6,2},{7,3},{8,12},{9,13},{10,... | collective-permute-start | bytes 393224 | tf_op jit(solution)/shard_map/ppermute | solution.py:39
  (4 other events, 37.2 us)

commit v3 on v2

--- a/solution.py
+++ b/solution.py
@@ -368,7 +368,7 @@
     rows, width = arrays[0].shape
     depth = width // groups
 
-    per = 2
+    per = 4
     steps = groups // per
 
     def kernel(*refs):
@@ -548,6 +548,7 @@
     attended, *partial_a = attend(control, joined, segment, groups, attention_out_weight)
     partial_b = out_projection(control, attended, 1, attention_out_weight)
     kept_a, sent_a = reduce_step(*partial_a, steps[0])
+    sent_a = after(sent_a, partial_b)
 
     sent_a, joined, banks = tied(sent_a, joined, banks)
     for mask in req_masks[-2::-1]:
@@ -556,12 +557,15 @@
     factors = pick(held_at, *banks)
 
     vectors = norm_gain_vector, norm_bias_vector
-    residual_a, rows_a = norm(
-        block_hidden_input, 0, reduce_rows(kept_a, sent_a, steps[1:]), *vectors
-    )
-    rows_a = grow(rows_a, steps[-1])
+    sum_a = reduce_rows(kept_a, sent_a, steps[1:])
+    partial_b = reduce_step(*partial_b, steps[0])
+    sum_a = after(sum_a, partial_b)
+    residual_a, rows_a = norm(block_hidden_input, 0, sum_a, *vectors)
+    for masks in steps[1:-1]:
+        partial_b = reduce_step(*partial_b, masks)
+    rows_a = grow(rows_a, steps[-1], partial_b)
     sum_b, (key_pages_out, value_pages_out), (down_flat, up_flat), _ = tied(
-        reduce_rows(*partial_b, steps), pages_out, factors, rows_a
+        reduce_rows(*partial_b, steps[-1:]), pages_out, factors, rows_a
     )
     residual_b, rows_b = norm(block_hidden_input, 1, sum_b, *vectors)
     ahead = steps[-2::-1]

time: 181 us -> 178 us (0.983)
    ppermute x18, waiting for transfers between devices: 81.3 us -> 77.4 us  [swap(): return lax.ppermute(x, ('req', 'mlp'), pairs)]
    ppermute x10, waiting for transfers between devices: 0.03 us -> 3.28 us  [exchange(): return lax.ppermute(x, axis, [(i, i ^ mask) for i in range(size)])]
  transfers between devices with their start and end apart: 29 -> 29, of which waited for: 18 -> 19; matrix products, arithmetic and copies ran while one was open for 1% -> 1% of each run, Pallas kernels for 21% -> 21%
where the time goes in v3:
time: 178 us
  waiting for transfers between devices  98.3 us (55%)
  Pallas kernels  46.2 us (26%)
  starting transfers between devices  29.5 us (17%)
  other arithmetic  1.82 us (1%)
    ppermute x18, waiting for transfers between devices, swap(): return lax.ppermute(x, ('req', 'mlp'), pairs)  77.4 us
    all_to_all x1, waiting for transfers between devices, shards(): lax.all_to_all(join((queries, keys, values), groups), 'mlp', split_axis=0...  17.6 us
    pallas_call x3, Pallas kernels, feedfwd_in(): pl.pallas_call(kernel, grid=(steps,), in_specs=[rows] * (2 * count) + [pl...  16.6 us
    ppermute x18, starting transfers between devices, swap(): return lax.ppermute(x, ('req', 'mlp'), pairs)  12.9 us
    ppermute x10, starting transfers between devices, exchange(): return lax.ppermute(x, axis, [(i, i ^ mask) for i in range(size)])  9.33 us
    all_to_all x1, starting transfers between devices, shards(): lax.all_to_all(join((queries, keys, values), groups), 'mlp', split_axis=0...  7.28 us
    pallas_call x1, Pallas kernels, feedfwd_out_first(): pl.pallas_call(kernel, grid_spec=pltpu.PrefetchScalarGridSpec(num_scalar_...  5.81 us
    pallas_call x1, Pallas kernels, attend(): pl.pallas_call(kernel, grid_spec=pltpu.PrefetchScalarGridSpec(num_scalar_...  5.58 us
  transfers between devices with their start and end apart: 29, of which 19 were waited for; matrix products, arithmetic and copies ran while one was open for 1% of the time, Pallas kernels for 21%

profile of v3, /device:TPU:0, one launch (start us, length us, event | category | flops | bytes accessed | tf_op | source)
XLA Modules:
  0.0 177.8 jit_solution(14156545306108019284)
XLA Ops:
  0.7 2.1 %join.1 = bf16[8,32,1536]{2,1,0:T(8,128)(2,1)} custom-call(bf16[32,4096]{1,0:T(8,128)(2,1)} %refs_0_.1, bf16[32,4096]{1,0:T(8,128)(2,1)} %refs_1_.1, bf16[32,4096]{1,0:T(8,128)(2,1)} %refs_2_.1), custom_call_target="tpu_custom_call" | custom-call | bytes 1 | tf_op jit(solution)/shard_map/join/pallas_call | solution.py:380
  2.8 7.3 %all-to-all-start = ((bf16[8,32,1536]{2,1,0:T(8,128)(2,1)}), bf16[8,32,1536]{2,1,0:T(8,128)(2,1)S(1)}, u32[]{:S(2)}, u32[]{:S(2)}) async-start(bf16[8,32,1536]{2,1,0:T(8,128)(2,1)} %join.1), calls=%async_computation | async-start | bytes 1572864 | tf_op jit(solution)/shard_map/all_to_all | solution.py:540
  10.1 1.6 collective-permute-start.2
  12.6 17.6 %all-to-all-done = bf16[8,32,1536]{2,1,0:T(8,128)(2,1)S(1)} async-done(((bf16[8,32,1536]{2,1,0:T(8,128)(2,1)}), bf16[8,32,1536]{2,1,0:T(8,128)(2,1)S(1)}, u32[]{:S(2)}, u32[]{:S(2)}) %all-to-all-start) | async-done | bytes 786464 | tf_op jit(solution)/shard_map/all_to_all | solution.py:540
  30.4 5.6 %attend.1 = (bf16[8,32,512]{2,1,0:T(8,128)(2,1)S(1)}, bf16[64,5120]{1,0:T(8,128)(2,1)S(1)}, bf16[64,5120]{1,0:T(8,128)(2,1)S(1)}) custom-call(s32[9]{0:T(128)S(1)} %pad_add_fusion.control_ref, bf16[256,1536]{1,0:T(8,128)(2,1)S(1)} %bitcast.13, s32[256,1]{1,0:T(8,128)S(1)} %copy.27.col_ref, s32[1,256]{1,0:T(1,128)S(1)} %bitcast.24, bf16[512,5120]{1,0:T(8,128)(2,1)} %w_ref.4), custom_call_target="tpu_custom_call" | custom-call | bytes 1 | tf_op jit(solution)/shard_map/attend/pallas_call | solution.py:426
  36.0 1.4 collective-permute-start
  37.4 4.4 %out_projection.1 = (bf16[64,5120]{1,0:T(8,128)(2,1)S(1)}, bf16[64,5120]{1,0:T(8,128)(2,1)S(1)}) custom-call(s32[9]{0:T(128)S(1)} %pad_add_fusion.control_ref, bf16[8,32,512]{2,1,0:T(8,128)(2,1)S(1)} %get-tuple-element.82.x_ref, bf16[512,5120]{1,0:T(8,128)(2,1)} %w_ref.4), custom_call_target="tpu_custom_call" | custom-call | bytes 1 | tf_op jit(solution)/shard_map/out_projection/pallas_call | solution.py:103
  41.9 0.7 collective-permute-start.5
  42.6 1.5 collective-permute-start.1
  44.1 2.6 %collective-permute-done.got_ref = bf16[64,5120]{1,0:T(8,128)(2,1)S(1)} collective-permute-done((bf16[64,5120]{1,0:T(8,128)(2,1)S(1)}, bf16[64,5120]{1,0:T(8,128)(2,1)S(1)}, u32[]{:S(2)}, u32[]{:S(2)}) %collective-permute-start) | collective-permute-done | bytes 655392 | tf_op jit(solution)/shard_map/ppermute | solution.py:39
  46.8 3.3 %collective-permute-done.1.refs_1_ = bf16[16,16,640]{2,1,0:T(8,128)(2,1)S(1)} collective-permute-done((bf16[16,16,640]{2,1,0:T(8,128)(2,1)S(1)}, bf16[16,16,640]{2,1,0:T(8,128)(2,1)S(1)}, u32[]{:S(2)}, u32[]{:S(2)}) %collective-permute-start.1) | collective-permute-done | bytes 327712 | tf_op jit(solution)/shard_map/ppermute | solution.py:31
  50.4 6.3 %collective-permute-done.5.got_ref = bf16[64,5120]{1,0:T(8,128)(2,1)S(1)} collective-permute-done((bf16[64,5120]{1,0:T(8,128)(2,1)S(1)}, bf16[64,5120]{1,0:T(8,128)(2,1)S(1)}, u32[]{:S(2)}, u32[]{:S(2)}) %collective-permute-start.5) | collective-permute-done | bytes 655392 | tf_op jit(solution)/shard_map/ppermute | solution.py:39
  57.2 1.3 collective-permute-start.4
  59.2 2.1 %write_pages.1 = (bf16[3,128,512]{2,1,0:T(8,128)(2,1)}, bf16[3,128,512]{2,1,0:T(8,128)(2,1)}) custom-call(s32[3]{0:T(128)S(1)} %broadcast_add_fusion.source_ref, bf16[256,1536]{1,0:T(8,128)(2,1)S(1)} %bitcast.14, bf16[256,1536]{1,0:T(8,128)(2,1)S(1)} %bitcast.15, bf16[3,128,512]{2,1,0:T(8,128)(2,1)S(1)} %copy-done.4, bf16[3,128,512]{2,1,0:T(8,128)(2,1)S(1)} %copy-done.5), custom_call_target="tpu_custom_call" | custom-call | bytes 8388608 | tf_op jit(solution)/shard_map/write_pages/pallas_call | solution.py:471
  61.3 3.4 %collective-permute-done.6.got_ref = bf16[32,5120]{1,0:T(8,128)(2,1)S(1)} collective-permute-done((bf16[32,5120]{1,0:T(8,128)(2,1)S(1)}, bf16[32,5120]{1,0:T(8,128)(2,1)S(1)}, u32[]{:S(2)}, u32[]{:S(2)}) %collective-permute-start.6) | collective-permute-done | bytes 327712 | tf_op jit(solution)/shard_map/ppermute | solution.py:39
  64.8 3.1 %collective-permute-done.4.b_ref = bf16[16,5120]{1,0:T(8,128)(2,1)S(1)} collective-permute-done((bf16[16,5120]{1,0:T(8,128)(2,1)S(1)}, bf16[16,5120]{1,0:T(8,128)(2,1)S(1)}, u32[]{:S(2)}, u32[]{:S(2)}) %collective-permute-start.4) | collective-permute-done | bytes 163872 | tf_op jit(solution)/shard_map/ppermute | solution.py:39
  68.6 9.7 %collective-permute-done.12 = bf16[16,5120]{1,0:T(8,128)(2,1)S(1)} collective-permute-done((bf16[16,5120]{1,0:T(8,128)(2,1)S(1)}, bf16[16,5120]{1,0:T(8,128)(2,1)S(1)}, u32[]{:S(2)}, u32[]{:S(2)}) %collective-permute-start.12) | collective-permute-done | bytes 163872 | tf_op jit(solution)/shard_map/ppermute | solution.py:39
  78.3 0.6 collective-permute-start.13
  78.9 3.7 %pick.1 = (bf16[256,640]{1,0:T(8,128)(2,1)S(1)}, bf16[256,1728]{1,0:T(8,128)(2,1)S(1)}) custom-call(s32[16]{0:T(128)S(1)} %select_reduce_fusion.at_ref, bf16[16,16,640]{2,1,0:T(8,128)(2,1)S(1)} %bitcast.18, bf16[16,16,640]{2,1,0:T(8,128)(2,1)S(1)} %collective-permute-done.1.refs_1_, bf16[16,16,640]{2,1,0:T(8,128)(2,1)S(1)} %collective-permute-done.8.refs_2_, ...), custom_call_target="tpu_custom_call" | custom-call | bytes 8388608 | tf_op jit(solution)/shard_map/pick/pallas_call | solution.py:351
  82.7 4.5 %collective-permute-done.7.b_ref = bf16[16,5120]{1,0:T(8,128)(2,1)S(1)} collective-permute-done((bf16[16,5120]{1,0:T(8,128)(2,1)S(1)}, bf16[16,5120]{1,0:T(8,128)(2,1)S(1)}, u32[]{:S(2)}, u32[]{:S(2)}) %collective-permute-start.7) | collective-permute-done | bytes 163872 | tf_op jit(solution)/shard_map/ppermute | solution.py:39
  87.6 1.2 collective-permute-done.13
  88.8 1.5 collective-permute-start.14
  90.3 5.6 %collective-permute-done.15 = bf16[16,5120]{1,0:T(8,128)(2,1)S(1)} collective-permute-done((bf16[16,5120]{1,0:T(8,128)(2,1)S(1)}, bf16[16,5120]{1,0:T(8,128)(2,1)S(1)}, u32[]{:S(2)}, u32[]{:S(2)}) %collective-permute-start.15) | collective-permute-done | bytes 163872 | tf_op jit(solution)/shard_map/ppermute | solution.py:39
  96.1 7.8 %collective-permute-done.16 = bf16[32,5120]{1,0:T(8,128)(2,1)S(1)} collective-permute-done((bf16[32,5120]{1,0:T(8,128)(2,1)S(1)}, bf16[32,5120]{1,0:T(8,128)(2,1)S(1)}, u32[]{:S(2)}, u32[]{:S(2)}) %collective-permute-start.16) | collective-permute-done | bytes 327712 | tf_op jit(solution)/shard_map/ppermute | solution.py:39
  103.9 1.2 collective-permute-start.17
  105.4 0.8 down_products.2
  106.2 5.5 %feedfwd_in.3.refs_5_ = f32[128,1728]{1,0:T(8,128)S(1)} custom-call(bf16[64,5120]{1,0:T(8,128)(2,1)S(1)} %pad_maximum_fusion.a_ref.refs_0_, bf16[64,5120]{1,0:T(8,128)(2,1)S(1)} %collective-permute-done.14.b_ref.refs_1_, bf16[1728,5120]{1,0:T(8,128)(2,1)} %bitcast.25), custom_call_target="tpu_custom_call" | custom-call | flops 1132462080 | bytes 8847360 | tf_op jit(solution)/shard_map/feedfwd_in/pallas_call | solution.py:199
  111.8 2.8 %collective-permute-done.17.b_ref.refs_1_.refs_3_ = bf16[64,5120]{1,0:T(8,128)(2,1)S(1)} collective-permute-done((bf16[64,5120]{1,0:T(8,128)(2,1)S(1)}, bf16[64,5120]{1,0:T(8,128)(2,1)S(1)}, u32[]{:S(2)}, u32[]{:S(2)}) %collective-permute-start.17) | collective-permute-done | bytes 655392 | tf_op jit(solution)/shard_map/ppermute | solution.py:39
  114.6 0.8 down_products.3
  115.4 1.2 collective-permute-start.18
  116.6 5.6 %feedfwd_in.4.refs_6_ = f32[128,1728]{1,0:T(8,128)S(1)} custom-call(bf16[64,5120]{1,0:T(8,128)(2,1)S(1)} %constant_dynamic-update-slice_fusion.2.a_ref.refs_0_.refs_2_, bf16[64,5120]{1,0:T(8,128)(2,1)S(1)} %collective-permute-done.17.b_ref.refs_1_.refs_3_, bf16[1728,5120]{1,0:T(8,128)(2,1)} %bitcast.26), custom_call_target="tpu_custom_call" | custom-call | flops 1132462080 | bytes 8847360 | tf_op jit(solution)/shard_map/feedfwd_in/pallas_call | solution.py:199
  122.3 0.7 collective-permute-start.21
  122.9 3.8 %collective-permute-start.20 = (f32[16,256]{1,0:T(8,128)S(1)}, f32[16,256]{1,0:T(8,128)S(1)}, u32[]{:S(2)}, u32[]{:S(2)}) collective-permute-start(f32[16,256]{1,0:T(8,128)S(1)} %fusion.3), channel_id=1, source_target_pairs={{0,4},{1,5},{2,6},{3,7},{4,0},{5,1},{6,2},{7,3},{8,12},{9,13},{10,... | collective-permute-start | bytes 49160 | tf_op jit(solution)/shard_map/ppermute | solution.py:31
  126.7 5.5 %feedfwd_in.5 = (f32[128,1728]{1,0:T(8,128)S(1)}, f32[128,1728]{1,0:T(8,128)S(1)}) custom-call(bf16[64,5120]{1,0:T(8,128)(2,1)S(1)} %pad_maximum_fusion.a_ref.refs_0_, bf16[64,5120]{1,0:T(8,128)(2,1)S(1)} %collective-permute-done.14.b_ref.refs_1_, bf16[64,5120]{1,0:T(8,128)(2,1)S(1)} %constant_dynamic-update-slice_fusion.2.a_ref.refs_0_.refs_2_, ...), custom_call_target="tpu_custom_call" | custom-call | flops 2264924160 | bytes 8847360 | tf_op jit(solution)/shard_map/feedfwd_in/pallas_call | solution.py:199
  132.3 5.8 %feedfwd_out_first.1 = (bf16[256,1728]{1,0:T(8,128)(2,1)S(1)}, bf16[128,3072]{1,0:T(8,128)(2,1)S(1)}, bf16[128,3072]{1,0:T(8,128)(2,1)S(1)}) custom-call(s32[9]{0:T(128)S(1)} %pad_add_fusion.control_ref, f32[128,1728]{1,0:T(8,128)S(1)} %get-tuple-element.120.refs_0_, f32[128,1728]{1,0:T(8,128)S(1)} %get-tuple-element.121.refs_1_, ...), custom_call_target="tpu_custom_call" | custom-call | bytes 1 | tf_op jit(solution)/shard_map/feedfwd_out_first/pallas_call | solution.py:306
  138.2 1.0 collective-permute-start.22
  139.1 2.8 %feedfwd_out.1 = (bf16[128,2048]{1,0:T(8,128)(2,1)S(1)}, bf16[128,2048]{1,0:T(8,128)(2,1)S(1)}) custom-call(bf16[256,1728]{1,0:T(8,128)(2,1)S(1)} %get-tuple-element.128.x_ref, bf16[1728,5120]{1,0:T(8,128)(2,1)S(1)} %bitcast.12), custom_call_target="tpu_custom_call" | custom-call | bytes 1 | tf_op jit(solution)/shard_map/feedfwd_out/pallas_call | solution.py:132
  141.9 8.6 %collective-permute-done.22.got_ref = bf16[128,3072]{1,0:T(8,128)(2,1)S(1)} collective-permute-done((bf16[128,3072]{1,0:T(8,128)(2,1)S(1)}, bf16[128,3072]{1,0:T(8,128)(2,1)S(1)}, u32[]{:S(2)}, u32[]{:S(2)}) %collective-permute-start.22) | collective-permute-done | bytes 786464 | tf_op jit(solution)/shard_map/ppermute | solution.py:39
  150.7 1.3 collective-permute-start.24
  152.0 9.0 %collective-permute-done.23.got_ref = bf16[64,3072]{1,0:T(8,128)(2,1)S(1)} collective-permute-done((bf16[64,3072]{1,0:T(8,128)(2,1)S(1)}, bf16[64,3072]{1,0:T(8,128)(2,1)S(1)}, u32[]{:S(2)}, u32[]{:S(2)}) %collective-permute-start.23) | collective-permute-done | bytes 393248 | tf_op jit(solution)/shard_map/ppermute | solution.py:39
  161.1 0.6 collective-permute-done.24.got_ref
  161.9 0.6 collective-permute-start.26
  162.5 1.2 collective-permute-start.25
  163.6 5.9 %collective-permute-done.26.got_ref = bf16[64,2048]{1,0:T(8,128)(2,1)S(1)} collective-permute-done((bf16[64,2048]{1,0:T(8,128)(2,1)S(1)}, bf16[64,2048]{1,0:T(8,128)(2,1)S(1)}, u32[]{:S(2)}, u32[]{:S(2)}) %collective-permute-start.26) | collective-permute-done | bytes 262176 | tf_op jit(solution)/shard_map/ppermute | solution.py:39
  169.6 1.1 collective-permute-start.27
  170.7 2.6 %collective-permute-done.25 = bf16[32,3072]{1,0:T(8,128)(2,1)S(1)} collective-permute-done((bf16[32,3072]{1,0:T(8,128)(2,1)S(1)}, bf16[32,3072]{1,0:T(8,128)(2,1)S(1)}, u32[]{:S(2)}, u32[]{:S(2)}) %collective-permute-start.25) | collective-permute-done | bytes 196640 | tf_op jit(solution)/shard_map/ppermute | solution.py:39
  173.3 3.6 %collective-permute-done.27 = bf16[32,2048]{1,0:T(8,128)(2,1)S(1)} collective-permute-done((bf16[32,2048]{1,0:T(8,128)(2,1)S(1)}, bf16[32,2048]{1,0:T(8,128)(2,1)S(1)}, u32[]{:S(2)}, u32[]{:S(2)}) %collective-permute-start.27) | collective-permute-done | bytes 131104 | tf_op jit(solution)/shard_map/ppermute | solution.py:39
  177.0 0.8 fusion
  (111 shorter events, 5.0 us)
Async XLA Ops:
  0.6 11.3 %copy-start.17 = (s32[4]{0:T(128)S(1)}, s32[4]{0:T(128)}, u32[]{:S(2)}) copy-start(s32[4]{0:T(128)} %constant.39.clone) | copy-start | bytes 52
  0.6 11.3 %copy-start.12 = (s32[8]{0:T(128)S(1)}, s32[8]{0:T(128)}, u32[]{:S(2)}) copy-start(s32[8]{0:T(128)} %constant.37.clone) | copy-start | bytes 100
  0.7 11.3 %copy-start.13 = (s32[8]{0:T(128)S(1)}, s32[8]{0:T(128)}, u32[]{:S(2)}) copy-start(s32[8]{0:T(128)} %constant.38.clone) | copy-start | bytes 100
  0.7 9.4 %copy-start.1 = (bf16[16,16,1728]{2,1,0:T(8,128)(2,1)S(1)}, bf16[16,16,1728]{2,1,0:T(8,128)(2,1)}, u32[]{:S(2)}) copy-start(bf16[16,16,1728]{2,1,0:T(8,128)(2,1)} %refs_4_) | copy-start | bytes 2654212
  0.7 11.0 %copy-start.11 = (s32[1,16]{1,0:T(1,128)S(1)}, s32[1,16]{1,0:T(1,128)}, u32[]{:S(2)}) copy-start(s32[1,16]{1,0:T(1,128)} %param.33) | copy-start | bytes 196
  0.7 11.6 %copy-start.14 = (s32[64]{0:T(128)S(1)}, s32[64]{0:T(128)}, u32[]{:S(2)}) copy-start(s32[64]{0:T(128)} %param.36) | copy-start | bytes 772
  0.7 11.6 %copy-start.15 = (s32[1,16]{1,0:T(1,128)S(1)}, s32[1,16]{1,0:T(1,128)}, u32[]{:S(2)}) copy-start(s32[1,16]{1,0:T(1,128)} %param.35) | copy-start | bytes 196
  2.8 27.5 %all-to-all-start = ((bf16[8,32,1536]{2,1,0:T(8,128)(2,1)}), bf16[8,32,1536]{2,1,0:T(8,128)(2,1)S(1)}, u32[]{:S(2)}, u32[]{:S(2)}) async-start(bf16[8,32,1536]{2,1,0:T(8,128)(2,1)} %join.1), calls=%async_computation | async-start | bytes 1572864 | tf_op jit(solution)/shard_map/all_to_all | solution.py:540
  10.1 40.0 %collective-permute-start.2 = (bf16[16,16,1728]{2,1,0:T(8,128)(2,1)S(1)}, bf16[16,16,1728]{2,1,0:T(8,128)(2,1)S(1)}, u32[]{:S(2)}, u32[]{:S(2)}) collective-permute-start(bf16[16,16,1728]{2,1,0:T(8,128)(2,1)S(1)} %copy-done.1), channel_id=1, source_target_pairs={{0,16},{8,24},{16,0},{24,8},{1,17},{9,25},{17,1},{25,9},{2,18},{10... | collective-permute-start | bytes 2654216 | tf_op jit(solution)/shard_map/ppermute | solution.py:31
  36.0 10.7 %collective-permute-start = (bf16[64,5120]{1,0:T(8,128)(2,1)S(1)}, bf16[64,5120]{1,0:T(8,128)(2,1)S(1)}, u32[]{:S(2)}, u32[]{:S(2)}) collective-permute-start(bf16[64,5120]{1,0:T(8,128)(2,1)S(1)} %get-tuple-element.79), channel_id=1, source_target_pairs={{0,1},{1,0},{2,3},{3,2},{4,5},{5,4},{6,7},{7,6},{8,10},{9,11},{10,... | collective-permute-start | bytes 1966088 | tf_op jit(solution)/shard_map/ppermute | solution.py:39
  41.9 14.9 %collective-permute-start.5 = (bf16[64,5120]{1,0:T(8,128)(2,1)S(1)}, bf16[64,5120]{1,0:T(8,128)(2,1)S(1)}, u32[]{:S(2)}, u32[]{:S(2)}) collective-permute-start(bf16[64,5120]{1,0:T(8,128)(2,1)S(1)} %get-tuple-element.84), channel_id=1, source_target_pairs={{0,1},{1,0},{2,3},{3,2},{4,5},{5,4},{6,7},{7,6},{8,10},{9,11},{10,... | collective-permute-start | bytes 1966088 | tf_op jit(solution)/shard_map/ppermute | solution.py:39
  42.6 7.5 %collective-permute-start.1 = (bf16[16,16,640]{2,1,0:T(8,128)(2,1)S(1)}, bf16[16,16,640]{2,1,0:T(8,128)(2,1)S(1)}, u32[]{:S(2)}, u32[]{:S(2)}) collective-permute-start(bf16[16,16,640]{2,1,0:T(8,128)(2,1)S(1)} %bitcast.16), channel_id=1, source_target_pairs={{0,16},{8,24},{16,0},{24,8},{1,17},{9,25},{17,1},{25,9},{2,18},{10... | collective-permute-start | bytes 983048 | tf_op jit(solution)/shard_map/ppermute | solution.py:31
  46.6 10.3 %copy-start.16 = (s32[1,2]{1,0:T(1,128)S(1)}, s32[1,2]{1,0:T(1,128)}, u32[]{:S(2)}) copy-start(s32[1,2]{1,0:T(1,128)} %param.34) | copy-start | bytes 28
  46.8 12.4 %copy-start.4 = (bf16[3,128,512]{2,1,0:T(8,128)(2,1)S(1)}, bf16[3,128,512]{2,1,0:T(8,128)(2,1)}, u32[]{:S(2)}) copy-start(bf16[3,128,512]{2,1,0:T(8,128)(2,1)} %key_cache_ref.1) | copy-start | bytes 1179652
  46.8 12.4 %copy-start.5 = (bf16[3,128,512]{2,1,0:T(8,128)(2,1)S(1)}, bf16[3,128,512]{2,1,0:T(8,128)(2,1)}, u32[]{:S(2)}) copy-start(bf16[3,128,512]{2,1,0:T(8,128)(2,1)} %value_cache_ref.1) | copy-start | bytes 1179652
  50.1 7.1 %collective-permute-start.3 = (bf16[32,5120]{1,0:T(8,128)(2,1)S(1)}, bf16[32,5120]{1,0:T(8,128)(2,1)S(1)}, u32[]{:S(2)}, u32[]{:S(2)}) collective-permute-start(bf16[32,5120]{1,0:T(8,128)(2,1)S(1)} %get-tuple-element.86), channel_id=1, source_target_pairs={{0,2},{1,3},{2,0},{3,1},{4,6},{5,7},{6,4},{7,5},{8,9},{9,8},{10,11... | collective-permute-start | bytes 983048 | tf_op jit(solution)/shard_map/ppermute | solution.py:39
  56.9 7.8 %collective-permute-start.6 = (bf16[32,5120]{1,0:T(8,128)(2,1)S(1)}, bf16[32,5120]{1,0:T(8,128)(2,1)S(1)}, u32[]{:S(2)}, u32[]{:S(2)}) collective-permute-start(bf16[32,5120]{1,0:T(8,128)(2,1)S(1)} %get-tuple-element.90), channel_id=1, source_target_pairs={{0,2},{1,3},{2,0},{3,1},{4,6},{5,7},{6,4},{7,5},{8,9},{9,8},{10,11... | collective-permute-start | bytes 983048 | tf_op jit(solution)/shard_map/ppermute | solution.py:39
  57.2 10.6 %collective-permute-start.4 = (bf16[16,5120]{1,0:T(8,128)(2,1)S(1)}, bf16[16,5120]{1,0:T(8,128)(2,1)S(1)}, u32[]{:S(2)}, u32[]{:S(2)}) collective-permute-start(bf16[16,5120]{1,0:T(8,128)(2,1)S(1)} %get-tuple-element.88), channel_id=1, source_target_pairs={{0,4},{1,5},{2,6},{3,7},{4,0},{5,1},{6,2},{7,3},{8,12},{9,13},{10,... | collective-permute-start | bytes 491528 | tf_op jit(solution)/shard_map/ppermute | solution.py:39
  58.5 9.3 %copy-start.10 = (f32[5120]{0:T(1024)S(1)}, f32[5120]{0:T(1024)}, u32[]{:S(2)}) copy-start(f32[5120]{0:T(1024)} %param.28) | copy-start | bytes 61444
  58.5 19.7 %collective-permute-start.8 = (bf16[16,16,640]{2,1,0:T(8,128)(2,1)S(1)}, bf16[16,16,640]{2,1,0:T(8,128)(2,1)S(1)}, u32[]{:S(2)}, u32[]{:S(2)}) collective-permute-start(bf16[16,16,640]{2,1,0:T(8,128)(2,1)S(1)} %bitcast.17), channel_id=1, source_target_pairs={{0,8},{8,0},{16,24},{24,16},{1,9},{9,1},{17,25},{25,17},{2,10},{10... | collective-permute-start | bytes 983048 | tf_op jit(solution)/shard_map/ppermute | solution.py:31
  58.6 20.3 %collective-permute-start.9 = (bf16[16,16,640]{2,1,0:T(8,128)(2,1)S(1)}, bf16[16,16,640]{2,1,0:T(8,128)(2,1)S(1)}, u32[]{:S(2)}, u32[]{:S(2)}) collective-permute-start(bf16[16,16,640]{2,1,0:T(8,128)(2,1)S(1)} %collective-permute-done.1.refs_1_), channel_id=1, source_target_pairs={{0,8},{8,0},{16,24},{24,16},{1,9},{9,1},{17,25},{25,17},{2,10},{10... | collective-permute-start | bytes 983048 | tf_op jit(solution)/shard_map/ppermute | solution.py:31
  59.1 19.8 %collective-permute-start.10 = (bf16[16,16,1728]{2,1,0:T(8,128)(2,1)S(1)}, bf16[16,16,1728]{2,1,0:T(8,128)(2,1)S(1)}, u32[]{:S(2)}, u32[]{:S(2)}) collective-permute-start(bf16[16,16,1728]{2,1,0:T(8,128)(2,1)S(1)} %copy-done.1), channel_id=1, source_target_pairs={{0,8},{8,0},{16,24},{24,16},{1,9},{9,1},{17,25},{25,17},{2,10},{10... | collective-permute-start | bytes 2654216 | tf_op jit(solution)/shard_map/ppermute | solution.py:31
  64.7 14.2 %collective-permute-start.11 = (bf16[16,16,1728]{2,1,0:T(8,128)(2,1)S(1)}, bf16[16,16,1728]{2,1,0:T(8,128)(2,1)S(1)}, u32[]{:S(2)}, u32[]{:S(2)}) collective-permute-start(bf16[16,16,1728]{2,1,0:T(8,128)(2,1)S(1)} %collective-permute-done.2.refs_5_), channel_id=1, source_target_pairs={{0,8},{8,0},{16,24},{24,16},{1,9},{9,1},{17,25},{25,17},{2,10},{10... | collective-permute-start | bytes 2654216 | tf_op jit(solution)/shard_map/ppermute | solution.py:31
  68.2 10.1 %collective-permute-start.12 = (bf16[16,5120]{1,0:T(8,128)(2,1)S(1)}, bf16[16,5120]{1,0:T(8,128)(2,1)S(1)}, u32[]{:S(2)}, u32[]{:S(2)}) collective-permute-start(bf16[16,5120]{1,0:T(8,128)(2,1)S(1)} %get-tuple-element.106), channel_id=1, source_target_pairs={{0,4},{1,5},{2,6},{3,7},{4,0},{5,1},{6,2},{7,3},{8,12},{9,13},{10,... | collective-permute-start | bytes 491528 | tf_op jit(solution)/shard_map/ppermute | solution.py:39
  78.3 8.9 %collective-permute-start.7 = (bf16[16,5120]{1,0:T(8,128)(2,1)S(1)}, bf16[16,5120]{1,0:T(8,128)(2,1)S(1)}, u32[]{:S(2)}, u32[]{:S(2)}) collective-permute-start(bf16[16,5120]{1,0:T(8,128)(2,1)S(1)} %get-tuple-element.95), channel_id=1, source_target_pairs={{0,4},{1,5},{2,6},{3,7},{4,0},{5,1},{6,2},{7,3},{8,12},{9,13},{10,... | collective-permute-start | bytes 491528 | tf_op jit(solution)/shard_map/ppermute | solution.py:39
  78.3 10.5 %collective-permute-start.13 = (bf16[32,5120]{1,0:T(8,128)(2,1)S(1)}, bf16[32,5120]{1,0:T(8,128)(2,1)S(1)}, u32[]{:S(2)}, u32[]{:S(2)}) collective-permute-start(bf16[32,5120]{1,0:T(8,128)(2,1)S(1)} %constant_dynamic-update-slice_fusion), channel_id=1, source_target_pairs={{0,2},{1,3},{2,0},{3,1},{4,6},{5,7},{6,4},{7,5},{8,9},{9,8},{10,11... | collective-permute-start | bytes 983048 | tf_op jit(solution)/shard_map/ppermute | solution.py:39
  82.7 13.3 %copy-start.2 = (bf16[256,1728]{1,0:T(8,128)(2,1)}, bf16[256,1728]{1,0:T(8,128)(2,1)S(1)}, u32[]{:S(2)}) copy-start(bf16[256,1728]{1,0:T(8,128)(2,1)S(1)} %get-tuple-element.123.refs_5_) | copy-start | bytes 2654212
  87.5 8.4 %collective-permute-start.15 = (bf16[16,5120]{1,0:T(8,128)(2,1)S(1)}, bf16[16,5120]{1,0:T(8,128)(2,1)S(1)}, u32[]{:S(2)}, u32[]{:S(2)}) collective-permute-start(bf16[16,5120]{1,0:T(8,128)(2,1)S(1)} %get-tuple-element.111), channel_id=1, source_target_pairs={{0,4},{1,5},{2,6},{3,7},{4,0},{5,1},{6,2},{7,3},{8,12},{9,13},{10,... | collective-permute-start | bytes 491528 | tf_op jit(solution)/shard_map/ppermute | solution.py:39
  88.8 15.1 %collective-permute-start.14 = (bf16[64,5120]{1,0:T(8,128)(2,1)S(1)}, bf16[64,5120]{1,0:T(8,128)(2,1)S(1)}, u32[]{:S(2)}, u32[]{:S(2)}) collective-permute-start(bf16[64,5120]{1,0:T(8,128)(2,1)S(1)} %pad_maximum_fusion.a_ref.refs_0_), channel_id=1, source_target_pairs={{0,1},{1,0},{2,3},{3,2},{4,5},{5,4},{6,7},{7,6},{8,10},{9,11},{10,... | collective-permute-start | bytes 1966088 | tf_op jit(solution)/shard_map/ppermute | solution.py:39
  96.0 7.9 %collective-permute-start.16 = (bf16[32,5120]{1,0:T(8,128)(2,1)S(1)}, bf16[32,5120]{1,0:T(8,128)(2,1)S(1)}, u32[]{:S(2)}, u32[]{:S(2)}) collective-permute-start(bf16[32,5120]{1,0:T(8,128)(2,1)S(1)} %pad_maximum_fusion.1), channel_id=1, source_target_pairs={{0,2},{1,3},{2,0},{3,1},{4,6},{5,7},{6,4},{7,5},{8,9},{9,8},{10,11... | collective-permute-start | bytes 983048 | tf_op jit(solution)/shard_map/ppermute | solution.py:39
  103.9 10.7 %collective-permute-start.17 = (bf16[64,5120]{1,0:T(8,128)(2,1)S(1)}, bf16[64,5120]{1,0:T(8,128)(2,1)S(1)}, u32[]{:S(2)}, u32[]{:S(2)}) collective-permute-start(bf16[64,5120]{1,0:T(8,128)(2,1)S(1)} %constant_dynamic-update-slice_fusion.2.a_ref.refs_0_.refs_2_), channel_id=1, source_target_pairs={{0,1},{1,0},{2,3},{3,2},{4,5},{5,4},{6,7},{7,6},{8,10},{9,11},{10,... | collective-permute-start | bytes 1966088 | tf_op jit(solution)/shard_map/ppermute | solution.py:39
  115.4 6.8 %collective-permute-start.18 = (f32[16,256]{1,0:T(8,128)S(1)}, f32[16,256]{1,0:T(8,128)S(1)}, u32[]{:S(2)}, u32[]{:S(2)}) collective-permute-start(f32[16,256]{1,0:T(8,128)S(1)} %pad_maximum_fusion.2), channel_id=1, source_target_pairs={{0,1},{1,0},{2,3},{3,2},{4,5},{5,4},{6,7},{7,6},{8,9},{9,8},{10,11... | collective-permute-start | bytes 49160 | tf_op jit(solution)/shard_map/ppermute | solution.py:31
  116.6 15.6 %slice-start = ((s8[17694720]{0:T(1024)(128)(4,1)}), s8[4194304]{0:T(1024)(128)(4,1)S(1)}, s32[]{:S(2)}) async-start(s8[17694720]{0:T(1024)(128)(4,1)} %bitcast.11), calls=%async_computation.1 | async-start | bytes 8388608
  116.6 15.7 %slice-start.1 = ((s8[17694720]{0:T(1024)(128)(4,1)}), s8[4194304]{0:T(1024)(128)(4,1)S(1)}, s32[]{:S(2)}) async-start(s8[17694720]{0:T(1024)(128)(4,1)} %bitcast.11), calls=%async_computation.2 | async-start | bytes 8388608
  116.6 15.7 %slice-start.2 = ((s8[17694720]{0:T(1024)(128)(4,1)}), s8[4194304]{0:T(1024)(128)(4,1)S(1)}, s32[]{:S(2)}) async-start(s8[17694720]{0:T(1024)(128)(4,1)} %bitcast.11), calls=%async_computation.3 | async-start | bytes 8388608
  122.2 10.1 %slice-start.3 = ((s8[17694720]{0:T(1024)(128)(4,1)}), s8[4194304]{0:T(1024)(128)(4,1)S(1)}, s32[]{:S(2)}) async-start(s8[17694720]{0:T(1024)(128)(4,1)} %bitcast.11), calls=%async_computation.4 | async-start | bytes 8388608
  122.3 10.0 %slice-start.4 = ((s8[17694720]{0:T(1024)(128)(4,1)}), s8[917504]{0:T(1024)(128)(4,1)S(1)}, s32[]{:S(2)}) async-start(s8[17694720]{0:T(1024)(128)(4,1)} %bitcast.11), calls=%async_computation.5 | async-start | bytes 1835008
  122.3 10.0 %copy-start.3 = (bf16[256,1728]{1,0:T(8,128)(2,1)S(1)}, bf16[256,1728]{1,0:T(8,128)(2,1)}, u32[]{:S(2)}) copy-start(bf16[256,1728]{1,0:T(8,128)(2,1)} %copy-done.2) | copy-start | bytes 2654212
  122.3 9.9 %collective-permute-start.21 = (f32[16,256]{1,0:T(8,128)S(1)}, f32[16,256]{1,0:T(8,128)S(1)}, u32[]{:S(2)}, u32[]{:S(2)}) collective-permute-start(f32[16,256]{1,0:T(8,128)S(1)} %fusion.3), channel_id=1, source_target_pairs={{0,6},{1,7},{2,4},{3,5},{4,2},{5,3},{6,0},{7,1},{8,14},{9,15},{10,... | collective-permute-start | bytes 49160 | tf_op jit(solution)/shard_map/ppermute | solution.py:31
  122.9 9.3 %collective-permute-start.19 = (f32[16,256]{1,0:T(8,128)S(1)}, f32[16,256]{1,0:T(8,128)S(1)}, u32[]{:S(2)}, u32[]{:S(2)}) collective-permute-start(f32[16,256]{1,0:T(8,128)S(1)} %fusion.3), channel_id=1, source_target_pairs={{0,2},{1,3},{2,0},{3,1},{4,6},{5,7},{6,4},{7,5},{8,10},{9,11},{10,... | collective-permute-start | bytes 49160 | tf_op jit(solution)/shard_map/ppermute | solution.py:31
  122.9 9.3 %collective-permute-start.20 = (f32[16,256]{1,0:T(8,128)S(1)}, f32[16,256]{1,0:T(8,128)S(1)}, u32[]{:S(2)}, u32[]{:S(2)}) collective-permute-start(f32[16,256]{1,0:T(8,128)S(1)} %fusion.3), channel_id=1, source_target_pairs={{0,4},{1,5},{2,6},{3,7},{4,0},{5,1},{6,2},{7,3},{8,12},{9,13},{10,... | collective-permute-start | bytes 49160 | tf_op jit(solution)/shard_map/ppermute | solution.py:31
  138.2 12.4 %collective-permute-start.22 = (bf16[128,3072]{1,0:T(8,128)(2,1)S(1)}, bf16[128,3072]{1,0:T(8,128)(2,1)S(1)}, u32[]{:S(2)}, u32[]{:S(2)}) collective-permute-start(bf16[128,3072]{1,0:T(8,128)(2,1)S(1)} %get-tuple-element.125), channel_id=1, source_target_pairs={{0,1},{1,0},{2,3},{3,2},{4,5},{5,4},{6,7},{7,6},{8,10},{9,11},{10,... | collective-permute-start | bytes 2359304 | tf_op jit(solution)/shard_map/ppermute | solution.py:39
  150.7 11.0 %collective-permute-start.24 = (bf16[128,2048]{1,0:T(8,128)(2,1)S(1)}, bf16[128,2048]{1,0:T(8,128)(2,1)S(1)}, u32[]{:S(2)}, u32[]{:S(2)}) collective-permute-start(bf16[128,2048]{1,0:T(8,128)(2,1)S(1)} %get-tuple-element.136), channel_id=1, source_target_pairs={{0,1},{1,0},{2,3},{3,2},{4,5},{5,4},{6,7},{7,6},{8,10},{9,11},{10,... | collective-permute-start | bytes 1572872 | tf_op jit(solution)/shard_map/ppermute | solution.py:39
  152.0 9.0 %collective-permute-start.23 = (bf16[64,3072]{1,0:T(8,128)(2,1)S(1)}, bf16[64,3072]{1,0:T(8,128)(2,1)S(1)}, u32[]{:S(2)}, u32[]{:S(2)}) collective-permute-start(bf16[64,3072]{1,0:T(8,128)(2,1)S(1)} %get-tuple-element.132), channel_id=1, source_target_pairs={{0,2},{1,3},{2,0},{3,1},{4,6},{5,7},{6,4},{7,5},{8,9},{9,8},{10,11... | collective-permute-start | bytes 1179656 | tf_op jit(solution)/shard_map/ppermute | solution.py:39
  161.9 15.1 %copy-start.8 = (f32[16,5120]{1,0:T(8,128)S(1)}, f32[16,5120]{1,0:T(8,128)}, u32[]{:S(2)}) copy-start(f32[16,5120]{1,0:T(8,128)} %copy-done.7) | copy-start | bytes 983044
  161.9 7.7 %collective-permute-start.26 = (bf16[64,2048]{1,0:T(8,128)(2,1)S(1)}, bf16[64,2048]{1,0:T(8,128)(2,1)S(1)}, u32[]{:S(2)}, u32[]{:S(2)}) collective-permute-start(bf16[64,2048]{1,0:T(8,128)(2,1)S(1)} %get-tuple-element.142), channel_id=1, source_target_pairs={{0,2},{1,3},{2,0},{3,1},{4,6},{5,7},{6,4},{7,5},{8,9},{9,8},{10,11... | collective-permute-start | bytes 786440 | tf_op jit(solution)/shard_map/ppermute | solution.py:39
  162.5 10.8 %collective-permute-start.25 = (bf16[32,3072]{1,0:T(8,128)(2,1)S(1)}, bf16[32,3072]{1,0:T(8,128)(2,1)S(1)}, u32[]{:S(2)}, u32[]{:S(2)}) collective-permute-start(bf16[32,3072]{1,0:T(8,128)(2,1)S(1)} %get-tuple-element.140), channel_id=1, source_target_pairs={{0,4},{1,5},{2,6},{3,7},{4,0},{5,1},{6,2},{7,3},{8,12},{9,13},{10,... | collective-permute-start | bytes 589832 | tf_op jit(solution)/shard_map/ppermute | solution.py:39
  169.6 7.3 %collective-permute-start.27 = (bf16[32,2048]{1,0:T(8,128)(2,1)S(1)}, bf16[32,2048]{1,0:T(8,128)(2,1)S(1)}, u32[]{:S(2)}, u32[]{:S(2)}) collective-permute-start(bf16[32,2048]{1,0:T(8,128)(2,1)S(1)} %get-tuple-element.144), channel_id=1, source_target_pairs={{0,4},{1,5},{2,6},{3,7},{4,0},{5,1},{6,2},{7,3},{8,12},{9,13},{10,... | collective-permute-start | bytes 393224 | tf_op jit(solution)/shard_map/ppermute | solution.py:39
  (4 other events, 32.3 us)

commit v4 on v3

--- a/solution.py
+++ b/solution.py
@@ -598,19 +598,17 @@
     )
     acc = feedfwd_in([rows_a, rows_b], win, 1, acc_a + acc_b)
 
-    wide = width * 3 // 5
-    tile = wide // 3
+    wide = width // 2
+    tile = wide // 2
     activated, *partial_a = feedfwd_out_first(
         control, acc, lowrank, segments, up_flat, feedfwd_out_weight, wide, tile, groups
     )
     partial_b = feedfwd_out(activated, feedfwd_out_weight, wide, width - wide, tile)
     partial_a = reduce_step(*partial_a, steps[0])
-    partial_a, partial_b = tied(partial_a, partial_b)
-    partial_b = reduce_step(*partial_b, steps[0])
+    partial_b = reduce_step(*after(partial_b, partial_a), steps[0])
     for masks in steps[1:-1]:
         partial_a = reduce_step(*partial_a, masks)
-        partial_a, partial_b = tied(partial_a, partial_b)
-        partial_b = reduce_step(*partial_b, masks)
+        partial_b = reduce_step(*after(partial_b, partial_a), masks)
     sums = (
         (partial_a[0], swap(partial_a[1], steps[-1])),
         (partial_b[0], swap(partial_b[1], steps[-1])),

time: 178 us -> 177 us (level)
  no operation moved by 1% of the time
where the time goes in v4:
time: 177 us
  waiting for transfers between devices  97.8 us (55%)
  Pallas kernels  46.1 us (26%)
  starting transfers between devices  29.3 us (17%)
  other arithmetic  1.79 us (1%)
    ppermute x18, waiting for transfers between devices, swap(): return lax.ppermute(x, ('req', 'mlp'), pairs)  76.9 us
    all_to_all x1, waiting for transfers between devices, shards(): lax.all_to_all(join((queries, keys, values), groups), 'mlp', split_axis=0...  17.6 us
    pallas_call x3, Pallas kernels, feedfwd_in(): pl.pallas_call(kernel, grid=(steps,), in_specs=[rows] * (2 * count) + [pl...  16.6 us
    ppermute x18, starting transfers between devices, swap(): return lax.ppermute(x, ('req', 'mlp'), pairs)  12.7 us
    ppermute x10, starting transfers between devices, exchange(): return lax.ppermute(x, axis, [(i, i ^ mask) for i in range(size)])  9.33 us
    all_to_all x1, starting transfers between devices, shards(): lax.all_to_all(join((queries, keys, values), groups), 'mlp', split_axis=0...  7.28 us
    pallas_call x1, Pallas kernels, attend(): pl.pallas_call(kernel, grid_spec=pltpu.PrefetchScalarGridSpec(num_scalar_...  5.58 us
    pallas_call x1, Pallas kernels, feedfwd_out_first(): pl.pallas_call(kernel, grid_spec=pltpu.PrefetchScalarGridSpec(num_scalar_...  5.06 us
  transfers between devices with their start and end apart: 29, of which 19 were waited for; matrix products, arithmetic and copies ran while one was open for 1% of the time, Pallas kernels for 21%

profile of v4, /device:TPU:0, one launch (start us, length us, event | category | flops | bytes accessed | tf_op | source)
XLA Modules:
  0.0 176.9 jit_solution(2592075375334243183)
XLA Ops:
  0.7 2.1 %join.1 = bf16[8,32,1536]{2,1,0:T(8,128)(2,1)} custom-call(bf16[32,4096]{1,0:T(8,128)(2,1)} %refs_0_.1, bf16[32,4096]{1,0:T(8,128)(2,1)} %refs_1_.1, bf16[32,4096]{1,0:T(8,128)(2,1)} %refs_2_.1), custom_call_target="tpu_custom_call" | custom-call | bytes 1 | tf_op jit(solution)/shard_map/join/pallas_call | solution.py:380
  2.8 7.3 %all-to-all-start = ((bf16[8,32,1536]{2,1,0:T(8,128)(2,1)}), bf16[8,32,1536]{2,1,0:T(8,128)(2,1)S(1)}, u32[]{:S(2)}, u32[]{:S(2)}) async-start(bf16[8,32,1536]{2,1,0:T(8,128)(2,1)} %join.1), calls=%async_computation | async-start | bytes 1572864 | tf_op jit(solution)/shard_map/all_to_all | solution.py:540
  10.1 1.6 collective-permute-start.2
  12.6 17.6 %all-to-all-done = bf16[8,32,1536]{2,1,0:T(8,128)(2,1)S(1)} async-done(((bf16[8,32,1536]{2,1,0:T(8,128)(2,1)}), bf16[8,32,1536]{2,1,0:T(8,128)(2,1)S(1)}, u32[]{:S(2)}, u32[]{:S(2)}) %all-to-all-start) | async-done | bytes 786464 | tf_op jit(solution)/shard_map/all_to_all | solution.py:540
  30.4 5.6 %attend.1 = (bf16[8,32,512]{2,1,0:T(8,128)(2,1)S(1)}, bf16[64,5120]{1,0:T(8,128)(2,1)S(1)}, bf16[64,5120]{1,0:T(8,128)(2,1)S(1)}) custom-call(s32[9]{0:T(128)S(1)} %pad_add_fusion.control_ref, bf16[256,1536]{1,0:T(8,128)(2,1)S(1)} %bitcast.13, s32[256,1]{1,0:T(8,128)S(1)} %copy.27.col_ref, s32[1,256]{1,0:T(1,128)S(1)} %bitcast.24, bf16[512,5120]{1,0:T(8,128)(2,1)} %w_ref.4), custom_call_target="tpu_custom_call" | custom-call | bytes 1 | tf_op jit(solution)/shard_map/attend/pallas_call | solution.py:426
  36.0 1.4 collective-permute-start
  37.4 4.4 %out_projection.1 = (bf16[64,5120]{1,0:T(8,128)(2,1)S(1)}, bf16[64,5120]{1,0:T(8,128)(2,1)S(1)}) custom-call(s32[9]{0:T(128)S(1)} %pad_add_fusion.control_ref, bf16[8,32,512]{2,1,0:T(8,128)(2,1)S(1)} %get-tuple-element.78.x_ref, bf16[512,5120]{1,0:T(8,128)(2,1)} %w_ref.4), custom_call_target="tpu_custom_call" | custom-call | bytes 1 | tf_op jit(solution)/shard_map/out_projection/pallas_call | solution.py:103
  41.9 0.7 collective-permute-start.5
  42.6 1.5 collective-permute-start.1
  44.1 2.6 %collective-permute-done.got_ref = bf16[64,5120]{1,0:T(8,128)(2,1)S(1)} collective-permute-done((bf16[64,5120]{1,0:T(8,128)(2,1)S(1)}, bf16[64,5120]{1,0:T(8,128)(2,1)S(1)}, u32[]{:S(2)}, u32[]{:S(2)}) %collective-permute-start) | collective-permute-done | bytes 655392 | tf_op jit(solution)/shard_map/ppermute | solution.py:39
  46.8 3.3 %collective-permute-done.1.refs_1_ = bf16[16,16,640]{2,1,0:T(8,128)(2,1)S(1)} collective-permute-done((bf16[16,16,640]{2,1,0:T(8,128)(2,1)S(1)}, bf16[16,16,640]{2,1,0:T(8,128)(2,1)S(1)}, u32[]{:S(2)}, u32[]{:S(2)}) %collective-permute-start.1) | collective-permute-done | bytes 327712 | tf_op jit(solution)/shard_map/ppermute | solution.py:31
  50.4 6.3 %collective-permute-done.5.got_ref = bf16[64,5120]{1,0:T(8,128)(2,1)S(1)} collective-permute-done((bf16[64,5120]{1,0:T(8,128)(2,1)S(1)}, bf16[64,5120]{1,0:T(8,128)(2,1)S(1)}, u32[]{:S(2)}, u32[]{:S(2)}) %collective-permute-start.5) | collective-permute-done | bytes 655392 | tf_op jit(solution)/shard_map/ppermute | solution.py:39
  57.2 1.3 collective-permute-start.4
  58.6 0.5 collective-permute-start.9
  59.2 2.1 %write_pages.1 = (bf16[3,128,512]{2,1,0:T(8,128)(2,1)}, bf16[3,128,512]{2,1,0:T(8,128)(2,1)}) custom-call(s32[3]{0:T(128)S(1)} %broadcast_add_fusion.source_ref, bf16[256,1536]{1,0:T(8,128)(2,1)S(1)} %bitcast.14, bf16[256,1536]{1,0:T(8,128)(2,1)S(1)} %bitcast.15, bf16[3,128,512]{2,1,0:T(8,128)(2,1)S(1)} %copy-done.4, bf16[3,128,512]{2,1,0:T(8,128)(2,1)S(1)} %copy-done.5), custom_call_target="tpu_custom_call" | custom-call | bytes 8388608 | tf_op jit(solution)/shard_map/write_pages/pallas_call | solution.py:471
  61.3 3.4 %collective-permute-done.6.got_ref = bf16[32,5120]{1,0:T(8,128)(2,1)S(1)} collective-permute-done((bf16[32,5120]{1,0:T(8,128)(2,1)S(1)}, bf16[32,5120]{1,0:T(8,128)(2,1)S(1)}, u32[]{:S(2)}, u32[]{:S(2)}) %collective-permute-start.6) | collective-permute-done | bytes 327712 | tf_op jit(solution)/shard_map/ppermute | solution.py:39
  64.8 3.1 %collective-permute-done.4.b_ref = bf16[16,5120]{1,0:T(8,128)(2,1)S(1)} collective-permute-done((bf16[16,5120]{1,0:T(8,128)(2,1)S(1)}, bf16[16,5120]{1,0:T(8,128)(2,1)S(1)}, u32[]{:S(2)}, u32[]{:S(2)}) %collective-permute-start.4) | collective-permute-done | bytes 163872 | tf_op jit(solution)/shard_map/ppermute | solution.py:39
  68.6 9.7 %collective-permute-done.12 = bf16[16,5120]{1,0:T(8,128)(2,1)S(1)} collective-permute-done((bf16[16,5120]{1,0:T(8,128)(2,1)S(1)}, bf16[16,5120]{1,0:T(8,128)(2,1)S(1)}, u32[]{:S(2)}, u32[]{:S(2)}) %collective-permute-start.12) | collective-permute-done | bytes 163872 | tf_op jit(solution)/shard_map/ppermute | solution.py:39
  78.3 0.6 collective-permute-start.13
  78.9 3.7 %pick.1 = (bf16[256,640]{1,0:T(8,128)(2,1)S(1)}, bf16[256,1728]{1,0:T(8,128)(2,1)S(1)}) custom-call(s32[16]{0:T(128)S(1)} %select_reduce_fusion.at_ref, bf16[16,16,640]{2,1,0:T(8,128)(2,1)S(1)} %bitcast.18, bf16[16,16,640]{2,1,0:T(8,128)(2,1)S(1)} %collective-permute-done.1.refs_1_, bf16[16,16,640]{2,1,0:T(8,128)(2,1)S(1)} %collective-permute-done.8.refs_2_, ...), custom_call_target="tpu_custom_call" | custom-call | bytes 8388608 | tf_op jit(solution)/shard_map/pick/pallas_call | solution.py:351
  82.7 4.5 %collective-permute-done.7.b_ref = bf16[16,5120]{1,0:T(8,128)(2,1)S(1)} collective-permute-done((bf16[16,5120]{1,0:T(8,128)(2,1)S(1)}, bf16[16,5120]{1,0:T(8,128)(2,1)S(1)}, u32[]{:S(2)}, u32[]{:S(2)}) %collective-permute-start.7) | collective-permute-done | bytes 163872 | tf_op jit(solution)/shard_map/ppermute | solution.py:39
  87.6 1.2 collective-permute-done.13
  88.8 1.5 collective-permute-start.14
  90.3 5.6 %collective-permute-done.15 = bf16[16,5120]{1,0:T(8,128)(2,1)S(1)} collective-permute-done((bf16[16,5120]{1,0:T(8,128)(2,1)S(1)}, bf16[16,5120]{1,0:T(8,128)(2,1)S(1)}, u32[]{:S(2)}, u32[]{:S(2)}) %collective-permute-start.15) | collective-permute-done | bytes 163872 | tf_op jit(solution)/shard_map/ppermute | solution.py:39
  96.1 7.8 %collective-permute-done.16 = bf16[32,5120]{1,0:T(8,128)(2,1)S(1)} collective-permute-done((bf16[32,5120]{1,0:T(8,128)(2,1)S(1)}, bf16[32,5120]{1,0:T(8,128)(2,1)S(1)}, u32[]{:S(2)}, u32[]{:S(2)}) %collective-permute-start.16) | collective-permute-done | bytes 327712 | tf_op jit(solution)/shard_map/ppermute | solution.py:39
  103.9 1.2 collective-permute-start.17
  105.4 0.8 down_products.2
  106.2 5.5 %feedfwd_in.3.refs_5_ = f32[128,1728]{1,0:T(8,128)S(1)} custom-call(bf16[64,5120]{1,0:T(8,128)(2,1)S(1)} %pad_maximum_fusion.a_ref.refs_0_, bf16[64,5120]{1,0:T(8,128)(2,1)S(1)} %collective-permute-done.14.b_ref.refs_1_, bf16[1728,5120]{1,0:T(8,128)(2,1)} %bitcast.25), custom_call_target="tpu_custom_call" | custom-call | flops 1132462080 | bytes 8847360 | tf_op jit(solution)/shard_map/feedfwd_in/pallas_call | solution.py:199
  111.8 2.8 %collective-permute-done.17.b_ref.refs_1_.refs_3_ = bf16[64,5120]{1,0:T(8,128)(2,1)S(1)} collective-permute-done((bf16[64,5120]{1,0:T(8,128)(2,1)S(1)}, bf16[64,5120]{1,0:T(8,128)(2,1)S(1)}, u32[]{:S(2)}, u32[]{:S(2)}) %collective-permute-start.17) | collective-permute-done | bytes 655392 | tf_op jit(solution)/shard_map/ppermute | solution.py:39
  114.6 0.8 down_products.3
  115.4 1.2 collective-permute-start.18
  116.6 5.6 %feedfwd_in.4.refs_6_ = f32[128,1728]{1,0:T(8,128)S(1)} custom-call(bf16[64,5120]{1,0:T(8,128)(2,1)S(1)} %constant_dynamic-update-slice_fusion.2.a_ref.refs_0_.refs_2_, bf16[64,5120]{1,0:T(8,128)(2,1)S(1)} %collective-permute-done.17.b_ref.refs_1_.refs_3_, bf16[1728,5120]{1,0:T(8,128)(2,1)} %bitcast.26), custom_call_target="tpu_custom_call" | custom-call | flops 1132462080 | bytes 8847360 | tf_op jit(solution)/shard_map/feedfwd_in/pallas_call | solution.py:199
  122.3 0.7 collective-permute-start.21
  122.9 3.8 %collective-permute-start.20 = (f32[16,256]{1,0:T(8,128)S(1)}, f32[16,256]{1,0:T(8,128)S(1)}, u32[]{:S(2)}, u32[]{:S(2)}) collective-permute-start(f32[16,256]{1,0:T(8,128)S(1)} %fusion.3), channel_id=1, source_target_pairs={{0,4},{1,5},{2,6},{3,7},{4,0},{5,1},{6,2},{7,3},{8,12},{9,13},{10,... | collective-permute-start | bytes 49160 | tf_op jit(solution)/shard_map/ppermute | solution.py:31
  126.7 5.5 %feedfwd_in.5 = (f32[128,1728]{1,0:T(8,128)S(1)}, f32[128,1728]{1,0:T(8,128)S(1)}) custom-call(bf16[64,5120]{1,0:T(8,128)(2,1)S(1)} %pad_maximum_fusion.a_ref.refs_0_, bf16[64,5120]{1,0:T(8,128)(2,1)S(1)} %collective-permute-done.14.b_ref.refs_1_, bf16[64,5120]{1,0:T(8,128)(2,1)S(1)} %constant_dynamic-update-slice_fusion.2.a_ref.refs_0_.refs_2_, ...), custom_call_target="tpu_custom_call" | custom-call | flops 2264924160 | bytes 8847360 | tf_op jit(solution)/shard_map/feedfwd_in/pallas_call | solution.py:199
  132.3 5.1 %feedfwd_out_first.1 = (bf16[256,1728]{1,0:T(8,128)(2,1)S(1)}, bf16[128,2560]{1,0:T(8,128)(2,1)S(1)}, bf16[128,2560]{1,0:T(8,128)(2,1)S(1)}) custom-call(s32[9]{0:T(128)S(1)} %pad_add_fusion.control_ref, f32[128,1728]{1,0:T(8,128)S(1)} %get-tuple-element.116.refs_0_, f32[128,1728]{1,0:T(8,128)S(1)} %get-tuple-element.117.refs_1_, ...), custom_call_target="tpu_custom_call" | custom-call | bytes 1 | tf_op jit(solution)/shard_map/feedfwd_out_first/pallas_call | solution.py:306
  137.4 1.0 collective-permute-start.22
  138.4 3.4 %feedfwd_out.1 = (bf16[128,2560]{1,0:T(8,128)(2,1)S(1)}, bf16[128,2560]{1,0:T(8,128)(2,1)S(1)}) custom-call(bf16[256,1728]{1,0:T(8,128)(2,1)S(1)} %get-tuple-element.126.x_ref, bf16[1728,5120]{1,0:T(8,128)(2,1)S(1)} %bitcast.12), custom_call_target="tpu_custom_call" | custom-call | bytes 1 | tf_op jit(solution)/shard_map/feedfwd_out/pallas_call | solution.py:132
  141.8 6.6 %collective-permute-done.22.got_ref = bf16[128,2560]{1,0:T(8,128)(2,1)S(1)} collective-permute-done((bf16[128,2560]{1,0:T(8,128)(2,1)S(1)}, bf16[128,2560]{1,0:T(8,128)(2,1)S(1)}, u32[]{:S(2)}, u32[]{:S(2)}) %collective-permute-start.22) | collective-permute-done | bytes 655392 | tf_op jit(solution)/shard_map/ppermute | solution.py:39
  148.6 1.3 collective-permute-start.25
  149.9 8.2 %collective-permute-done.23.got_ref = bf16[64,2560]{1,0:T(8,128)(2,1)S(1)} collective-permute-done((bf16[64,2560]{1,0:T(8,128)(2,1)S(1)}, bf16[64,2560]{1,0:T(8,128)(2,1)S(1)}, u32[]{:S(2)}, u32[]{:S(2)}) %collective-permute-start.23) | collective-permute-done | bytes 327712 | tf_op jit(solution)/shard_map/ppermute | solution.py:39
  158.2 1.6 collective-permute-done.25.got_ref
  160.0 0.7 collective-permute-start.26
  160.7 7.3 %collective-permute-done.26.got_ref = bf16[64,2560]{1,0:T(8,128)(2,1)S(1)} collective-permute-done((bf16[64,2560]{1,0:T(8,128)(2,1)S(1)}, bf16[64,2560]{1,0:T(8,128)(2,1)S(1)}, u32[]{:S(2)}, u32[]{:S(2)}) %collective-permute-start.26) | collective-permute-done | bytes 327712 | tf_op jit(solution)/shard_map/ppermute | solution.py:39
  168.1 1.9 %collective-permute-start.27 = (bf16[32,2560]{1,0:T(8,128)(2,1)S(1)}, bf16[32,2560]{1,0:T(8,128)(2,1)S(1)}, u32[]{:S(2)}, u32[]{:S(2)}) collective-permute-start(bf16[32,2560]{1,0:T(8,128)(2,1)S(1)} %get-tuple-element.136), channel_id=1, source_target_pairs={{0,4},{1,5},{2,6},{3,7},{4,0},{5,1},{6,2},{7,3},{8,12},{9,13},{10,... | collective-permute-start | bytes 491528 | tf_op jit(solution)/shard_map/ppermute | solution.py:39
  170.0 1.2 collective-permute-done.24
  171.3 4.9 %collective-permute-done.27 = bf16[32,2560]{1,0:T(8,128)(2,1)S(1)} collective-permute-done((bf16[32,2560]{1,0:T(8,128)(2,1)S(1)}, bf16[32,2560]{1,0:T(8,128)(2,1)S(1)}, u32[]{:S(2)}, u32[]{:S(2)}) %collective-permute-start.27) | collective-permute-done | bytes 163872 | tf_op jit(solution)/shard_map/ppermute | solution.py:39
  176.2 0.8 fusion
  (111 shorter events, 4.5 us)
Async XLA Ops:
  0.6 11.3 %copy-start.17 = (s32[4]{0:T(128)S(1)}, s32[4]{0:T(128)}, u32[]{:S(2)}) copy-start(s32[4]{0:T(128)} %constant.39.clone) | copy-start | bytes 52
  0.6 11.3 %copy-start.12 = (s32[8]{0:T(128)S(1)}, s32[8]{0:T(128)}, u32[]{:S(2)}) copy-start(s32[8]{0:T(128)} %constant.37.clone) | copy-start | bytes 100
  0.7 11.3 %copy-start.13 = (s32[8]{0:T(128)S(1)}, s32[8]{0:T(128)}, u32[]{:S(2)}) copy-start(s32[8]{0:T(128)} %constant.38.clone) | copy-start | bytes 100
  0.7 9.4 %copy-start.1 = (bf16[16,16,1728]{2,1,0:T(8,128)(2,1)S(1)}, bf16[16,16,1728]{2,1,0:T(8,128)(2,1)}, u32[]{:S(2)}) copy-start(bf16[16,16,1728]{2,1,0:T(8,128)(2,1)} %refs_4_) | copy-start | bytes 2654212
  0.7 11.0 %copy-start.11 = (s32[1,16]{1,0:T(1,128)S(1)}, s32[1,16]{1,0:T(1,128)}, u32[]{:S(2)}) copy-start(s32[1,16]{1,0:T(1,128)} %param.33) | copy-start | bytes 196
  0.7 11.6 %copy-start.14 = (s32[64]{0:T(128)S(1)}, s32[64]{0:T(128)}, u32[]{:S(2)}) copy-start(s32[64]{0:T(128)} %param.36) | copy-start | bytes 772
  0.7 11.6 %copy-start.15 = (s32[1,16]{1,0:T(1,128)S(1)}, s32[1,16]{1,0:T(1,128)}, u32[]{:S(2)}) copy-start(s32[1,16]{1,0:T(1,128)} %param.35) | copy-start | bytes 196
  2.8 27.5 %all-to-all-start = ((bf16[8,32,1536]{2,1,0:T(8,128)(2,1)}), bf16[8,32,1536]{2,1,0:T(8,128)(2,1)S(1)}, u32[]{:S(2)}, u32[]{:S(2)}) async-start(bf16[8,32,1536]{2,1,0:T(8,128)(2,1)} %join.1), calls=%async_computation | async-start | bytes 1572864 | tf_op jit(solution)/shard_map/all_to_all | solution.py:540
  10.1 40.0 %collective-permute-start.2 = (bf16[16,16,1728]{2,1,0:T(8,128)(2,1)S(1)}, bf16[16,16,1728]{2,1,0:T(8,128)(2,1)S(1)}, u32[]{:S(2)}, u32[]{:S(2)}) collective-permute-start(bf16[16,16,1728]{2,1,0:T(8,128)(2,1)S(1)} %copy-done.1), channel_id=1, source_target_pairs={{0,16},{8,24},{16,0},{24,8},{1,17},{9,25},{17,1},{25,9},{2,18},{10... | collective-permute-start | bytes 2654216 | tf_op jit(solution)/shard_map/ppermute | solution.py:31
  36.0 10.7 %collective-permute-start = (bf16[64,5120]{1,0:T(8,128)(2,1)S(1)}, bf16[64,5120]{1,0:T(8,128)(2,1)S(1)}, u32[]{:S(2)}, u32[]{:S(2)}) collective-permute-start(bf16[64,5120]{1,0:T(8,128)(2,1)S(1)} %get-tuple-element.75), channel_id=1, source_target_pairs={{0,1},{1,0},{2,3},{3,2},{4,5},{5,4},{6,7},{7,6},{8,10},{9,11},{10,... | collective-permute-start | bytes 1966088 | tf_op jit(solution)/shard_map/ppermute | solution.py:39
  41.9 14.9 %collective-permute-start.5 = (bf16[64,5120]{1,0:T(8,128)(2,1)S(1)}, bf16[64,5120]{1,0:T(8,128)(2,1)S(1)}, u32[]{:S(2)}, u32[]{:S(2)}) collective-permute-start(bf16[64,5120]{1,0:T(8,128)(2,1)S(1)} %get-tuple-element.80), channel_id=1, source_target_pairs={{0,1},{1,0},{2,3},{3,2},{4,5},{5,4},{6,7},{7,6},{8,10},{9,11},{10,... | collective-permute-start | bytes 1966088 | tf_op jit(solution)/shard_map/ppermute | solution.py:39
  42.6 7.5 %collective-permute-start.1 = (bf16[16,16,640]{2,1,0:T(8,128)(2,1)S(1)}, bf16[16,16,640]{2,1,0:T(8,128)(2,1)S(1)}, u32[]{:S(2)}, u32[]{:S(2)}) collective-permute-start(bf16[16,16,640]{2,1,0:T(8,128)(2,1)S(1)} %bitcast.16), channel_id=1, source_target_pairs={{0,16},{8,24},{16,0},{24,8},{1,17},{9,25},{17,1},{25,9},{2,18},{10... | collective-permute-start | bytes 983048 | tf_op jit(solution)/shard_map/ppermute | solution.py:31
  46.6 10.3 %copy-start.16 = (s32[1,2]{1,0:T(1,128)S(1)}, s32[1,2]{1,0:T(1,128)}, u32[]{:S(2)}) copy-start(s32[1,2]{1,0:T(1,128)} %param.34) | copy-start | bytes 28
  46.8 12.4 %copy-start.4 = (bf16[3,128,512]{2,1,0:T(8,128)(2,1)S(1)}, bf16[3,128,512]{2,1,0:T(8,128)(2,1)}, u32[]{:S(2)}) copy-start(bf16[3,128,512]{2,1,0:T(8,128)(2,1)} %key_cache_ref.1) | copy-start | bytes 1179652
  46.8 12.4 %copy-start.5 = (bf16[3,128,512]{2,1,0:T(8,128)(2,1)S(1)}, bf16[3,128,512]{2,1,0:T(8,128)(2,1)}, u32[]{:S(2)}) copy-start(bf16[3,128,512]{2,1,0:T(8,128)(2,1)} %value_cache_ref.1) | copy-start | bytes 1179652
  50.1 7.1 %collective-permute-start.3 = (bf16[32,5120]{1,0:T(8,128)(2,1)S(1)}, bf16[32,5120]{1,0:T(8,128)(2,1)S(1)}, u32[]{:S(2)}, u32[]{:S(2)}) collective-permute-start(bf16[32,5120]{1,0:T(8,128)(2,1)S(1)} %get-tuple-element.82), channel_id=1, source_target_pairs={{0,2},{1,3},{2,0},{3,1},{4,6},{5,7},{6,4},{7,5},{8,9},{9,8},{10,11... | collective-permute-start | bytes 983048 | tf_op jit(solution)/shard_map/ppermute | solution.py:39
  56.9 7.8 %collective-permute-start.6 = (bf16[32,5120]{1,0:T(8,128)(2,1)S(1)}, bf16[32,5120]{1,0:T(8,128)(2,1)S(1)}, u32[]{:S(2)}, u32[]{:S(2)}) collective-permute-start(bf16[32,5120]{1,0:T(8,128)(2,1)S(1)} %get-tuple-element.86), channel_id=1, source_target_pairs={{0,2},{1,3},{2,0},{3,1},{4,6},{5,7},{6,4},{7,5},{8,9},{9,8},{10,11... | collective-permute-start | bytes 983048 | tf_op jit(solution)/shard_map/ppermute | solution.py:39
  57.2 10.6 %collective-permute-start.4 = (bf16[16,5120]{1,0:T(8,128)(2,1)S(1)}, bf16[16,5120]{1,0:T(8,128)(2,1)S(1)}, u32[]{:S(2)}, u32[]{:S(2)}) collective-permute-start(bf16[16,5120]{1,0:T(8,128)(2,1)S(1)} %get-tuple-element.84), channel_id=1, source_target_pairs={{0,4},{1,5},{2,6},{3,7},{4,0},{5,1},{6,2},{7,3},{8,12},{9,13},{10,... | collective-permute-start | bytes 491528 | tf_op jit(solution)/shard_map/ppermute | solution.py:39
  58.5 9.3 %copy-start.10 = (f32[5120]{0:T(1024)S(1)}, f32[5120]{0:T(1024)}, u32[]{:S(2)}) copy-start(f32[5120]{0:T(1024)} %param.28) | copy-start | bytes 61444
  58.5 19.7 %collective-permute-start.8 = (bf16[16,16,640]{2,1,0:T(8,128)(2,1)S(1)}, bf16[16,16,640]{2,1,0:T(8,128)(2,1)S(1)}, u32[]{:S(2)}, u32[]{:S(2)}) collective-permute-start(bf16[16,16,640]{2,1,0:T(8,128)(2,1)S(1)} %bitcast.17), channel_id=1, source_target_pairs={{0,8},{8,0},{16,24},{24,16},{1,9},{9,1},{17,25},{25,17},{2,10},{10... | collective-permute-start | bytes 983048 | tf_op jit(solution)/shard_map/ppermute | solution.py:31
  58.6 20.3 %collective-permute-start.9 = (bf16[16,16,640]{2,1,0:T(8,128)(2,1)S(1)}, bf16[16,16,640]{2,1,0:T(8,128)(2,1)S(1)}, u32[]{:S(2)}, u32[]{:S(2)}) collective-permute-start(bf16[16,16,640]{2,1,0:T(8,128)(2,1)S(1)} %collective-permute-done.1.refs_1_), channel_id=1, source_target_pairs={{0,8},{8,0},{16,24},{24,16},{1,9},{9,1},{17,25},{25,17},{2,10},{10... | collective-permute-start | bytes 983048 | tf_op jit(solution)/shard_map/ppermute | solution.py:31
  59.1 19.8 %collective-permute-start.10 = (bf16[16,16,1728]{2,1,0:T(8,128)(2,1)S(1)}, bf16[16,16,1728]{2,1,0:T(8,128)(2,1)S(1)}, u32[]{:S(2)}, u32[]{:S(2)}) collective-permute-start(bf16[16,16,1728]{2,1,0:T(8,128)(2,1)S(1)} %copy-done.1), channel_id=1, source_target_pairs={{0,8},{8,0},{16,24},{24,16},{1,9},{9,1},{17,25},{25,17},{2,10},{10... | collective-permute-start | bytes 2654216 | tf_op jit(solution)/shard_map/ppermute | solution.py:31
  64.7 14.2 %collective-permute-start.11 = (bf16[16,16,1728]{2,1,0:T(8,128)(2,1)S(1)}, bf16[16,16,1728]{2,1,0:T(8,128)(2,1)S(1)}, u32[]{:S(2)}, u32[]{:S(2)}) collective-permute-start(bf16[16,16,1728]{2,1,0:T(8,128)(2,1)S(1)} %collective-permute-done.2.refs_5_), channel_id=1, source_target_pairs={{0,8},{8,0},{16,24},{24,16},{1,9},{9,1},{17,25},{25,17},{2,10},{10... | collective-permute-start | bytes 2654216 | tf_op jit(solution)/shard_map/ppermute | solution.py:31
  68.2 10.1 %collective-permute-start.12 = (bf16[16,5120]{1,0:T(8,128)(2,1)S(1)}, bf16[16,5120]{1,0:T(8,128)(2,1)S(1)}, u32[]{:S(2)}, u32[]{:S(2)}) collective-permute-start(bf16[16,5120]{1,0:T(8,128)(2,1)S(1)} %get-tuple-element.102), channel_id=1, source_target_pairs={{0,4},{1,5},{2,6},{3,7},{4,0},{5,1},{6,2},{7,3},{8,12},{9,13},{10,... | collective-permute-start | bytes 491528 | tf_op jit(solution)/shard_map/ppermute | solution.py:39
  78.3 8.9 %collective-permute-start.7 = (bf16[16,5120]{1,0:T(8,128)(2,1)S(1)}, bf16[16,5120]{1,0:T(8,128)(2,1)S(1)}, u32[]{:S(2)}, u32[]{:S(2)}) collective-permute-start(bf16[16,5120]{1,0:T(8,128)(2,1)S(1)} %get-tuple-element.91), channel_id=1, source_target_pairs={{0,4},{1,5},{2,6},{3,7},{4,0},{5,1},{6,2},{7,3},{8,12},{9,13},{10,... | collective-permute-start | bytes 491528 | tf_op jit(solution)/shard_map/ppermute | solution.py:39
  78.3 10.5 %collective-permute-start.13 = (bf16[32,5120]{1,0:T(8,128)(2,1)S(1)}, bf16[32,5120]{1,0:T(8,128)(2,1)S(1)}, u32[]{:S(2)}, u32[]{:S(2)}) collective-permute-start(bf16[32,5120]{1,0:T(8,128)(2,1)S(1)} %constant_dynamic-update-slice_fusion), channel_id=1, source_target_pairs={{0,2},{1,3},{2,0},{3,1},{4,6},{5,7},{6,4},{7,5},{8,9},{9,8},{10,11... | collective-permute-start | bytes 983048 | tf_op jit(solution)/shard_map/ppermute | solution.py:39
  82.7 13.3 %copy-start.2 = (bf16[256,1728]{1,0:T(8,128)(2,1)}, bf16[256,1728]{1,0:T(8,128)(2,1)S(1)}, u32[]{:S(2)}) copy-start(bf16[256,1728]{1,0:T(8,128)(2,1)S(1)} %get-tuple-element.119.refs_5_) | copy-start | bytes 2654212
  87.5 8.4 %collective-permute-start.15 = (bf16[16,5120]{1,0:T(8,128)(2,1)S(1)}, bf16[16,5120]{1,0:T(8,128)(2,1)S(1)}, u32[]{:S(2)}, u32[]{:S(2)}) collective-permute-start(bf16[16,5120]{1,0:T(8,128)(2,1)S(1)} %get-tuple-element.107), channel_id=1, source_target_pairs={{0,4},{1,5},{2,6},{3,7},{4,0},{5,1},{6,2},{7,3},{8,12},{9,13},{10,... | collective-permute-start | bytes 491528 | tf_op jit(solution)/shard_map/ppermute | solution.py:39
  88.8 15.1 %collective-permute-start.14 = (bf16[64,5120]{1,0:T(8,128)(2,1)S(1)}, bf16[64,5120]{1,0:T(8,128)(2,1)S(1)}, u32[]{:S(2)}, u32[]{:S(2)}) collective-permute-start(bf16[64,5120]{1,0:T(8,128)(2,1)S(1)} %pad_maximum_fusion.a_ref.refs_0_), channel_id=1, source_target_pairs={{0,1},{1,0},{2,3},{3,2},{4,5},{5,4},{6,7},{7,6},{8,10},{9,11},{10,... | collective-permute-start | bytes 1966088 | tf_op jit(solution)/shard_map/ppermute | solution.py:39
  96.0 7.9 %collective-permute-start.16 = (bf16[32,5120]{1,0:T(8,128)(2,1)S(1)}, bf16[32,5120]{1,0:T(8,128)(2,1)S(1)}, u32[]{:S(2)}, u32[]{:S(2)}) collective-permute-start(bf16[32,5120]{1,0:T(8,128)(2,1)S(1)} %pad_maximum_fusion.1), channel_id=1, source_target_pairs={{0,2},{1,3},{2,0},{3,1},{4,6},{5,7},{6,4},{7,5},{8,9},{9,8},{10,11... | collective-permute-start | bytes 983048 | tf_op jit(solution)/shard_map/ppermute | solution.py:39
  103.9 10.7 %collective-permute-start.17 = (bf16[64,5120]{1,0:T(8,128)(2,1)S(1)}, bf16[64,5120]{1,0:T(8,128)(2,1)S(1)}, u32[]{:S(2)}, u32[]{:S(2)}) collective-permute-start(bf16[64,5120]{1,0:T(8,128)(2,1)S(1)} %constant_dynamic-update-slice_fusion.2.a_ref.refs_0_.refs_2_), channel_id=1, source_target_pairs={{0,1},{1,0},{2,3},{3,2},{4,5},{5,4},{6,7},{7,6},{8,10},{9,11},{10,... | collective-permute-start | bytes 1966088 | tf_op jit(solution)/shard_map/ppermute | solution.py:39
  115.4 6.8 %collective-permute-start.18 = (f32[16,256]{1,0:T(8,128)S(1)}, f32[16,256]{1,0:T(8,128)S(1)}, u32[]{:S(2)}, u32[]{:S(2)}) collective-permute-start(f32[16,256]{1,0:T(8,128)S(1)} %pad_maximum_fusion.2), channel_id=1, source_target_pairs={{0,1},{1,0},{2,3},{3,2},{4,5},{5,4},{6,7},{7,6},{8,9},{9,8},{10,11... | collective-permute-start | bytes 49160 | tf_op jit(solution)/shard_map/ppermute | solution.py:31
  116.6 15.6 %slice-start = ((s8[17694720]{0:T(1024)(128)(4,1)}), s8[4194304]{0:T(1024)(128)(4,1)S(1)}, s32[]{:S(2)}) async-start(s8[17694720]{0:T(1024)(128)(4,1)} %bitcast.11), calls=%async_computation.1 | async-start | bytes 8388608
  116.6 15.7 %slice-start.1 = ((s8[17694720]{0:T(1024)(128)(4,1)}), s8[4194304]{0:T(1024)(128)(4,1)S(1)}, s32[]{:S(2)}) async-start(s8[17694720]{0:T(1024)(128)(4,1)} %bitcast.11), calls=%async_computation.2 | async-start | bytes 8388608
  116.6 15.7 %slice-start.2 = ((s8[17694720]{0:T(1024)(128)(4,1)}), s8[4194304]{0:T(1024)(128)(4,1)S(1)}, s32[]{:S(2)}) async-start(s8[17694720]{0:T(1024)(128)(4,1)} %bitcast.11), calls=%async_computation.3 | async-start | bytes 8388608
  122.2 10.1 %slice-start.3 = ((s8[17694720]{0:T(1024)(128)(4,1)}), s8[4194304]{0:T(1024)(128)(4,1)S(1)}, s32[]{:S(2)}) async-start(s8[17694720]{0:T(1024)(128)(4,1)} %bitcast.11), calls=%async_computation.4 | async-start | bytes 8388608
  122.3 10.0 %slice-start.4 = ((s8[17694720]{0:T(1024)(128)(4,1)}), s8[917504]{0:T(1024)(128)(4,1)S(1)}, s32[]{:S(2)}) async-start(s8[17694720]{0:T(1024)(128)(4,1)} %bitcast.11), calls=%async_computation.5 | async-start | bytes 1835008
  122.3 10.0 %copy-start.3 = (bf16[256,1728]{1,0:T(8,128)(2,1)S(1)}, bf16[256,1728]{1,0:T(8,128)(2,1)}, u32[]{:S(2)}) copy-start(bf16[256,1728]{1,0:T(8,128)(2,1)} %copy-done.2) | copy-start | bytes 2654212
  122.3 9.9 %collective-permute-start.21 = (f32[16,256]{1,0:T(8,128)S(1)}, f32[16,256]{1,0:T(8,128)S(1)}, u32[]{:S(2)}, u32[]{:S(2)}) collective-permute-start(f32[16,256]{1,0:T(8,128)S(1)} %fusion.3), channel_id=1, source_target_pairs={{0,6},{1,7},{2,4},{3,5},{4,2},{5,3},{6,0},{7,1},{8,14},{9,15},{10,... | collective-permute-start | bytes 49160 | tf_op jit(solution)/shard_map/ppermute | solution.py:31
  122.9 9.3 %collective-permute-start.19 = (f32[16,256]{1,0:T(8,128)S(1)}, f32[16,256]{1,0:T(8,128)S(1)}, u32[]{:S(2)}, u32[]{:S(2)}) collective-permute-start(f32[16,256]{1,0:T(8,128)S(1)} %fusion.3), channel_id=1, source_target_pairs={{0,2},{1,3},{2,0},{3,1},{4,6},{5,7},{6,4},{7,5},{8,10},{9,11},{10,... | collective-permute-start | bytes 49160 | tf_op jit(solution)/shard_map/ppermute | solution.py:31
  122.9 9.3 %collective-permute-start.20 = (f32[16,256]{1,0:T(8,128)S(1)}, f32[16,256]{1,0:T(8,128)S(1)}, u32[]{:S(2)}, u32[]{:S(2)}) collective-permute-start(f32[16,256]{1,0:T(8,128)S(1)} %fusion.3), channel_id=1, source_target_pairs={{0,4},{1,5},{2,6},{3,7},{4,0},{5,1},{6,2},{7,3},{8,12},{9,13},{10,... | collective-permute-start | bytes 49160 | tf_op jit(solution)/shard_map/ppermute | solution.py:31
  137.4 11.0 %collective-permute-start.22 = (bf16[128,2560]{1,0:T(8,128)(2,1)S(1)}, bf16[128,2560]{1,0:T(8,128)(2,1)S(1)}, u32[]{:S(2)}, u32[]{:S(2)}) collective-permute-start(bf16[128,2560]{1,0:T(8,128)(2,1)S(1)} %get-tuple-element.121), channel_id=1, source_target_pairs={{0,1},{1,0},{2,3},{3,2},{4,5},{5,4},{6,7},{7,6},{8,10},{9,11},{10,... | collective-permute-start | bytes 1966088 | tf_op jit(solution)/shard_map/ppermute | solution.py:39
  148.6 11.2 %collective-permute-start.25 = (bf16[128,2560]{1,0:T(8,128)(2,1)S(1)}, bf16[128,2560]{1,0:T(8,128)(2,1)S(1)}, u32[]{:S(2)}, u32[]{:S(2)}) collective-permute-start(bf16[128,2560]{1,0:T(8,128)(2,1)S(1)} %get-tuple-element.130), channel_id=1, source_target_pairs={{0,1},{1,0},{2,3},{3,2},{4,5},{5,4},{6,7},{7,6},{8,10},{9,11},{10,... | collective-permute-start | bytes 1966088 | tf_op jit(solution)/shard_map/ppermute | solution.py:39
  149.9 8.2 %collective-permute-start.23 = (bf16[64,2560]{1,0:T(8,128)(2,1)S(1)}, bf16[64,2560]{1,0:T(8,128)(2,1)S(1)}, u32[]{:S(2)}, u32[]{:S(2)}) collective-permute-start(bf16[64,2560]{1,0:T(8,128)(2,1)S(1)} %get-tuple-element.123), channel_id=1, source_target_pairs={{0,2},{1,3},{2,0},{3,1},{4,6},{5,7},{6,4},{7,5},{8,9},{9,8},{10,11... | collective-permute-start | bytes 983048 | tf_op jit(solution)/shard_map/ppermute | solution.py:39
  159.9 16.2 %copy-start.8 = (f32[16,5120]{1,0:T(8,128)S(1)}, f32[16,5120]{1,0:T(8,128)}, u32[]{:S(2)}) copy-start(f32[16,5120]{1,0:T(8,128)} %copy-done.7) | copy-start | bytes 983044
  160.0 8.1 %collective-permute-start.26 = (bf16[64,2560]{1,0:T(8,128)(2,1)S(1)}, bf16[64,2560]{1,0:T(8,128)(2,1)S(1)}, u32[]{:S(2)}, u32[]{:S(2)}) collective-permute-start(bf16[64,2560]{1,0:T(8,128)(2,1)S(1)} %get-tuple-element.134), channel_id=1, source_target_pairs={{0,2},{1,3},{2,0},{3,1},{4,6},{5,7},{6,4},{7,5},{8,9},{9,8},{10,11... | collective-permute-start | bytes 983048 | tf_op jit(solution)/shard_map/ppermute | solution.py:39
  160.7 10.6 %collective-permute-start.24 = (bf16[32,2560]{1,0:T(8,128)(2,1)S(1)}, bf16[32,2560]{1,0:T(8,128)(2,1)S(1)}, u32[]{:S(2)}, u32[]{:S(2)}) collective-permute-start(bf16[32,2560]{1,0:T(8,128)(2,1)S(1)} %get-tuple-element.125), channel_id=1, source_target_pairs={{0,4},{1,5},{2,6},{3,7},{4,0},{5,1},{6,2},{7,3},{8,12},{9,13},{10,... | collective-permute-start | bytes 491528 | tf_op jit(solution)/shard_map/ppermute | solution.py:39
  168.1 8.0 %collective-permute-start.27 = (bf16[32,2560]{1,0:T(8,128)(2,1)S(1)}, bf16[32,2560]{1,0:T(8,128)(2,1)S(1)}, u32[]{:S(2)}, u32[]{:S(2)}) collective-permute-start(bf16[32,2560]{1,0:T(8,128)(2,1)S(1)} %get-tuple-element.136), channel_id=1, source_target_pairs={{0,4},{1,5},{2,6},{3,7},{4,0},{5,1},{6,2},{7,3},{8,12},{9,13},{10,... | collective-permute-start | bytes 491528 | tf_op jit(solution)/shard_map/ppermute | solution.py:39
  (4 other events, 32.3 us)

commit v5 on v4

--- a/solution.py
+++ b/solution.py
@@ -368,7 +368,7 @@
     rows, width = arrays[0].shape
     depth = width // groups
 
-    per = 4
+    per = groups
     steps = groups // per
 
     def kernel(*refs):

time: 177 us -> 177 us (level)
  no operation moved by 1% of the time
where the time goes in v5:
time: 177 us
  waiting for transfers between devices  97.5 us (55%)
  Pallas kernels  46.2 us (26%)
  starting transfers between devices  29.5 us (17%)
  other arithmetic  1.79 us (1%)
    ppermute x18, waiting for transfers between devices, swap(): return lax.ppermute(x, ('req', 'mlp'), pairs)  76.6 us
    all_to_all x1, waiting for transfers between devices, shards(): lax.all_to_all(join((queries, keys, values), groups), 'mlp', split_axis=0...  17.6 us
    pallas_call x3, Pallas kernels, feedfwd_in(): pl.pallas_call(kernel, grid=(steps,), in_specs=[rows] * (2 * count) + [pl...  16.6 us
    ppermute x18, starting transfers between devices, swap(): return lax.ppermute(x, ('req', 'mlp'), pairs)  12.9 us
    ppermute x10, starting transfers between devices, exchange(): return lax.ppermute(x, axis, [(i, i ^ mask) for i in range(size)])  9.33 us
    all_to_all x1, starting transfers between devices, shards(): lax.all_to_all(join((queries, keys, values), groups), 'mlp', split_axis=0...  7.28 us
    pallas_call x1, Pallas kernels, attend(): pl.pallas_call(kernel, grid_spec=pltpu.PrefetchScalarGridSpec(num_scalar_...  5.58 us
    pallas_call x1, Pallas kernels, feedfwd_out_first(): pl.pallas_call(kernel, grid_spec=pltpu.PrefetchScalarGridSpec(num_scalar_...  5.06 us
  transfers between devices with their start and end apart: 29, of which 19 were waited for; matrix products, arithmetic and copies ran while one was open for 1% of the time, Pallas kernels for 21%

profile of v5, /device:TPU:0, one launch (start us, length us, event | category | flops | bytes accessed | tf_op | source)
XLA Modules:
  0.0 176.9 jit_solution(3293843250088988999)
XLA Ops:
  0.7 2.1 %join.1 = bf16[8,32,1536]{2,1,0:T(8,128)(2,1)} custom-call(bf16[32,4096]{1,0:T(8,128)(2,1)} %refs_0_.1, bf16[32,4096]{1,0:T(8,128)(2,1)} %refs_1_.1, bf16[32,4096]{1,0:T(8,128)(2,1)} %refs_2_.1), custom_call_target="tpu_custom_call" | custom-call | bytes 1 | tf_op jit(solution)/shard_map/join/pallas_call | solution.py:380
  2.8 7.3 %all-to-all-start = ((bf16[8,32,1536]{2,1,0:T(8,128)(2,1)}), bf16[8,32,1536]{2,1,0:T(8,128)(2,1)S(1)}, u32[]{:S(2)}, u32[]{:S(2)}) async-start(bf16[8,32,1536]{2,1,0:T(8,128)(2,1)} %join.1), calls=%async_computation | async-start | bytes 1572864 | tf_op jit(solution)/shard_map/all_to_all | solution.py:540
  10.1 1.6 collective-permute-start.2
  12.7 17.6 %all-to-all-done = bf16[8,32,1536]{2,1,0:T(8,128)(2,1)S(1)} async-done(((bf16[8,32,1536]{2,1,0:T(8,128)(2,1)}), bf16[8,32,1536]{2,1,0:T(8,128)(2,1)S(1)}, u32[]{:S(2)}, u32[]{:S(2)}) %all-to-all-start) | async-done | bytes 786464 | tf_op jit(solution)/shard_map/all_to_all | solution.py:540
  30.4 5.6 %attend.1 = (bf16[8,32,512]{2,1,0:T(8,128)(2,1)S(1)}, bf16[64,5120]{1,0:T(8,128)(2,1)S(1)}, bf16[64,5120]{1,0:T(8,128)(2,1)S(1)}) custom-call(s32[9]{0:T(128)S(1)} %pad_add_fusion.control_ref, bf16[256,1536]{1,0:T(8,128)(2,1)S(1)} %bitcast.13, s32[256,1]{1,0:T(8,128)S(1)} %copy.27.col_ref, s32[1,256]{1,0:T(1,128)S(1)} %bitcast.24, bf16[512,5120]{1,0:T(8,128)(2,1)} %w_ref.4), custom_call_target="tpu_custom_call" | custom-call | bytes 1 | tf_op jit(solution)/shard_map/attend/pallas_call | solution.py:426
  36.0 1.4 collective-permute-start
  37.5 4.4 %out_projection.1 = (bf16[64,5120]{1,0:T(8,128)(2,1)S(1)}, bf16[64,5120]{1,0:T(8,128)(2,1)S(1)}) custom-call(s32[9]{0:T(128)S(1)} %pad_add_fusion.control_ref, bf16[8,32,512]{2,1,0:T(8,128)(2,1)S(1)} %get-tuple-element.78.x_ref, bf16[512,5120]{1,0:T(8,128)(2,1)} %w_ref.4), custom_call_target="tpu_custom_call" | custom-call | bytes 1 | tf_op jit(solution)/shard_map/out_projection/pallas_call | solution.py:103
  41.9 0.7 collective-permute-start.5
  42.6 1.5 collective-permute-start.1
  44.1 2.6 %collective-permute-done.got_ref = bf16[64,5120]{1,0:T(8,128)(2,1)S(1)} collective-permute-done((bf16[64,5120]{1,0:T(8,128)(2,1)S(1)}, bf16[64,5120]{1,0:T(8,128)(2,1)S(1)}, u32[]{:S(2)}, u32[]{:S(2)}) %collective-permute-start) | collective-permute-done | bytes 655392 | tf_op jit(solution)/shard_map/ppermute | solution.py:39
  46.9 3.3 %collective-permute-done.1.refs_1_ = bf16[16,16,640]{2,1,0:T(8,128)(2,1)S(1)} collective-permute-done((bf16[16,16,640]{2,1,0:T(8,128)(2,1)S(1)}, bf16[16,16,640]{2,1,0:T(8,128)(2,1)S(1)}, u32[]{:S(2)}, u32[]{:S(2)}) %collective-permute-start.1) | collective-permute-done | bytes 327712 | tf_op jit(solution)/shard_map/ppermute | solution.py:31
  50.5 6.3 %collective-permute-done.5.got_ref = bf16[64,5120]{1,0:T(8,128)(2,1)S(1)} collective-permute-done((bf16[64,5120]{1,0:T(8,128)(2,1)S(1)}, bf16[64,5120]{1,0:T(8,128)(2,1)S(1)}, u32[]{:S(2)}, u32[]{:S(2)}) %collective-permute-start.5) | collective-permute-done | bytes 655392 | tf_op jit(solution)/shard_map/ppermute | solution.py:39
  57.2 1.3 collective-permute-start.4
  58.7 0.5 collective-permute-start.9
  59.3 2.1 %write_pages.1 = (bf16[3,128,512]{2,1,0:T(8,128)(2,1)}, bf16[3,128,512]{2,1,0:T(8,128)(2,1)}) custom-call(s32[3]{0:T(128)S(1)} %broadcast_add_fusion.source_ref, bf16[256,1536]{1,0:T(8,128)(2,1)S(1)} %bitcast.14, bf16[256,1536]{1,0:T(8,128)(2,1)S(1)} %bitcast.15, bf16[3,128,512]{2,1,0:T(8,128)(2,1)S(1)} %copy-done.4, bf16[3,128,512]{2,1,0:T(8,128)(2,1)S(1)} %copy-done.5), custom_call_target="tpu_custom_call" | custom-call | bytes 8388608 | tf_op jit(solution)/shard_map/write_pages/pallas_call | solution.py:471
  61.4 3.4 %collective-permute-done.6.got_ref = bf16[32,5120]{1,0:T(8,128)(2,1)S(1)} collective-permute-done((bf16[32,5120]{1,0:T(8,128)(2,1)S(1)}, bf16[32,5120]{1,0:T(8,128)(2,1)S(1)}, u32[]{:S(2)}, u32[]{:S(2)}) %collective-permute-start.6) | collective-permute-done | bytes 327712 | tf_op jit(solution)/shard_map/ppermute | solution.py:39
  64.8 3.1 %collective-permute-done.4.b_ref = bf16[16,5120]{1,0:T(8,128)(2,1)S(1)} collective-permute-done((bf16[16,5120]{1,0:T(8,128)(2,1)S(1)}, bf16[16,5120]{1,0:T(8,128)(2,1)S(1)}, u32[]{:S(2)}, u32[]{:S(2)}) %collective-permute-start.4) | collective-permute-done | bytes 163872 | tf_op jit(solution)/shard_map/ppermute | solution.py:39
  68.7 9.7 %collective-permute-done.12 = bf16[16,5120]{1,0:T(8,128)(2,1)S(1)} collective-permute-done((bf16[16,5120]{1,0:T(8,128)(2,1)S(1)}, bf16[16,5120]{1,0:T(8,128)(2,1)S(1)}, u32[]{:S(2)}, u32[]{:S(2)}) %collective-permute-start.12) | collective-permute-done | bytes 163872 | tf_op jit(solution)/shard_map/ppermute | solution.py:39
  78.3 0.6 collective-permute-start.13
  79.0 3.7 %pick.1 = (bf16[256,640]{1,0:T(8,128)(2,1)S(1)}, bf16[256,1728]{1,0:T(8,128)(2,1)S(1)}) custom-call(s32[16]{0:T(128)S(1)} %select_reduce_fusion.at_ref, bf16[16,16,640]{2,1,0:T(8,128)(2,1)S(1)} %bitcast.18, bf16[16,16,640]{2,1,0:T(8,128)(2,1)S(1)} %collective-permute-done.1.refs_1_, bf16[16,16,640]{2,1,0:T(8,128)(2,1)S(1)} %collective-permute-done.8.refs_2_, ...), custom_call_target="tpu_custom_call" | custom-call | bytes 8388608 | tf_op jit(solution)/shard_map/pick/pallas_call | solution.py:351
  82.7 4.5 %collective-permute-done.7.b_ref = bf16[16,5120]{1,0:T(8,128)(2,1)S(1)} collective-permute-done((bf16[16,5120]{1,0:T(8,128)(2,1)S(1)}, bf16[16,5120]{1,0:T(8,128)(2,1)S(1)}, u32[]{:S(2)}, u32[]{:S(2)}) %collective-permute-start.7) | collective-permute-done | bytes 163872 | tf_op jit(solution)/shard_map/ppermute | solution.py:39
  87.6 1.2 collective-permute-done.13
  88.9 1.5 collective-permute-start.14
  90.4 5.6 %collective-permute-done.15 = bf16[16,5120]{1,0:T(8,128)(2,1)S(1)} collective-permute-done((bf16[16,5120]{1,0:T(8,128)(2,1)S(1)}, bf16[16,5120]{1,0:T(8,128)(2,1)S(1)}, u32[]{:S(2)}, u32[]{:S(2)}) %collective-permute-start.15) | collective-permute-done | bytes 163872 | tf_op jit(solution)/shard_map/ppermute | solution.py:39
  96.1 7.8 %collective-permute-done.16 = bf16[32,5120]{1,0:T(8,128)(2,1)S(1)} collective-permute-done((bf16[32,5120]{1,0:T(8,128)(2,1)S(1)}, bf16[32,5120]{1,0:T(8,128)(2,1)S(1)}, u32[]{:S(2)}, u32[]{:S(2)}) %collective-permute-start.16) | collective-permute-done | bytes 327712 | tf_op jit(solution)/shard_map/ppermute | solution.py:39
  104.0 1.2 collective-permute-start.17
  105.5 0.8 down_products.2
  106.3 5.5 %feedfwd_in.3.refs_5_ = f32[128,1728]{1,0:T(8,128)S(1)} custom-call(bf16[64,5120]{1,0:T(8,128)(2,1)S(1)} %pad_maximum_fusion.a_ref.refs_0_, bf16[64,5120]{1,0:T(8,128)(2,1)S(1)} %collective-permute-done.14.b_ref.refs_1_, bf16[1728,5120]{1,0:T(8,128)(2,1)} %bitcast.25), custom_call_target="tpu_custom_call" | custom-call | flops 1132462080 | bytes 8847360 | tf_op jit(solution)/shard_map/feedfwd_in/pallas_call | solution.py:199
  111.8 2.8 %collective-permute-done.17.b_ref.refs_1_.refs_3_ = bf16[64,5120]{1,0:T(8,128)(2,1)S(1)} collective-permute-done((bf16[64,5120]{1,0:T(8,128)(2,1)S(1)}, bf16[64,5120]{1,0:T(8,128)(2,1)S(1)}, u32[]{:S(2)}, u32[]{:S(2)}) %collective-permute-start.17) | collective-permute-done | bytes 655392 | tf_op jit(solution)/shard_map/ppermute | solution.py:39
  114.7 0.8 down_products.3
  115.5 1.2 collective-permute-start.18
  116.7 5.6 %feedfwd_in.4.refs_6_ = f32[128,1728]{1,0:T(8,128)S(1)} custom-call(bf16[64,5120]{1,0:T(8,128)(2,1)S(1)} %constant_dynamic-update-slice_fusion.2.a_ref.refs_0_.refs_2_, bf16[64,5120]{1,0:T(8,128)(2,1)S(1)} %collective-permute-done.17.b_ref.refs_1_.refs_3_, bf16[1728,5120]{1,0:T(8,128)(2,1)} %bitcast.26), custom_call_target="tpu_custom_call" | custom-call | flops 1132462080 | bytes 8847360 | tf_op jit(solution)/shard_map/feedfwd_in/pallas_call | solution.py:199
  122.3 0.7 collective-permute-start.21
  123.0 3.8 %collective-permute-start.20 = (f32[16,256]{1,0:T(8,128)S(1)}, f32[16,256]{1,0:T(8,128)S(1)}, u32[]{:S(2)}, u32[]{:S(2)}) collective-permute-start(f32[16,256]{1,0:T(8,128)S(1)} %fusion.3), channel_id=1, source_target_pairs={{0,4},{1,5},{2,6},{3,7},{4,0},{5,1},{6,2},{7,3},{8,12},{9,13},{10,... | collective-permute-start | bytes 49160 | tf_op jit(solution)/shard_map/ppermute | solution.py:31
  126.8 5.5 %feedfwd_in.5 = (f32[128,1728]{1,0:T(8,128)S(1)}, f32[128,1728]{1,0:T(8,128)S(1)}) custom-call(bf16[64,5120]{1,0:T(8,128)(2,1)S(1)} %pad_maximum_fusion.a_ref.refs_0_, bf16[64,5120]{1,0:T(8,128)(2,1)S(1)} %collective-permute-done.14.b_ref.refs_1_, bf16[64,5120]{1,0:T(8,128)(2,1)S(1)} %constant_dynamic-update-slice_fusion.2.a_ref.refs_0_.refs_2_, ...), custom_call_target="tpu_custom_call" | custom-call | flops 2264924160 | bytes 8847360 | tf_op jit(solution)/shard_map/feedfwd_in/pallas_call | solution.py:199
  132.4 5.1 %feedfwd_out_first.1 = (bf16[256,1728]{1,0:T(8,128)(2,1)S(1)}, bf16[128,2560]{1,0:T(8,128)(2,1)S(1)}, bf16[128,2560]{1,0:T(8,128)(2,1)S(1)}) custom-call(s32[9]{0:T(128)S(1)} %pad_add_fusion.control_ref, f32[128,1728]{1,0:T(8,128)S(1)} %get-tuple-element.116.refs_0_, f32[128,1728]{1,0:T(8,128)S(1)} %get-tuple-element.117.refs_1_, ...), custom_call_target="tpu_custom_call" | custom-call | bytes 1 | tf_op jit(solution)/shard_map/feedfwd_out_first/pallas_call | solution.py:306
  137.5 1.0 collective-permute-start.22
  138.4 3.4 %feedfwd_out.1 = (bf16[128,2560]{1,0:T(8,128)(2,1)S(1)}, bf16[128,2560]{1,0:T(8,128)(2,1)S(1)}) custom-call(bf16[256,1728]{1,0:T(8,128)(2,1)S(1)} %get-tuple-element.126.x_ref, bf16[1728,5120]{1,0:T(8,128)(2,1)S(1)} %bitcast.12), custom_call_target="tpu_custom_call" | custom-call | bytes 1 | tf_op jit(solution)/shard_map/feedfwd_out/pallas_call | solution.py:132
  141.9 6.6 %collective-permute-done.22.got_ref = bf16[128,2560]{1,0:T(8,128)(2,1)S(1)} collective-permute-done((bf16[128,2560]{1,0:T(8,128)(2,1)S(1)}, bf16[128,2560]{1,0:T(8,128)(2,1)S(1)}, u32[]{:S(2)}, u32[]{:S(2)}) %collective-permute-start.22) | collective-permute-done | bytes 655392 | tf_op jit(solution)/shard_map/ppermute | solution.py:39
  148.6 1.3 collective-permute-start.25
  149.9 8.2 %collective-permute-done.23.got_ref = bf16[64,2560]{1,0:T(8,128)(2,1)S(1)} collective-permute-done((bf16[64,2560]{1,0:T(8,128)(2,1)S(1)}, bf16[64,2560]{1,0:T(8,128)(2,1)S(1)}, u32[]{:S(2)}, u32[]{:S(2)}) %collective-permute-start.23) | collective-permute-done | bytes 327712 | tf_op jit(solution)/shard_map/ppermute | solution.py:39
  158.2 1.6 collective-permute-done.25.got_ref
  160.0 0.8 collective-permute-start.26
  160.7 7.2 %collective-permute-done.26.got_ref = bf16[64,2560]{1,0:T(8,128)(2,1)S(1)} collective-permute-done((bf16[64,2560]{1,0:T(8,128)(2,1)S(1)}, bf16[64,2560]{1,0:T(8,128)(2,1)S(1)}, u32[]{:S(2)}, u32[]{:S(2)}) %collective-permute-start.26) | collective-permute-done | bytes 327712 | tf_op jit(solution)/shard_map/ppermute | solution.py:39
  168.0 2.0 %collective-permute-start.27 = (bf16[32,2560]{1,0:T(8,128)(2,1)S(1)}, bf16[32,2560]{1,0:T(8,128)(2,1)S(1)}, u32[]{:S(2)}, u32[]{:S(2)}) collective-permute-start(bf16[32,2560]{1,0:T(8,128)(2,1)S(1)} %get-tuple-element.136), channel_id=1, source_target_pairs={{0,4},{1,5},{2,6},{3,7},{4,0},{5,1},{6,2},{7,3},{8,12},{9,13},{10,... | collective-permute-start | bytes 491528 | tf_op jit(solution)/shard_map/ppermute | solution.py:39
  170.0 1.3 collective-permute-done.24
  171.4 4.7 %collective-permute-done.27 = bf16[32,2560]{1,0:T(8,128)(2,1)S(1)} collective-permute-done((bf16[32,2560]{1,0:T(8,128)(2,1)S(1)}, bf16[32,2560]{1,0:T(8,128)(2,1)S(1)}, u32[]{:S(2)}, u32[]{:S(2)}) %collective-permute-start.27) | collective-permute-done | bytes 163872 | tf_op jit(solution)/shard_map/ppermute | solution.py:39
  176.1 0.8 fusion
  (111 shorter events, 4.5 us)
Async XLA Ops:
  0.6 11.4 %copy-start.17 = (s32[4]{0:T(128)S(1)}, s32[4]{0:T(128)}, u32[]{:S(2)}) copy-start(s32[4]{0:T(128)} %constant.39.clone) | copy-start | bytes 52
  0.6 11.4 %copy-start.12 = (s32[8]{0:T(128)S(1)}, s32[8]{0:T(128)}, u32[]{:S(2)}) copy-start(s32[8]{0:T(128)} %constant.37.clone) | copy-start | bytes 100
  0.7 11.4 %copy-start.13 = (s32[8]{0:T(128)S(1)}, s32[8]{0:T(128)}, u32[]{:S(2)}) copy-start(s32[8]{0:T(128)} %constant.38.clone) | copy-start | bytes 100
  0.7 9.5 %copy-start.1 = (bf16[16,16,1728]{2,1,0:T(8,128)(2,1)S(1)}, bf16[16,16,1728]{2,1,0:T(8,128)(2,1)}, u32[]{:S(2)}) copy-start(bf16[16,16,1728]{2,1,0:T(8,128)(2,1)} %refs_4_) | copy-start | bytes 2654212
  0.7 11.0 %copy-start.11 = (s32[1,16]{1,0:T(1,128)S(1)}, s32[1,16]{1,0:T(1,128)}, u32[]{:S(2)}) copy-start(s32[1,16]{1,0:T(1,128)} %param.33) | copy-start | bytes 196
  0.7 11.6 %copy-start.14 = (s32[64]{0:T(128)S(1)}, s32[64]{0:T(128)}, u32[]{:S(2)}) copy-start(s32[64]{0:T(128)} %param.36) | copy-start | bytes 772
  0.7 11.6 %copy-start.15 = (s32[1,16]{1,0:T(1,128)S(1)}, s32[1,16]{1,0:T(1,128)}, u32[]{:S(2)}) copy-start(s32[1,16]{1,0:T(1,128)} %param.35) | copy-start | bytes 196
  2.8 27.5 %all-to-all-start = ((bf16[8,32,1536]{2,1,0:T(8,128)(2,1)}), bf16[8,32,1536]{2,1,0:T(8,128)(2,1)S(1)}, u32[]{:S(2)}, u32[]{:S(2)}) async-start(bf16[8,32,1536]{2,1,0:T(8,128)(2,1)} %join.1), calls=%async_computation | async-start | bytes 1572864 | tf_op jit(solution)/shard_map/all_to_all | solution.py:540
  10.1 40.0 %collective-permute-start.2 = (bf16[16,16,1728]{2,1,0:T(8,128)(2,1)S(1)}, bf16[16,16,1728]{2,1,0:T(8,128)(2,1)S(1)}, u32[]{:S(2)}, u32[]{:S(2)}) collective-permute-start(bf16[16,16,1728]{2,1,0:T(8,128)(2,1)S(1)} %copy-done.1), channel_id=1, source_target_pairs={{0,16},{8,24},{16,0},{24,8},{1,17},{9,25},{17,1},{25,9},{2,18},{10... | collective-permute-start | bytes 2654216 | tf_op jit(solution)/shard_map/ppermute | solution.py:31
  36.0 10.7 %collective-permute-start = (bf16[64,5120]{1,0:T(8,128)(2,1)S(1)}, bf16[64,5120]{1,0:T(8,128)(2,1)S(1)}, u32[]{:S(2)}, u32[]{:S(2)}) collective-permute-start(bf16[64,5120]{1,0:T(8,128)(2,1)S(1)} %get-tuple-element.75), channel_id=1, source_target_pairs={{0,1},{1,0},{2,3},{3,2},{4,5},{5,4},{6,7},{7,6},{8,10},{9,11},{10,... | collective-permute-start | bytes 1966088 | tf_op jit(solution)/shard_map/ppermute | solution.py:39
  41.9 14.9 %collective-permute-start.5 = (bf16[64,5120]{1,0:T(8,128)(2,1)S(1)}, bf16[64,5120]{1,0:T(8,128)(2,1)S(1)}, u32[]{:S(2)}, u32[]{:S(2)}) collective-permute-start(bf16[64,5120]{1,0:T(8,128)(2,1)S(1)} %get-tuple-element.80), channel_id=1, source_target_pairs={{0,1},{1,0},{2,3},{3,2},{4,5},{5,4},{6,7},{7,6},{8,10},{9,11},{10,... | collective-permute-start | bytes 1966088 | tf_op jit(solution)/shard_map/ppermute | solution.py:39
  42.6 7.5 %collective-permute-start.1 = (bf16[16,16,640]{2,1,0:T(8,128)(2,1)S(1)}, bf16[16,16,640]{2,1,0:T(8,128)(2,1)S(1)}, u32[]{:S(2)}, u32[]{:S(2)}) collective-permute-start(bf16[16,16,640]{2,1,0:T(8,128)(2,1)S(1)} %bitcast.16), channel_id=1, source_target_pairs={{0,16},{8,24},{16,0},{24,8},{1,17},{9,25},{17,1},{25,9},{2,18},{10... | collective-permute-start | bytes 983048 | tf_op jit(solution)/shard_map/ppermute | solution.py:31
  46.7 10.3 %copy-start.16 = (s32[1,2]{1,0:T(1,128)S(1)}, s32[1,2]{1,0:T(1,128)}, u32[]{:S(2)}) copy-start(s32[1,2]{1,0:T(1,128)} %param.34) | copy-start | bytes 28
  46.8 12.4 %copy-start.4 = (bf16[3,128,512]{2,1,0:T(8,128)(2,1)S(1)}, bf16[3,128,512]{2,1,0:T(8,128)(2,1)}, u32[]{:S(2)}) copy-start(bf16[3,128,512]{2,1,0:T(8,128)(2,1)} %key_cache_ref.1) | copy-start | bytes 1179652
  46.8 12.4 %copy-start.5 = (bf16[3,128,512]{2,1,0:T(8,128)(2,1)S(1)}, bf16[3,128,512]{2,1,0:T(8,128)(2,1)}, u32[]{:S(2)}) copy-start(bf16[3,128,512]{2,1,0:T(8,128)(2,1)} %value_cache_ref.1) | copy-start | bytes 1179652
  50.1 7.1 %collective-permute-start.3 = (bf16[32,5120]{1,0:T(8,128)(2,1)S(1)}, bf16[32,5120]{1,0:T(8,128)(2,1)S(1)}, u32[]{:S(2)}, u32[]{:S(2)}) collective-permute-start(bf16[32,5120]{1,0:T(8,128)(2,1)S(1)} %get-tuple-element.82), channel_id=1, source_target_pairs={{0,2},{1,3},{2,0},{3,1},{4,6},{5,7},{6,4},{7,5},{8,9},{9,8},{10,11... | collective-permute-start | bytes 983048 | tf_op jit(solution)/shard_map/ppermute | solution.py:39
  56.9 7.8 %collective-permute-start.6 = (bf16[32,5120]{1,0:T(8,128)(2,1)S(1)}, bf16[32,5120]{1,0:T(8,128)(2,1)S(1)}, u32[]{:S(2)}, u32[]{:S(2)}) collective-permute-start(bf16[32,5120]{1,0:T(8,128)(2,1)S(1)} %get-tuple-element.86), channel_id=1, source_target_pairs={{0,2},{1,3},{2,0},{3,1},{4,6},{5,7},{6,4},{7,5},{8,9},{9,8},{10,11... | collective-permute-start | bytes 983048 | tf_op jit(solution)/shard_map/ppermute | solution.py:39
  57.2 10.6 %collective-permute-start.4 = (bf16[16,5120]{1,0:T(8,128)(2,1)S(1)}, bf16[16,5120]{1,0:T(8,128)(2,1)S(1)}, u32[]{:S(2)}, u32[]{:S(2)}) collective-permute-start(bf16[16,5120]{1,0:T(8,128)(2,1)S(1)} %get-tuple-element.84), channel_id=1, source_target_pairs={{0,4},{1,5},{2,6},{3,7},{4,0},{5,1},{6,2},{7,3},{8,12},{9,13},{10,... | collective-permute-start | bytes 491528 | tf_op jit(solution)/shard_map/ppermute | solution.py:39
  58.6 9.3 %copy-start.10 = (f32[5120]{0:T(1024)S(1)}, f32[5120]{0:T(1024)}, u32[]{:S(2)}) copy-start(f32[5120]{0:T(1024)} %param.28) | copy-start | bytes 61444
  58.6 19.7 %collective-permute-start.8 = (bf16[16,16,640]{2,1,0:T(8,128)(2,1)S(1)}, bf16[16,16,640]{2,1,0:T(8,128)(2,1)S(1)}, u32[]{:S(2)}, u32[]{:S(2)}) collective-permute-start(bf16[16,16,640]{2,1,0:T(8,128)(2,1)S(1)} %bitcast.17), channel_id=1, source_target_pairs={{0,8},{8,0},{16,24},{24,16},{1,9},{9,1},{17,25},{25,17},{2,10},{10... | collective-permute-start | bytes 983048 | tf_op jit(solution)/shard_map/ppermute | solution.py:31
  58.7 20.3 %collective-permute-start.9 = (bf16[16,16,640]{2,1,0:T(8,128)(2,1)S(1)}, bf16[16,16,640]{2,1,0:T(8,128)(2,1)S(1)}, u32[]{:S(2)}, u32[]{:S(2)}) collective-permute-start(bf16[16,16,640]{2,1,0:T(8,128)(2,1)S(1)} %collective-permute-done.1.refs_1_), channel_id=1, source_target_pairs={{0,8},{8,0},{16,24},{24,16},{1,9},{9,1},{17,25},{25,17},{2,10},{10... | collective-permute-start | bytes 983048 | tf_op jit(solution)/shard_map/ppermute | solution.py:31
  59.2 19.8 %collective-permute-start.10 = (bf16[16,16,1728]{2,1,0:T(8,128)(2,1)S(1)}, bf16[16,16,1728]{2,1,0:T(8,128)(2,1)S(1)}, u32[]{:S(2)}, u32[]{:S(2)}) collective-permute-start(bf16[16,16,1728]{2,1,0:T(8,128)(2,1)S(1)} %copy-done.1), channel_id=1, source_target_pairs={{0,8},{8,0},{16,24},{24,16},{1,9},{9,1},{17,25},{25,17},{2,10},{10... | collective-permute-start | bytes 2654216 | tf_op jit(solution)/shard_map/ppermute | solution.py:31
  64.7 14.2 %collective-permute-start.11 = (bf16[16,16,1728]{2,1,0:T(8,128)(2,1)S(1)}, bf16[16,16,1728]{2,1,0:T(8,128)(2,1)S(1)}, u32[]{:S(2)}, u32[]{:S(2)}) collective-permute-start(bf16[16,16,1728]{2,1,0:T(8,128)(2,1)S(1)} %collective-permute-done.2.refs_5_), channel_id=1, source_target_pairs={{0,8},{8,0},{16,24},{24,16},{1,9},{9,1},{17,25},{25,17},{2,10},{10... | collective-permute-start | bytes 2654216 | tf_op jit(solution)/shard_map/ppermute | solution.py:31
  68.2 10.1 %collective-permute-start.12 = (bf16[16,5120]{1,0:T(8,128)(2,1)S(1)}, bf16[16,5120]{1,0:T(8,128)(2,1)S(1)}, u32[]{:S(2)}, u32[]{:S(2)}) collective-permute-start(bf16[16,5120]{1,0:T(8,128)(2,1)S(1)} %get-tuple-element.102), channel_id=1, source_target_pairs={{0,4},{1,5},{2,6},{3,7},{4,0},{5,1},{6,2},{7,3},{8,12},{9,13},{10,... | collective-permute-start | bytes 491528 | tf_op jit(solution)/shard_map/ppermute | solution.py:39
  78.3 8.9 %collective-permute-start.7 = (bf16[16,5120]{1,0:T(8,128)(2,1)S(1)}, bf16[16,5120]{1,0:T(8,128)(2,1)S(1)}, u32[]{:S(2)}, u32[]{:S(2)}) collective-permute-start(bf16[16,5120]{1,0:T(8,128)(2,1)S(1)} %get-tuple-element.91), channel_id=1, source_target_pairs={{0,4},{1,5},{2,6},{3,7},{4,0},{5,1},{6,2},{7,3},{8,12},{9,13},{10,... | collective-permute-start | bytes 491528 | tf_op jit(solution)/shard_map/ppermute | solution.py:39
  78.3 10.5 %collective-permute-start.13 = (bf16[32,5120]{1,0:T(8,128)(2,1)S(1)}, bf16[32,5120]{1,0:T(8,128)(2,1)S(1)}, u32[]{:S(2)}, u32[]{:S(2)}) collective-permute-start(bf16[32,5120]{1,0:T(8,128)(2,1)S(1)} %constant_dynamic-update-slice_fusion), channel_id=1, source_target_pairs={{0,2},{1,3},{2,0},{3,1},{4,6},{5,7},{6,4},{7,5},{8,9},{9,8},{10,11... | collective-permute-start | bytes 983048 | tf_op jit(solution)/shard_map/ppermute | solution.py:39
  82.7 13.3 %copy-start.2 = (bf16[256,1728]{1,0:T(8,128)(2,1)}, bf16[256,1728]{1,0:T(8,128)(2,1)S(1)}, u32[]{:S(2)}) copy-start(bf16[256,1728]{1,0:T(8,128)(2,1)S(1)} %get-tuple-element.119.refs_5_) | copy-start | bytes 2654212
  87.5 8.4 %collective-permute-start.15 = (bf16[16,5120]{1,0:T(8,128)(2,1)S(1)}, bf16[16,5120]{1,0:T(8,128)(2,1)S(1)}, u32[]{:S(2)}, u32[]{:S(2)}) collective-permute-start(bf16[16,5120]{1,0:T(8,128)(2,1)S(1)} %get-tuple-element.107), channel_id=1, source_target_pairs={{0,4},{1,5},{2,6},{3,7},{4,0},{5,1},{6,2},{7,3},{8,12},{9,13},{10,... | collective-permute-start | bytes 491528 | tf_op jit(solution)/shard_map/ppermute | solution.py:39
  88.9 15.1 %collective-permute-start.14 = (bf16[64,5120]{1,0:T(8,128)(2,1)S(1)}, bf16[64,5120]{1,0:T(8,128)(2,1)S(1)}, u32[]{:S(2)}, u32[]{:S(2)}) collective-permute-start(bf16[64,5120]{1,0:T(8,128)(2,1)S(1)} %pad_maximum_fusion.a_ref.refs_0_), channel_id=1, source_target_pairs={{0,1},{1,0},{2,3},{3,2},{4,5},{5,4},{6,7},{7,6},{8,10},{9,11},{10,... | collective-permute-start | bytes 1966088 | tf_op jit(solution)/shard_map/ppermute | solution.py:39
  96.0 7.9 %collective-permute-start.16 = (bf16[32,5120]{1,0:T(8,128)(2,1)S(1)}, bf16[32,5120]{1,0:T(8,128)(2,1)S(1)}, u32[]{:S(2)}, u32[]{:S(2)}) collective-permute-start(bf16[32,5120]{1,0:T(8,128)(2,1)S(1)} %pad_maximum_fusion.1), channel_id=1, source_target_pairs={{0,2},{1,3},{2,0},{3,1},{4,6},{5,7},{6,4},{7,5},{8,9},{9,8},{10,11... | collective-permute-start | bytes 983048 | tf_op jit(solution)/shard_map/ppermute | solution.py:39
  104.0 10.7 %collective-permute-start.17 = (bf16[64,5120]{1,0:T(8,128)(2,1)S(1)}, bf16[64,5120]{1,0:T(8,128)(2,1)S(1)}, u32[]{:S(2)}, u32[]{:S(2)}) collective-permute-start(bf16[64,5120]{1,0:T(8,128)(2,1)S(1)} %constant_dynamic-update-slice_fusion.2.a_ref.refs_0_.refs_2_), channel_id=1, source_target_pairs={{0,1},{1,0},{2,3},{3,2},{4,5},{5,4},{6,7},{7,6},{8,10},{9,11},{10,... | collective-permute-start | bytes 1966088 | tf_op jit(solution)/shard_map/ppermute | solution.py:39
  115.5 6.8 %collective-permute-start.18 = (f32[16,256]{1,0:T(8,128)S(1)}, f32[16,256]{1,0:T(8,128)S(1)}, u32[]{:S(2)}, u32[]{:S(2)}) collective-permute-start(f32[16,256]{1,0:T(8,128)S(1)} %pad_maximum_fusion.2), channel_id=1, source_target_pairs={{0,1},{1,0},{2,3},{3,2},{4,5},{5,4},{6,7},{7,6},{8,9},{9,8},{10,11... | collective-permute-start | bytes 49160 | tf_op jit(solution)/shard_map/ppermute | solution.py:31
  116.7 15.6 %slice-start = ((s8[17694720]{0:T(1024)(128)(4,1)}), s8[4194304]{0:T(1024)(128)(4,1)S(1)}, s32[]{:S(2)}) async-start(s8[17694720]{0:T(1024)(128)(4,1)} %bitcast.11), calls=%async_computation.1 | async-start | bytes 8388608
  116.7 15.7 %slice-start.1 = ((s8[17694720]{0:T(1024)(128)(4,1)}), s8[4194304]{0:T(1024)(128)(4,1)S(1)}, s32[]{:S(2)}) async-start(s8[17694720]{0:T(1024)(128)(4,1)} %bitcast.11), calls=%async_computation.2 | async-start | bytes 8388608
  116.7 15.7 %slice-start.2 = ((s8[17694720]{0:T(1024)(128)(4,1)}), s8[4194304]{0:T(1024)(128)(4,1)S(1)}, s32[]{:S(2)}) async-start(s8[17694720]{0:T(1024)(128)(4,1)} %bitcast.11), calls=%async_computation.3 | async-start | bytes 8388608
  122.3 10.1 %slice-start.3 = ((s8[17694720]{0:T(1024)(128)(4,1)}), s8[4194304]{0:T(1024)(128)(4,1)S(1)}, s32[]{:S(2)}) async-start(s8[17694720]{0:T(1024)(128)(4,1)} %bitcast.11), calls=%async_computation.4 | async-start | bytes 8388608
  122.3 10.0 %slice-start.4 = ((s8[17694720]{0:T(1024)(128)(4,1)}), s8[917504]{0:T(1024)(128)(4,1)S(1)}, s32[]{:S(2)}) async-start(s8[17694720]{0:T(1024)(128)(4,1)} %bitcast.11), calls=%async_computation.5 | async-start | bytes 1835008
  122.3 10.0 %copy-start.3 = (bf16[256,1728]{1,0:T(8,128)(2,1)S(1)}, bf16[256,1728]{1,0:T(8,128)(2,1)}, u32[]{:S(2)}) copy-start(bf16[256,1728]{1,0:T(8,128)(2,1)} %copy-done.2) | copy-start | bytes 2654212
  122.3 9.9 %collective-permute-start.21 = (f32[16,256]{1,0:T(8,128)S(1)}, f32[16,256]{1,0:T(8,128)S(1)}, u32[]{:S(2)}, u32[]{:S(2)}) collective-permute-start(f32[16,256]{1,0:T(8,128)S(1)} %fusion.3), channel_id=1, source_target_pairs={{0,6},{1,7},{2,4},{3,5},{4,2},{5,3},{6,0},{7,1},{8,14},{9,15},{10,... | collective-permute-start | bytes 49160 | tf_op jit(solution)/shard_map/ppermute | solution.py:31
  123.0 9.3 %collective-permute-start.19 = (f32[16,256]{1,0:T(8,128)S(1)}, f32[16,256]{1,0:T(8,128)S(1)}, u32[]{:S(2)}, u32[]{:S(2)}) collective-permute-start(f32[16,256]{1,0:T(8,128)S(1)} %fusion.3), channel_id=1, source_target_pairs={{0,2},{1,3},{2,0},{3,1},{4,6},{5,7},{6,4},{7,5},{8,10},{9,11},{10,... | collective-permute-start | bytes 49160 | tf_op jit(solution)/shard_map/ppermute | solution.py:31
  123.0 9.3 %collective-permute-start.20 = (f32[16,256]{1,0:T(8,128)S(1)}, f32[16,256]{1,0:T(8,128)S(1)}, u32[]{:S(2)}, u32[]{:S(2)}) collective-permute-start(f32[16,256]{1,0:T(8,128)S(1)} %fusion.3), channel_id=1, source_target_pairs={{0,4},{1,5},{2,6},{3,7},{4,0},{5,1},{6,2},{7,3},{8,12},{9,13},{10,... | collective-permute-start | bytes 49160 | tf_op jit(solution)/shard_map/ppermute | solution.py:31
  137.5 11.0 %collective-permute-start.22 = (bf16[128,2560]{1,0:T(8,128)(2,1)S(1)}, bf16[128,2560]{1,0:T(8,128)(2,1)S(1)}, u32[]{:S(2)}, u32[]{:S(2)}) collective-permute-start(bf16[128,2560]{1,0:T(8,128)(2,1)S(1)} %get-tuple-element.121), channel_id=1, source_target_pairs={{0,1},{1,0},{2,3},{3,2},{4,5},{5,4},{6,7},{7,6},{8,10},{9,11},{10,... | collective-permute-start | bytes 1966088 | tf_op jit(solution)/shard_map/ppermute | solution.py:39
  148.6 11.2 %collective-permute-start.25 = (bf16[128,2560]{1,0:T(8,128)(2,1)S(1)}, bf16[128,2560]{1,0:T(8,128)(2,1)S(1)}, u32[]{:S(2)}, u32[]{:S(2)}) collective-permute-start(bf16[128,2560]{1,0:T(8,128)(2,1)S(1)} %get-tuple-element.130), channel_id=1, source_target_pairs={{0,1},{1,0},{2,3},{3,2},{4,5},{5,4},{6,7},{7,6},{8,10},{9,11},{10,... | collective-permute-start | bytes 1966088 | tf_op jit(solution)/shard_map/ppermute | solution.py:39
  149.9 8.2 %collective-permute-start.23 = (bf16[64,2560]{1,0:T(8,128)(2,1)S(1)}, bf16[64,2560]{1,0:T(8,128)(2,1)S(1)}, u32[]{:S(2)}, u32[]{:S(2)}) collective-permute-start(bf16[64,2560]{1,0:T(8,128)(2,1)S(1)} %get-tuple-element.123), channel_id=1, source_target_pairs={{0,2},{1,3},{2,0},{3,1},{4,6},{5,7},{6,4},{7,5},{8,9},{9,8},{10,11... | collective-permute-start | bytes 983048 | tf_op jit(solution)/shard_map/ppermute | solution.py:39
  159.9 16.1 %copy-start.8 = (f32[16,5120]{1,0:T(8,128)S(1)}, f32[16,5120]{1,0:T(8,128)}, u32[]{:S(2)}) copy-start(f32[16,5120]{1,0:T(8,128)} %copy-done.7) | copy-start | bytes 983044
  160.0 8.0 %collective-permute-start.26 = (bf16[64,2560]{1,0:T(8,128)(2,1)S(1)}, bf16[64,2560]{1,0:T(8,128)(2,1)S(1)}, u32[]{:S(2)}, u32[]{:S(2)}) collective-permute-start(bf16[64,2560]{1,0:T(8,128)(2,1)S(1)} %get-tuple-element.134), channel_id=1, source_target_pairs={{0,2},{1,3},{2,0},{3,1},{4,6},{5,7},{6,4},{7,5},{8,9},{9,8},{10,11... | collective-permute-start | bytes 983048 | tf_op jit(solution)/shard_map/ppermute | solution.py:39
  160.7 10.6 %collective-permute-start.24 = (bf16[32,2560]{1,0:T(8,128)(2,1)S(1)}, bf16[32,2560]{1,0:T(8,128)(2,1)S(1)}, u32[]{:S(2)}, u32[]{:S(2)}) collective-permute-start(bf16[32,2560]{1,0:T(8,128)(2,1)S(1)} %get-tuple-element.125), channel_id=1, source_target_pairs={{0,4},{1,5},{2,6},{3,7},{4,0},{5,1},{6,2},{7,3},{8,12},{9,13},{10,... | collective-permute-start | bytes 491528 | tf_op jit(solution)/shard_map/ppermute | solution.py:39
  168.0 8.0 %collective-permute-start.27 = (bf16[32,2560]{1,0:T(8,128)(2,1)S(1)}, bf16[32,2560]{1,0:T(8,128)(2,1)S(1)}, u32[]{:S(2)}, u32[]{:S(2)}) collective-permute-start(bf16[32,2560]{1,0:T(8,128)(2,1)S(1)} %get-tuple-element.136), channel_id=1, source_target_pairs={{0,4},{1,5},{2,6},{3,7},{4,0},{5,1},{6,2},{7,3},{8,12},{9,13},{10,... | collective-permute-start | bytes 491528 | tf_op jit(solution)/shard_map/ppermute | solution.py:39
  (4 other events, 32.3 us)
